TPU v7x, 32 devices: a whole 2x2x4 slice. The times are simulated.
32 devices in a mesh: grp: 4 (over y, core), ctx: 8 (over z, x).
Axes of the slice: x: 2, y: 2, z: 4, core: 2. Of those that a mesh axis runs over, the one named last changes fastest.
Arguments:
- cache: bfloat16 [4, 16384, 576], P('grp', 'ctx'), may hold values from -6 to 6
- queries: bfloat16 [4, 4, 4, 128, 576], P(None, 'grp', None, 'ctx'), may hold values from -72 to 72
- new_latent: bfloat16 [4, 4, 4, 576], P(None, 'grp'), may hold values from -12 to 12
- lengths: int32 [4], replicated, may hold values from 8192 to 16384, as said below
- donor: int32 [4], replicated, may hold values from 0 to 3, as said below
- value_up: bfloat16 [128, 512, 128], P('ctx'), may hold values from -2 to 2
- out_proj: bfloat16 [16384, 7168], P('ctx'), may hold values from -0.0625 to 0.0625
Outputs:
- attn_out: bfloat16 [4, 4, 4, 7168], P(None, 'grp', None, 'ctx')
Inputs may be any that keep to these rules, and one draw needn't show every extreme that they name: `lengths`: in every draw some prompt has all 16384 positions valid. `donor`: A slot whose entry is its own index holds a hard prompt; every other entry names such a slot. Slot 3 always holds a hard prompt, and each draw has at least one slot that is not hard.
All inputs are finite; a program needn't handle non-finite values.
Results may differ from a plain program's by a relative error of at most 0.0058.
Values may be sent and summed in bfloat16 or wider, within the bound.
No kernel may reach another device: no remote copies, remote signals or barrier semaphores. Data moves between devices by JAX's collectives and lax.ppermute only.
A program may use at most 128 MiB of HBM per device.

v0:
```python
import jax
import jax.numpy as jnp
from jax import lax
from jax.sharding import PartitionSpec as P

HANDOVER = 3


score_scale = 192.0 ** (-0.5)
far_below = -1e30


def block_partial(query_rows, cache_rows, valid_mask, latent_width):
    logits = (
        lax.dot_general(
            query_rows, cache_rows, (((1,), (1,)), ((), ())), preferred_element_type=jnp.float32
        )
        * score_scale
    )
    logits = jnp.where(valid_mask[None, :], logits, far_below)
    top_score = jnp.max(logits, axis=1)
    weights = jnp.where(valid_mask[None, :], jnp.exp(logits - top_score[:, None]), 0.0)
    weight_sum = jnp.sum(weights, axis=1)
    partial_out = jnp.dot(
        weights.astype(jnp.bfloat16),
        cache_rows[:, :latent_width],
        preferred_element_type=jnp.float32,
    )
    return (top_score, weight_sum, partial_out)


def combine(earlier, later):
    top_score = jnp.maximum(earlier[0], later[0])
    scale_one = jnp.exp(earlier[0] - top_score)
    scale_two = jnp.exp(later[0] - top_score)
    return (
        top_score,
        earlier[1] * scale_one + later[1] * scale_two,
        earlier[2] * scale_one[..., None] + later[2] * scale_two[..., None],
    )


def serve(query_part, fresh_rows, prompt_rows, limits, value_up, out_proj):
    slot_count, sample_count, owned_heads, key_width = query_part.shape
    latent_width = value_up.shape[1]
    gathered = lax.all_gather(query_part, "ctx", axis=2, tiled=True)
    head_count = gathered.shape[2]
    row_count = sample_count * head_count
    local_len = prompt_rows.shape[0]
    positions = lax.axis_index("ctx") * local_len + lax.iota(jnp.int32, local_len)
    top_list, sum_list, part_list = ([], [], [])
    query_rows = gathered[0].reshape(row_count, key_width)
    valid_mask = positions < limits[0]
    found_part = block_partial(query_rows, prompt_rows, valid_mask, latent_width)
    top_list.append(found_part[0].reshape(sample_count, head_count))
    sum_list.append(found_part[1].reshape(sample_count, head_count))
    part_list.append(found_part[2].reshape(sample_count, head_count, latent_width))
    top_score = jnp.stack(top_list)
    weight_sum = jnp.stack(sum_list)
    partial_out = jnp.stack(part_list)
    top_all, sum_all, part_all = (
        lax.all_to_all(top_score[None], "ctx", split_axis=3, concat_axis=0, tiled=True),
        lax.all_to_all(weight_sum[None], "ctx", split_axis=3, concat_axis=0, tiled=True),
        lax.all_to_all(partial_out[None], "ctx", split_axis=3, concat_axis=0, tiled=True),
    )
    top_score = jnp.max(top_all, axis=0)
    factor = jnp.exp(top_all - top_score[None])
    weight_sum = jnp.sum(sum_all * factor, axis=0)
    partial_out = jnp.sum(part_all * factor[..., None], axis=0)
    highest = lax.Precision.HIGHEST
    query_wide = query_part.astype(jnp.float32)
    fresh_wide = fresh_rows.astype(jnp.float32)
    fresh_logits = (
        jnp.einsum("kshc,tksc->ksht", query_wide, fresh_wide, precision=highest) * score_scale
    )
    fresh_top = jnp.max(fresh_logits, axis=3)
    fresh_weights = jnp.exp(fresh_logits - fresh_top[..., None])
    fresh_sum = jnp.sum(fresh_weights, axis=3)
    fresh_part = jnp.einsum(
        "ksht,tksl->kshl", fresh_weights, fresh_wide[..., :latent_width], precision=highest
    )
    top_score, weight_sum, partial_out = combine(
        (top_score, weight_sum, partial_out), (fresh_top, fresh_sum, fresh_part)
    )
    attended = (partial_out / weight_sum[..., None]).astype(jnp.bfloat16)
    head_values = jnp.einsum(
        "kshl,hlv->kshv", attended, value_up, preferred_element_type=jnp.float32
    ).astype(jnp.bfloat16)
    term = jnp.dot(
        head_values.reshape(slot_count * sample_count, owned_heads * head_values.shape[3]),
        out_proj,
        preferred_element_type=jnp.float32,
    )
    mixed_out = lax.psum_scatter(term, "ctx", scatter_dimension=1, tiled=True).astype(jnp.bfloat16)
    return mixed_out.reshape(slot_count, sample_count, mixed_out.shape[1])


def body(cache, queries, new_latent, lengths, donor, value_up, out_proj):
    my_group = lax.axis_index("grp")
    group_count = lax.axis_size("grp")
    labels = lax.iota(jnp.int32, group_count)
    own_len = jnp.sum(jnp.where(labels == my_group, lengths, 0))
    own_rows = cache[0]
    results = []
    for step_index in range(HANDOVER):
        results.append(
            serve(
                queries[step_index],
                new_latent[: step_index + 1],
                own_rows,
                own_len[None],
                value_up,
                out_proj,
            )
        )
    source = jnp.sum(jnp.where(labels == my_group, donor, 0))
    shards = lax.all_gather(cache, "grp", axis=0, tiled=True)
    inside = (source >= 0) & (source < shards.shape[0])
    picked = lax.dynamic_index_in_dim(
        shards, jnp.clip(source, 0, shards.shape[0] - 1), 0, keepdims=False
    )
    moved_rows = jnp.where(inside, picked, jnp.zeros_like(own_rows))
    moved_len = jnp.sum(jnp.where(labels == source, lengths, 0))
    step_index = 3
    results.append(
        serve(queries[step_index], new_latent, moved_rows, moved_len[None], value_up, out_proj)
    )
    return jnp.stack(results)


def solution(mesh):
    return jax.shard_map(
        body,
        mesh=mesh,
        in_specs=(
            P("grp", "ctx", None),
            P(None, "grp", None, "ctx", None),
            P(None, "grp", None, None),
            P(),
            P(),
            P("ctx", None, None),
            P("ctx", None),
        ),
        out_specs=P(None, "grp", None, "ctx"),
        check_vma=False,
    )
```

profile of v0, /device:TPU:0, one launch (start us, length us, event | category | flops | bytes accessed | tf_op | source)
XLA Modules:
  0.0 656.6 jit_solution(14157457836206320762)
XLA Ops:
  9.4 1.9 fusion.96
  13.1 33.5 %all-gather = bf16[1,1,4,128,576]{4,3,2,1,0:T(8,128)(2,1)S(1)} all-gather(bf16[1,1,4,16,576]{4,3,2,1,0:T(8,128)(2,1)S(1)} %get-tuple-element.25), channel_id=2, replica_groups=mesh['grp'=4,'ctx'=8] {'ctx'}, dimensions={3}, use_global_device_ids=true | all-gather | bytes 663552 | tf_op jit(solution)/shard_map/all_gather | solution.py:46
  46.5 31.8 %all-gather.2 = bf16[1,1,4,128,576]{4,3,2,1,0:T(8,128)(2,1)S(1)} all-gather(bf16[1,1,4,16,576]{4,3,2,1,0:T(8,128)(2,1)S(1)} %get-tuple-element.27), channel_id=4, replica_groups=mesh['grp'=4,'ctx'=8] {'ctx'}, dimensions={3}, use_global_device_ids=true | all-gather | bytes 663552 | tf_op jit(solution)/shard_map/all_gather | solution.py:46
  78.3 31.8 %all-gather.1 = bf16[1,1,4,128,576]{4,3,2,1,0:T(8,128)(2,1)S(1)} all-gather(bf16[1,1,4,16,576]{4,3,2,1,0:T(8,128)(2,1)S(1)} %get-tuple-element.24), channel_id=3, replica_groups=mesh['grp'=4,'ctx'=8] {'ctx'}, dimensions={3}, use_global_device_ids=true | all-gather | bytes 663552 | tf_op jit(solution)/shard_map/all_gather | solution.py:46
  110.1 3.5 fusion.99
  113.6 2.0 fusion
  115.7 5.3 fusion.4
  121.8 5.7 all-to-all-start.2
  130.3 34.2 %all-gather.3 = bf16[1,1,4,128,576]{4,3,2,1,0:T(8,128)(2,1)} all-gather(bf16[1,1,4,16,576]{4,3,2,1,0:T(8,128)(2,1)S(1)} %get-tuple-element.26), channel_id=5, replica_groups=mesh['grp'=4,'ctx'=8] {'ctx'}, dimensions={3}, use_global_device_ids=true | all-gather | bytes 663552 | tf_op jit(solution)/shard_map/all_gather | solution.py:46
  164.5 4.3 fusion.18
  169.3 2.3 fusion.14
  171.6 2.3 fusion.16
  173.9 2.9 fusion.6
  178.8 5.4 all-to-all-start.1
  186.9 4.3 all-to-all-done.1
  191.2 3.3 all-to-all-start.5
  196.6 4.7 all-to-all-done.5
  201.4 3.5 all-to-all-start.4
  207.6 4.6 all-to-all-done.4
  212.1 4.4 all-to-all-start.8
  219.2 4.2 all-to-all-done.8
  223.4 3.3 all-to-all-start.7
  228.1 1.6 copy.177
  229.7 4.4 all-to-all-done.7
  234.2 4.6 all-to-all-start
  241.8 2.9 copy.184
  244.7 2.9 copy.195
  252.2 10.3 %all-to-all-done = f32[1,1,4,128,512]{4,2,1,0,3:T(4,128)S(1)} async-done(((f32[1,1,4,128,512]{4,2,1,0,3:T(4,128)}), f32[1,1,4,128,512]{4,2,1,0,3:T(4,128)S(1)}, u32[]{:S(2)}, u32[]{:S(2)}) %all-to-all-start) | async-done | bytes 1048608 | tf_op jit(solution)/shard_map/all_to_all | solution.py:64
  262.4 4.2 all-to-all-start.3
  267.2 17.0 %convolution_bitcast_fusion.3 = f32[7168,4]{1,0:T(8,128)} fusion(bf16[2048,7168]{1,0:T(8,128)(2,1)} %param.13, bf16[16,512,128]{2,1,0:T(8,128)(2,1)S(1)} %copy-done, bf16[4,16,512]{2,1,0:T(8,128)(2,1)S(1)} %divide_convert_fusion), kind=kOutput, calls=%fused_computation.3 | convolution fusion | flops 125837312 | bytes 31637504
  284.2 5.9 all-to-all-start.6
  292.2 17.2 %convolution_bitcast_fusion.2 = f32[7168,4]{1,0:T(8,128)} fusion(bf16[2048,7168]{1,0:T(8,128)(2,1)} %param.13, bf16[16,512,128]{2,1,0:T(8,128)(2,1)S(1)} %copy-done, bf16[4,16,512]{2,1,0:T(8,128)(2,1)S(1)} %fusion.50), kind=kOutput, calls=%fused_computation.2 | convolution fusion | flops 125837312 | bytes 31637504
  309.5 26.3 %all-to-all-done.6 = f32[1,1,4,128,512]{4,2,1,0,3:T(4,128)S(1)} async-done(((f32[1,1,4,128,512]{4,2,1,0,3:T(4,128)}), f32[1,1,4,128,512]{4,2,1,0,3:T(4,128)S(1)}, u32[]{:S(2)}, u32[]{:S(2)}) %all-to-all-start.6) | async-done | bytes 1048608 | tf_op jit(solution)/shard_map/all_to_all | solution.py:64
  336.1 1.9 select_bitcast_fusion
  338.0 2.3 fusion.3
  340.4 1.9 copy-done.4
  344.2 5.6 all-to-all-start.11
  350.8 6.0 all-to-all-done.11
  356.8 3.3 all-to-all-start.10
  360.2 4.7 fusion.12
  364.9 1.6 copy.206
  367.0 5.4 all-to-all-start.9
  372.8 17.1 %convolution_bitcast_fusion.1 = f32[7168,4]{1,0:T(8,128)} fusion(bf16[2048,7168]{1,0:T(8,128)(2,1)} %param.13, bf16[16,512,128]{2,1,0:T(8,128)(2,1)S(1)} %copy-done, bf16[4,16,512]{2,1,0:T(8,128)(2,1)S(1)} %fusion.51), kind=kOutput, calls=%fused_computation.1 | convolution fusion | flops 125837312 | bytes 31637504
  390.3 8.7 %all-to-all-done.9 = f32[1,1,4,128,512]{4,2,1,0,3:T(4,128)S(1)} async-done(((f32[1,1,4,128,512]{4,2,1,0,3:T(4,128)}), f32[1,1,4,128,512]{4,2,1,0,3:T(4,128)S(1)}, u32[]{:S(2)}, u32[]{:S(2)}) %all-to-all-start.9) | async-done | bytes 1048608 | tf_op jit(solution)/shard_map/all_to_all | solution.py:64
  399.6 17.0 %convolution_bitcast_fusion = f32[7168,4]{1,0:T(8,128)} fusion(bf16[2048,7168]{1,0:T(8,128)(2,1)} %param.13, bf16[16,512,128]{2,1,0:T(8,128)(2,1)S(1)} %copy-done, bf16[4,16,512]{2,1,0:T(8,128)(2,1)S(1)} %fusion.52), kind=kOutput, calls=%fused_computation | convolution fusion | flops 125837312 | bytes 31637504
  417.9 60.9 %reduce-scatter.15.cloned.1.call-done = f32[896,4]{1,0:T(8,128)} async-done(((f32[7168,4]{1,0:T(8,128)}), f32[896,4]{1,0:T(8,128)}) %reduce-scatter.15.cloned.1.call-update) | async-done | bytes 14352
  480.0 82.9 %reduce-scatter.17.cloned.1.call-done = f32[896,4]{1,0:T(8,128)} async-done(((f32[7168,4]{1,0:T(8,128)}), f32[896,4]{1,0:T(8,128)}) %reduce-scatter.17.cloned.1.call-update) | async-done | bytes 14352
  564.0 82.6 %reduce-scatter.19.cloned.1.call-done = f32[896,4]{1,0:T(8,128)} async-done(((f32[7168,4]{1,0:T(8,128)}), f32[896,4]{1,0:T(8,128)}) %reduce-scatter.19.cloned.1.call-update) | async-done | bytes 14352
  (145 shorter events, 40.1 us)
Async XLA Ops:
  7.4 259.8 %copy-start = (bf16[16,512,128]{2,1,0:T(8,128)(2,1)S(1)}, bf16[16,512,128]{2,1,0:T(8,128)(2,1)}, u32[]{:S(2)}) copy-start(bf16[16,512,128]{2,1,0:T(8,128)(2,1)} %param.12) | copy-start | bytes 6291460
  7.4 328.8 %all-gather.6.cloned.1.call-start = ((), (), s32[]{:S(2)}) async-start(), calls=%async_computation.16 | async-start | bytes 11796480 | tf_op jit(solution)/shard_map/all_gather | solution.py:117
  12.0 103.6 %copy-start.26 = (pred[2048]{0:T(1024)(128)(4,1)}, pred[2048]{0:T(1024)(128)(4,1)S(1)}, u32[]{:S(2)}) copy-start(pred[2048]{0:T(1024)(128)(4,1)S(1)} %fusion.81) | copy-start | bytes 6148
  78.3 35.3 %copy-start.6 = (bf16[1,2048,576]{1,2,0:T(8,128)(2,1)S(1)}, bf16[1,2048,576]{1,2,0:T(8,128)(2,1)}, u32[]{:S(2)}) copy-start(bf16[1,2048,576]{1,2,0:T(8,128)(2,1)} %param.7) | copy-start | bytes 7077892
  113.6 2.1 copy-start.1
  115.6 5.4 copy-start.29
  115.6 5.4 copy-start.30
  115.7 11.8 %copy-start.9 = (bf16[4,1,4,16,576]{4,3,2,1,0:T(8,128)(2,1)S(1)}, bf16[4,1,4,16,576]{4,3,2,1,0:T(8,128)(2,1)}, u32[]{:S(2)}) copy-start(bf16[4,1,4,16,576]{4,3,2,1,0:T(8,128)(2,1)} %param.8) | copy-start | bytes 884740
  115.7 11.8 %slice-start = ((bf16[4,1,4,576]{3,2,1,0:T(4,128)(2,1)}), bf16[2,1,4,576]{3,2,1,0:T(4,128)(2,1)S(1)}, s32[]{:S(2)}) async-start(bf16[4,1,4,576]{3,2,1,0:T(4,128)(2,1)} %param.9), calls=%async_computation.21 | async-start | bytes 20480 | tf_op jit(solution)/shard_map/slice | solution.py:109
  115.7 13.1 %slice-start.1 = ((bf16[4,1,4,576]{3,2,1,0:T(4,128)(2,1)}), bf16[3,1,4,576]{3,2,1,0:T(4,128)(2,1)S(1)}, s32[]{:S(2)}) async-start(bf16[4,1,4,576]{3,2,1,0:T(4,128)(2,1)} %param.9), calls=%async_computation.22 | async-start | bytes 30720 | tf_op jit(solution)/shard_map/slice | solution.py:109
  115.7 13.8 %copy-start.10 = (bf16[4,1,4,576]{3,2,1,0:T(4,128)(2,1)S(1)}, bf16[4,1,4,576]{3,2,1,0:T(4,128)(2,1)}, u32[]{:S(2)}) copy-start(bf16[4,1,4,576]{3,2,1,0:T(4,128)(2,1)} %param.9) | copy-start | bytes 55300
  121.8 57.0 %all-to-all-start.2 = ((f32[1,1,4,128]{2,1,0,3:T(1,128)}), f32[1,1,4,128]{2,1,0,3:T(1,128)S(1)}, u32[]{:S(2)}, u32[]{:S(2)}) async-start(f32[1,1,4,128]{2,1,0,3:T(1,128)} %copy.181), calls=%async_computation.2 | async-start | bytes 131072 | tf_op jit(solution)/shard_map/all_to_all | solution.py:63
  129.5 75.4 %copy-start.17 = (f32[4,16,3]{1,2,0:T(4,128)}, f32[4,16,3]{1,2,0:T(4,128)S(1)}, u32[]{:S(2)}) copy-start(f32[4,16,3]{1,2,0:T(4,128)S(1)} %get-tuple-element.37) | copy-start | bytes 2308
  130.3 86.3 %copy-start.15 = (f32[4,16,4]{1,2,0:T(4,128)}, f32[4,16,4]{1,2,0:T(4,128)S(1)}, u32[]{:S(2)}) copy-start(f32[4,16,4]{1,2,0:T(4,128)S(1)} %get-tuple-element.32) | copy-start | bytes 3076
  164.5 4.4 copy-start.2
  164.5 4.8 copy-start.7
  164.5 4.8 copy-start.24
  164.5 4.8 copy-start.27
  169.3 2.3 copy-start.3
  169.3 2.3 copy-start.25
  173.9 2.9 copy-start.11
  178.8 12.4 %all-to-all-start.1 = ((f32[1,1,4,128]{2,1,0,3:T(1,128)}), f32[1,1,4,128]{2,1,0,3:T(1,128)}, u32[]{:S(2)}, u32[]{:S(2)}) async-start(f32[1,1,4,128]{2,1,0,3:T(1,128)} %copy.179), calls=%async_computation.1 | async-start | bytes 131072 | tf_op jit(solution)/shard_map/all_to_all | solution.py:62
  185.6 53.7 %copy-start.12 = (bf16[4,1,4,576]{3,2,1,0:T(4,128)(2,1)S(1)}, bf16[4,1,4,576]{3,2,1,0:T(4,128)(2,1)}, u32[]{:S(2)}) copy-start(bf16[4,1,4,576]{3,2,1,0:T(4,128)(2,1)} %param.9) | copy-start | bytes 55300
  191.2 10.2 %all-to-all-start.5 = ((f32[1,1,4,128]{2,1,0,3:T(1,128)}), f32[1,1,4,128]{2,1,0,3:T(1,128)S(1)}, u32[]{:S(2)}, u32[]{:S(2)}) async-start(f32[1,1,4,128]{2,1,0,3:T(1,128)} %copy.192), calls=%async_computation.5 | async-start | bytes 131072 | tf_op jit(solution)/shard_map/all_to_all | solution.py:63
  201.4 10.7 %all-to-all-start.4 = ((f32[1,1,4,128]{2,1,0,3:T(1,128)}), f32[1,1,4,128]{2,1,0,3:T(1,128)S(1)}, u32[]{:S(2)}, u32[]{:S(2)}) async-start(f32[1,1,4,128]{2,1,0,3:T(1,128)} %copy.186), calls=%async_computation.4 | async-start | bytes 131072 | tf_op jit(solution)/shard_map/all_to_all | solution.py:62
  212.1 11.3 %all-to-all-start.8 = ((f32[1,1,4,128]{2,1,0,3:T(1,128)}), f32[1,1,4,128]{2,1,0,3:T(1,128)S(1)}, u32[]{:S(2)}, u32[]{:S(2)}) async-start(f32[1,1,4,128]{2,1,0,3:T(1,128)} %copy.203), calls=%async_computation.8 | async-start | bytes 131072 | tf_op jit(solution)/shard_map/all_to_all | solution.py:63
  223.4 10.7 %all-to-all-start.7 = ((f32[1,1,4,128]{2,1,0,3:T(1,128)}), f32[1,1,4,128]{2,1,0,3:T(1,128)S(1)}, u32[]{:S(2)}, u32[]{:S(2)}) async-start(f32[1,1,4,128]{2,1,0,3:T(1,128)} %copy.197), calls=%async_computation.7 | async-start | bytes 131072 | tf_op jit(solution)/shard_map/all_to_all | solution.py:62
  234.2 28.3 %all-to-all-start = ((f32[1,1,4,128,512]{4,2,1,0,3:T(4,128)}), f32[1,1,4,128,512]{4,2,1,0,3:T(4,128)S(1)}, u32[]{:S(2)}, u32[]{:S(2)}) async-start(f32[1,1,4,128,512]{4,2,1,0,3:T(4,128)} %copy.177), calls=%async_computation | async-start | bytes 2097152 | tf_op jit(solution)/shard_map/all_to_all | solution.py:64
  239.3 101.1 %copy-start.14 = (pred[2048]{0:T(1024)(128)(4,1)}, pred[2048]{0:T(1024)(128)(4,1)S(1)}, u32[]{:S(2)}) copy-start(pred[2048]{0:T(1024)(128)(4,1)S(1)} %fusion.80) | copy-start | bytes 6148
  262.4 21.8 %all-to-all-start.3 = ((f32[1,1,4,128,512]{4,2,1,0,3:T(4,128)}), f32[1,1,4,128,512]{4,2,1,0,3:T(4,128)}, u32[]{:S(2)}, u32[]{:S(2)}) async-start(f32[1,1,4,128,512]{4,2,1,0,3:T(4,128)} %copy.184), calls=%async_computation.3 | async-start | bytes 2097152 | tf_op jit(solution)/shard_map/all_to_all | solution.py:64
  266.7 150.0 %reduce-scatter.13.cloned.1.call-start = ((), (), s32[]{:S(2)}) async-start(), calls=%async_computation.17 | async-start | bytes 4128768
  284.2 7.7 %copy-start.19 = (bf16[2,1,4,512]{3,2,1,0:T(4,128)(2,1)S(1)}, bf16[2,1,4,512]{3,2,1,0:T(4,128)(2,1)}, u32[]{:S(2)}) copy-start(bf16[2,1,4,512]{3,2,1,0:T(4,128)(2,1)} %slice.50) | copy-start | bytes 24580
  284.2 7.7 %copy-start.23 = (f32[4,16]{1,0:T(4,128)S(1)}, f32[4,16]{1,0:T(4,128)}, u32[]{:S(2)}) copy-start(f32[4,16]{1,0:T(4,128)} %get-tuple-element.38) | copy-start | bytes 772
  284.2 7.8 %copy-start.28 = (f32[4,16,2]{1,2,0:T(2,128)S(1)}, f32[4,16,2]{1,2,0:T(2,128)}, u32[]{:S(2)}) copy-start(f32[4,16,2]{1,2,0:T(2,128)} %get-tuple-element.39) | copy-start | bytes 1540
  284.2 51.5 %all-to-all-start.6 = ((f32[1,1,4,128,512]{4,2,1,0,3:T(4,128)}), f32[1,1,4,128,512]{4,2,1,0,3:T(4,128)S(1)}, u32[]{:S(2)}, u32[]{:S(2)}) async-start(f32[1,1,4,128,512]{4,2,1,0,3:T(4,128)} %copy.195), calls=%async_computation.6 | async-start | bytes 2097152 | tf_op jit(solution)/shard_map/all_to_all | solution.py:64
  290.1 188.7 %reduce-scatter.15.cloned.1.call-start = ((), (), s32[]{:S(2)}) async-start(), calls=%async_computation.18 | async-start | bytes 4128768
  338.0 2.4 copy-start.5
  340.4 9.4 %copy-start.13 = (bf16[3,1,4,512]{3,2,1,0:T(4,128)(2,1)S(1)}, bf16[3,1,4,512]{3,2,1,0:T(4,128)(2,1)}, u32[]{:S(2)}) copy-start(bf16[3,1,4,512]{3,2,1,0:T(4,128)(2,1)} %slice.53) | copy-start | bytes 36868
  340.4 9.4 %copy-start.18 = (f32[4,16,3]{1,2,0:T(4,128)S(1)}, f32[4,16,3]{1,2,0:T(4,128)}, u32[]{:S(2)}) copy-start(f32[4,16,3]{1,2,0:T(4,128)} %copy-done.17) | copy-start | bytes 2308
  340.4 9.4 %copy-start.21 = (f32[4,16]{1,0:T(4,128)S(1)}, f32[4,16]{1,0:T(4,128)}, u32[]{:S(2)}) copy-start(f32[4,16]{1,0:T(4,128)} %get-tuple-element.36) | copy-start | bytes 772
  344.2 12.6 %all-to-all-start.11 = ((f32[1,1,4,128]{2,1,0,3:T(1,128)}), f32[1,1,4,128]{2,1,0,3:T(1,128)S(1)}, u32[]{:S(2)}, u32[]{:S(2)}) async-start(f32[1,1,4,128]{2,1,0,3:T(1,128)} %copy.214), calls=%async_computation.11 | async-start | bytes 131072 | tf_op jit(solution)/shard_map/all_to_all | solution.py:63
  356.8 10.2 %all-to-all-start.10 = ((f32[1,1,4,128]{2,1,0,3:T(1,128)}), f32[1,1,4,128]{2,1,0,3:T(1,128)S(1)}, u32[]{:S(2)}, u32[]{:S(2)}) async-start(f32[1,1,4,128]{2,1,0,3:T(1,128)} %copy.208), calls=%async_computation.10 | async-start | bytes 131072 | tf_op jit(solution)/shard_map/all_to_all | solution.py:62
  367.0 32.0 %all-to-all-start.9 = ((f32[1,1,4,128,512]{4,2,1,0,3:T(4,128)}), f32[1,1,4,128,512]{4,2,1,0,3:T(4,128)S(1)}, u32[]{:S(2)}, u32[]{:S(2)}) async-start(f32[1,1,4,128,512]{4,2,1,0,3:T(4,128)} %copy.206), calls=%async_computation.9 | async-start | bytes 2097152 | tf_op jit(solution)/shard_map/all_to_all | solution.py:64
  372.4 17.8 %copy-start.20 = (f32[4,16]{1,0:T(4,128)S(1)}, f32[4,16]{1,0:T(4,128)}, u32[]{:S(2)}) copy-start(f32[4,16]{1,0:T(4,128)} %get-tuple-element.31) | copy-start | bytes 772
  372.4 17.8 %copy-start.22 = (f32[4,16]{1,0:T(4,128)S(1)}, f32[4,16]{1,0:T(4,128)}, u32[]{:S(2)}) copy-start(f32[4,16]{1,0:T(4,128)} %fusion.83) | copy-start | bytes 772
  372.5 190.4 %reduce-scatter.17.cloned.1.call-start = ((), (), s32[]{:S(2)}) async-start(), calls=%async_computation.19 | async-start | bytes 4128768
  389.9 9.5 %copy-start.16 = (f32[4,16,4]{1,2,0:T(4,128)S(1)}, f32[4,16,4]{1,2,0:T(4,128)}, u32[]{:S(2)}) copy-start(f32[4,16,4]{1,2,0:T(4,128)} %copy-done.15) | copy-start | bytes 3076
  389.9 256.8 %reduce-scatter.19.cloned.1.call-start = ((), (), s32[]{:S(2)}) async-start(), calls=%async_computation.20 | async-start | bytes 4128768
  (2 other events, 3.9 us)
Sparse Core Ops, SparseCore 0:
  9.7 66.9 all-gather.5
Sparse Core Ops, SparseCore 1:
  284.3 108.1 reduce-scatter.12
  395.9 82.8 reduce-scatter.14
  482.3 80.5 reduce-scatter.16
  566.5 80.1 reduce-scatter.18
where the time goes:
time: 667 us; the launch traced here: 657 us
  waiting for transfers between devices  301 us (45%)
  blocking collectives  131 us (20%)
  matrix products  100 us (15%)
  starting transfers between devices  55.4 us (8%)
  local copies, waits for them, and re-layouts  30.2 us (5%)
  other arithmetic  20.6 us (3%)
  between operations  18 us (3%)
    unnamed x9, waiting for transfers between devices  227 us
    all_gather x4, blocking collectives, serve(): gathered = lax.all_gather(query_part, 'ctx', axis=2, tiled=True)  131 us
    unnamed x4, matrix products  68.3 us
    all_to_all x4, waiting for transfers between devices, serve(): lax.all_to_all(partial_out[None], 'ctx', split_axis=3, concat_axis=0, til...  45.2 us
    all_to_all x4, starting transfers between devices, serve(): lax.all_to_all(partial_out[None], 'ctx', split_axis=3, concat_axis=0, til...  20.1 us
    all_to_all x4, starting transfers between devices, serve(): lax.all_to_all(weight_sum[None], 'ctx', split_axis=3, concat_axis=0, tile...  19.1 us
    all_to_all x4, starting transfers between devices, serve(): lax.all_to_all(top_score[None], 'ctx', split_axis=3, concat_axis=0, tiled...  15.6 us
    all_to_all x4, waiting for transfers between devices, serve(): lax.all_to_all(weight_sum[None], 'ctx', split_axis=3, concat_axis=0, tile...  14.9 us
  transfers between devices with their start and end apart: 17, of which 13 were waited for; matrix products, arithmetic and copies ran while one was open for 22% of the time, Pallas kernels for 0%

commit v1 on v0

v1 whole, which is shorter than its diff:
```python
import functools

import jax
import jax.numpy as jnp
from jax import lax
from jax.experimental import pallas as pl
from jax.experimental.pallas import tpu as pltpu
from jax.sharding import PartitionSpec as P

HANDOVER = 3
EXTRA = 16
MIB = 1 << 20

score_scale = 192.0 ** (-0.5)
far_below = -1e30

ROWS_BY_ROWS = (((1,), (1,)), ((), ()))


def diagonal(n):
    return lax.broadcasted_iota(jnp.int32, (n, n), 0) == lax.broadcasted_iota(jnp.int32, (n, n), 1)


def to_row(column):
    n = column.shape[0]
    return jnp.sum(jnp.where(diagonal(n), column, 0.0), axis=0, keepdims=True)


def to_column(row):
    n = row.shape[1]
    return jnp.sum(jnp.where(diagonal(n), row, 0.0), axis=1, keepdims=True)


def split_three(value):
    high = value.astype(jnp.bfloat16).astype(jnp.float32)
    rest = value - high
    middle = rest.astype(jnp.bfloat16).astype(jnp.float32)
    return high, middle, rest - middle


def store_packed(out_ref, part, peak_row, total_row):
    rows, width = part.shape
    out_ref[0:rows, :] = part.astype(jnp.bfloat16)
    line = lax.broadcasted_iota(jnp.int32, (EXTRA, rows), 0)
    block = jnp.zeros((EXTRA, rows), jnp.float32)
    for at, piece in enumerate(split_three(peak_row) + split_three(total_row)):
        block = jnp.where(line == at, piece, block)
    if rows < width:
        out_ref[rows : rows + EXTRA, :] = jnp.zeros((EXTRA, width), jnp.bfloat16)
    out_ref[rows : rows + EXTRA, 0:rows] = block.astype(jnp.bfloat16)


def load_packed(ref):
    rows = ref.shape[0] - EXTRA
    block = ref[rows : rows + EXTRA, 0:rows].astype(jnp.float32)
    peak = block[0:1] + block[1:2] + block[2:3]
    total = block[3:4] + block[4:5] + block[5:6]
    return peak, total, ref[0:rows, :].astype(jnp.float32)


def attend_block(query, cache_ref, limit, score_ref, latent):
    rows = query.shape[0]
    length = cache_ref.shape[0]
    tile = min(512, length)
    peak = jnp.full((rows, 1), far_below, jnp.float32)
    for start in range(0, length, tile):
        scores = (
            lax.dot_general(
                query,
                cache_ref[start : start + tile, :],
                ROWS_BY_ROWS,
                preferred_element_type=jnp.float32,
            )
            * score_scale
        )
        position = start + lax.broadcasted_iota(jnp.int32, (1, tile), 1)
        scores = jnp.where(position < limit, scores, far_below)
        score_ref[0:rows, start : start + tile] = scores
        peak = jnp.maximum(peak, jnp.max(scores, axis=1, keepdims=True))
    total = jnp.zeros((rows, 1), jnp.float32)
    part = jnp.zeros((rows, latent), jnp.float32)
    for start in range(0, length, tile):
        weights = jnp.exp(score_ref[0:rows, start : start + tile] - peak)
        total = total + jnp.sum(weights, axis=1, keepdims=True)
        part = part + jnp.dot(
            weights.astype(jnp.bfloat16),
            cache_ref[start : start + tile, 0:latent],
            preferred_element_type=jnp.float32,
        )
    some = limit > 0
    return peak, jnp.where(some, total, 0.0), jnp.where(some, part, 0.0)


def fresh_block(query, fresh, first_step, samples, heads, latent):
    rows, columns = query.shape[0], fresh.shape[0]
    scores = (
        lax.dot_general(query, fresh, ROWS_BY_ROWS, preferred_element_type=jnp.float32)
        * score_scale
    )
    row = lax.broadcasted_iota(jnp.int32, (rows, columns), 0) // heads
    column = lax.broadcasted_iota(jnp.int32, (rows, columns), 1)
    seen = (column % samples == row % samples) & (column // samples <= row // samples + first_step)
    scores = jnp.where(seen, scores, far_below)
    peak = jnp.max(scores, axis=1, keepdims=True)
    weights = jnp.where(seen, jnp.exp(scores - peak), 0.0)
    total = jnp.sum(weights, axis=1, keepdims=True)
    part = jnp.dot(
        weights,
        fresh[:, 0:latent].astype(jnp.float32),
        precision=lax.Precision.HIGHEST,
        preferred_element_type=jnp.float32,
    )
    return peak, total, part


def attend_kernel(kinds, latent, fresh_info, *refs):
    count = len(kinds)
    limit_ref, cache_ref = refs[0], refs[1]
    queries = refs[2 : 2 + count]
    rest = list(refs[2 + count :])
    fresh_ref = rest.pop(0) if fresh_info else None
    score_ref = rest.pop()
    limit = limit_ref[0]
    for kind, query_ref in zip(kinds, queries):
        query = query_ref[...]
        peak, total, part = attend_block(query, cache_ref, limit, score_ref, latent)
        if kind == "own":
            other = fresh_block(query, fresh_ref[...], *fresh_info, latent)
            top = jnp.maximum(peak, other[0])
            one, two = jnp.exp(peak - top), jnp.exp(other[0] - top)
            total = total * one + other[1] * two
            part = part * one + other[2] * two
            peak = top
        peak_row, total_row = to_row(peak), to_row(total)
        if kind == "send":
            store_packed(rest.pop(0), part, peak_row, total_row)
        else:
            rest.pop(0)[...] = part
            stats_ref = rest.pop(0)
            line = lax.broadcasted_iota(jnp.int32, stats_ref.shape, 0)
            stats_ref[...] = jnp.where(line == 0, peak_row, total_row)


def whole(memory=pltpu.VMEM):
    return pl.BlockSpec(memory_space=memory)


def attend(kinds, queries, cache_rows, limit, latent, fresh=None, fresh_info=None):
    out_shape = []
    flops = 0
    for kind, query in zip(kinds, queries):
        rows = query.shape[0]
        flops += 2 * rows * cache_rows.shape[0] * (cache_rows.shape[1] + latent)
        if kind == "send":
            out_shape.append(jax.ShapeDtypeStruct((rows + EXTRA, latent), jnp.bfloat16))
        else:
            out_shape.append(jax.ShapeDtypeStruct((rows, latent), jnp.float32))
            out_shape.append(jax.ShapeDtypeStruct((8, rows), jnp.float32))
    most = max(query.shape[0] for query in queries)
    operands = [limit, cache_rows, *queries] + ([fresh] if fresh_info else [])
    outs = pl.pallas_call(
        functools.partial(attend_kernel, tuple(kinds), latent, fresh_info),
        out_shape=out_shape,
        in_specs=[whole(pltpu.SMEM)] + [whole()] * (len(operands) - 1),
        out_specs=[whole()] * len(out_shape),
        scratch_shapes=[pltpu.VMEM((most, cache_rows.shape[0]), jnp.float32)],
        compiler_params=pltpu.CompilerParams(vmem_limit_bytes=24 * MIB),
        cost_estimate=pl.CostEstimate(
            flops=flops, bytes_accessed=4 * MIB, transcendentals=flops // 2200
        ),
        name="attend_" + "_".join(kinds),
    )(*operands)
    outs = list(outs)
    results = []
    for kind in kinds:
        if kind == "send":
            results.append(outs.pop(0))
        else:
            results.append((outs.pop(0), outs.pop(0)))
    return results


def merge_kernel(count, *refs):
    for at in range(count):
        packed_ref, part_ref, stats_ref = refs[3 * at : 3 * at + 3]
        out_ref = refs[3 * count + at]
        peak, total, part = load_packed(packed_ref)
        own_peak, own_total = stats_ref[0:1, :], stats_ref[1:2, :]
        top = jnp.maximum(peak, own_peak)
        one, two = jnp.exp(peak - top), jnp.exp(own_peak - top)
        merged = part * to_column(one) + part_ref[...] * to_column(two)
        store_packed(out_ref, merged, top, total * one + own_total * two)


def merge(pairs):
    operands = []
    for packed, (part, stats) in pairs:
        operands += [packed, part, stats]
    return pl.pallas_call(
        functools.partial(merge_kernel, len(pairs)),
        out_shape=[jax.ShapeDtypeStruct(packed.shape, packed.dtype) for packed, _ in pairs],
        in_specs=[whole()] * len(operands),
        out_specs=[whole()] * len(pairs),
        compiler_params=pltpu.CompilerParams(vmem_limit_bytes=16 * MIB),
        cost_estimate=pl.CostEstimate(flops=1 << 20, bytes_accessed=2 * MIB, transcendentals=1024),
        name="merge",
    )(*operands)


def finish_kernel(chunks, heads, *refs):
    value_ref, out_ref, rows_ref = refs[-3:]
    lanes = rows_ref.shape[0]
    at = 0
    for index in range(chunks):
        left_ref, right_ref, part_ref, stats_ref = refs[4 * index : 4 * index + 4]
        left, right = load_packed(left_ref), load_packed(right_ref)
        own_peak, own_total = stats_ref[0:1, :], stats_ref[1:2, :]
        top = jnp.maximum(jnp.maximum(left[0], right[0]), own_peak)
        one, two, three = jnp.exp(left[0] - top), jnp.exp(right[0] - top), jnp.exp(own_peak - top)
        total = left[1] * one + right[1] * two + own_total * three
        merged = left[2] * to_column(one) + right[2] * to_column(two)
        merged = (merged + part_ref[...] * to_column(three)) / to_column(total)
        rows = merged.shape[0]
        for lane in range(lanes):
            rows_ref[lane, at : at + rows, :] = merged[:, lane * 128 : (lane + 1) * 128]
        at += rows
    width = value_ref.shape[2]
    for head in range(heads):
        picked = pl.ds(head, at // heads, stride=heads)
        attended = jnp.concatenate([rows_ref[lane, picked, :] for lane in range(lanes)], axis=1)
        attended = attended.astype(jnp.bfloat16)
        values = jnp.dot(attended, value_ref[head], preferred_element_type=jnp.float32)
        out_ref[:, head * width : (head + 1) * width] = values.astype(jnp.bfloat16)


def finish(chunk_parts, value_up):
    heads, latent, width = value_up.shape
    operands = []
    rows = 0
    for left, right, (part, stats) in chunk_parts:
        operands += [left, right, part, stats]
        rows += part.shape[0]
    operands.append(value_up)
    return pl.pallas_call(
        functools.partial(finish_kernel, len(chunk_parts), heads),
        out_shape=jax.ShapeDtypeStruct((rows // heads, heads * width), jnp.bfloat16),
        in_specs=[whole()] * len(operands),
        out_specs=whole(),
        scratch_shapes=[pltpu.VMEM((latent // 128, rows, 128), jnp.float32)],
        compiler_params=pltpu.CompilerParams(vmem_limit_bytes=16 * MIB),
        cost_estimate=pl.CostEstimate(flops=1 << 24, bytes_accessed=4 * MIB, transcendentals=1024),
        name="finish",
    )(*operands)


def project_kernel(values_ref, weight_ref, out_ref):
    out_ref[...] = jnp.dot(
        values_ref[...], weight_ref[...], preferred_element_type=jnp.float32
    ).astype(out_ref.dtype)


def project(values, out_proj, parts):
    rows, depth = values.shape
    width = out_proj.shape[1]
    share = width // parts
    cost = pl.CostEstimate(
        flops=2 * rows * depth * width, bytes_accessed=2 * depth * width, transcendentals=0
    )
    params = pltpu.CompilerParams(
        vmem_limit_bytes=24 * MIB, dimension_semantics=("arbitrary",)
    )
    tile = share
    while share % 128 and tile % 128:
        tile *= 2
    shared = share % 128 == 0
    if shared:
        out_shape = jax.ShapeDtypeStruct((parts, rows, share), jnp.bfloat16)
        out_spec = pl.BlockSpec((None, rows, share), lambda j: (j, 0, 0))
    else:
        out_shape = jax.ShapeDtypeStruct((rows, width), jnp.bfloat16)
        out_spec = pl.BlockSpec((rows, tile), lambda j: (0, j))
    out = pl.pallas_call(
        project_kernel,
        grid=(width // tile,),
        out_shape=out_shape,
        in_specs=[
            pl.BlockSpec((rows, depth), lambda j: (0, 0)),
            pl.BlockSpec((depth, tile), lambda j: (0, j)),
        ],
        out_specs=out_spec,
        compiler_params=params,
        cost_estimate=cost,
        name="project",
    )(values, out_proj)
    if not shared:
        out = out.reshape(rows, parts, share).transpose(1, 0, 2)
    return out


def handed_over(cache_rows, donor, my_group, group_count):
    source = jnp.sum(jnp.where(lax.iota(jnp.int32, group_count) == my_group, donor, 0))

    def gather_all():
        shards = lax.all_gather(cache_rows, "grp", axis=0, tiled=False)
        return lax.dynamic_index_in_dim(shards, source, 0, keepdims=False)

    if group_count != 4:
        return source, gather_all()
    half = cache_rows.shape[0] // 2
    core, plane = my_group % 2, my_group // 2
    core_swap = [(g, g ^ 1) for g in range(4)]
    plane_swap = [(g, g ^ 2) for g in range(4)]
    beside = lax.ppermute(cache_rows, "grp", core_swap)
    wanted, crowded = [], []
    for at in range(2):
        first, second = donor[2 * at], donor[2 * at + 1]
        first_far, second_far = first // 2 != at, second // 2 != at
        wanted.append(jnp.where(first_far, first, second))
        crowded.append(first_far & second_far & (first != second))
    asked = jnp.where(plane == 0, wanted[1], wanted[0])
    offered = jnp.where(
        asked % 2 == core,
        lax.dynamic_slice_in_dim(cache_rows, core * half, half, 0),
        lax.dynamic_slice_in_dim(beside, core * half, half, 0),
    )
    mine = lax.ppermute(offered, "grp", plane_swap)
    other = lax.ppermute(mine, "grp", core_swap)
    far_rows = jnp.concatenate(
        [jnp.where(core == 0, mine, other), jnp.where(core == 0, other, mine)]
    )
    near_rows = jnp.where(source == my_group, cache_rows, beside)
    rows = jnp.where(source // 2 == plane, near_rows, far_rows)
    rows = lax.cond(crowded[0] | crowded[1], gather_all, lambda: rows)
    return source, rows


def body(cache, queries, new_latent, lengths, donor, value_up, out_proj):
    my_group = lax.axis_index("grp")
    group_count = lax.axis_size("grp")
    parts = lax.axis_size("ctx")
    steps, _, samples, heads, key_width = queries.shape
    latent = value_up.shape[1]
    own_rows = cache[0]
    local_len = own_rows.shape[0]
    first = lax.axis_index("ctx") * local_len
    labels = lax.iota(jnp.int32, group_count)

    def limit_of(group):
        length = jnp.sum(jnp.where(labels == group, lengths, 0))
        return jnp.clip(length - first, 0, local_len).astype(jnp.int32)[None]

    source, moved_rows = handed_over(own_rows, donor, my_group, group_count)
    fresh = new_latent.reshape(steps * samples, key_width)

    ring = list(range(0, parts, 2)) + list(range(parts - 1, 0, -2))
    to_right = [(ring[i], ring[(i + 1) % parts]) for i in range(parts)]
    to_left = [(b, a) for a, b in to_right]
    right = functools.partial(lax.ppermute, axis_name="ctx", perm=to_right)
    left = functools.partial(lax.ppermute, axis_name="ctx", perm=to_left)
    reach = parts // 2

    query_rows = queries.reshape(steps, samples * heads, key_width)
    chunks = [
        (0, query_rows[:HANDOVER].reshape(-1, key_width), own_rows, limit_of(my_group)),
        (HANDOVER, query_rows[HANDOVER:].reshape(-1, key_width), moved_rows, limit_of(source)),
    ]
    gathered = []
    for _, own_query, _, _ in chunks:
        from_left, from_right = [own_query], [own_query]
        for hop in range(1, reach + 1):
            from_left.append(right(from_left[-1]))
            if hop < reach:
                from_right.append(left(from_right[-1]))
        gathered.append((from_left, from_right))
    finals = []
    for (first_step, own_query, rows, limit), (from_left, from_right) in zip(chunks, gathered):
        fresh_info = (first_step, samples, heads)
        (own_part,) = attend(["own"], [own_query], rows, limit, latent, fresh, fresh_info)
        part_left, part_right = {}, {}
        for hop in range(1, reach + 1):
            todo = [(part_left, from_left, "send" if hop == reach else "keep")]
            if hop < reach:
                todo.append((part_right, from_right, "send" if hop == reach - 1 else "keep"))
            results = attend(
                [kind for _, _, kind in todo], [q[hop] for _, q, _ in todo], rows, limit, latent
            )
            for (store, _, _), result in zip(todo, results):
                store[hop] = result
        going_left, going_right = part_left[reach], None
        for hop in range(reach, 0, -1):
            came = left(going_left)
            if hop == reach:
                going_right = part_right[reach - 1]
                going_left = merge([(came, part_left[hop - 1])])[0]
                continue
            came_right = right(going_right)
            if hop > 1:
                going_left, going_right = merge(
                    [(came, part_left[hop - 1]), (came_right, part_right[hop - 1])]
                )
            else:
                finals.append((came, came_right, own_part))
    head_values = finish(finals, value_up)
    term = project(head_values, out_proj, parts)
    shares = lax.all_to_all(term, "ctx", split_axis=0, concat_axis=0, tiled=True)
    mixed = jnp.sum(shares.astype(jnp.float32), axis=0).astype(jnp.bfloat16)
    return mixed.reshape(steps, 1, samples, mixed.shape[-1])


def solution(mesh):
    return jax.shard_map(
        body,
        mesh=mesh,
        in_specs=(
            P("grp", "ctx", None),
            P(None, "grp", None, "ctx", None),
            P(None, "grp", None, None),
            P(),
            P(),
            P("ctx", None, None),
            P("ctx", None),
        ),
        out_specs=P(None, "grp", None, "ctx"),
        check_vma=False,
    )
```

time: 667 us -> 193 us (0.29); the launches traced: 657 us -> 192 us
  waiting for transfers between devices: 301 us -> 33.1 us
  blocking collectives: 131 us -> 12.7 us
  matrix products: 100 us -> 0 us
  Pallas kernels: 0 us -> 41.7 us
  starting transfers between devices: 55.4 us -> 33.6 us
  between operations: 18 us -> 30.7 us
  other arithmetic: 20.6 us -> 12.3 us
    unnamed x9 -> x0, waiting for transfers between devices: 227 us -> none
    all_gather x4 -> x0, blocking collectives: 131 us -> none  [serve(): gathered = lax.all_gather(query_part, 'ctx', axis=2, tiled=True)]
    all_to_all x12 -> x0, waiting for transfers between devices: 73.9 us -> none  [the longest x4 45.2 us: serve(): lax.all_to_all(partial_out[None], 'ctx', split_axis=3, concat_axis=0, til...]
    unnamed x4 -> x0, matrix products: 68.3 us -> none
    all_to_all x12 -> x0, starting transfers between devices: 54.7 us -> none  [the longest x4 20.1 us: serve(): lax.all_to_all(partial_out[None], 'ctx', split_axis=3, concat_axis=0, til...]
    pallas_call x0 -> x18, Pallas kernels: none -> 41.7 us  [the longest x10 32.6 us: attend(): pl.pallas_call(functools.partial(attend_kernel, tuple(kinds), latent, fre...]
    ppermute x0 -> x31, starting transfers between devices: none -> 33.6 us  [the longest x8 12.6 us: body(): from_left.append(right(from_left[-1]))]
    ppermute x0 -> x31, waiting for transfers between devices: none -> 33.1 us  [the longest x1 25.1 us: handed_over(): mine = lax.ppermute(offered, 'grp', plane_swap)]
  transfers between devices with their start and end apart: 17 -> 31, of which waited for: 13 -> 3; matrix products, arithmetic and copies ran while one was open for 22% -> 13% of each run, Pallas kernels for 0% -> 17%
where the time goes in v1:
time: 193 us; the launch traced here: 192 us
  Pallas kernels  41.7 us (22%)
  starting transfers between devices  33.6 us (17%)
  waiting for transfers between devices  33.1 us (17%)
  between operations  30.7 us (16%)
  local copies, waits for them, and re-layouts  25.5 us (13%)
  blocking collectives  12.7 us (7%)
  other arithmetic  12.3 us (6%)
  loops' own time  2.86 us (1%)
    pallas_call x10, Pallas kernels, attend(): pl.pallas_call(functools.partial(attend_kernel, tuple(kinds), latent, fre...  32.6 us
    ppermute x1, waiting for transfers between devices, handed_over(): mine = lax.ppermute(offered, 'grp', plane_swap)  25.1 us
    unnamed x23, local copies, waits for them, and re-layouts  13.8 us
    all_to_all x1, blocking collectives, body(): lax.all_to_all(term, 'ctx', split_axis=0, concat_axis=0, tiled=True)  12.7 us
    ppermute x8, starting transfers between devices, body(): from_left.append(right(from_left[-1]))  12.6 us
    ppermute x8, starting transfers between devices, body(): came = left(going_left)  10.8 us
    another operation x2, local copies, waits for them, and re-layouts  8.72 us
    ppermute x8, waiting for transfers between devices, body(): from_left.append(right(from_left[-1]))  7.94 us
  transfers between devices with their start and end apart: 31, of which 3 were waited for; matrix products, arithmetic and copies ran while one was open for 13% of the time, Pallas kernels for 17%

profile of v1, /device:TPU:0, one launch (start us, length us, event | category | flops | bytes accessed | tf_op | source)
XLA Modules:
  0.0 192.5 jit_solution(3767264831234311264)
XLA Ops:
  6.5 0.5 collective-permute-start.14
  7.0 1.5 fusion.3
  16.4 2.6 %bitcast_select_fusion = bf16[1024,576]{0,1:T(8,128)(2,1)S(1)} fusion(bf16[2048,576]{0,1:T(8,128)(2,1)S(1)} %collective-permute-done.14, s32[]{:T(128)S(6)} %select_n.109, bf16[1,2048,576]{1,2,0:T(8,128)(2,1)} %param.9, pred[]{:T(512)S(6)} %eq.41), kind=kLoop, calls=%fused_computation.3 | loop fusion | flops 589824 | bytes 3538949 | tf_op jit(solution)/shard_map/jit(_where)/select_n | solution.py:321
  19.0 2.6 %collective-permute-start.15 = (bf16[1024,576]{0,1:T(8,128)(2,1)S(1)}, bf16[1024,576]{0,1:T(8,128)(2,1)}, u32[]{:S(2)}, u32[]{:S(2)}) collective-permute-start(bf16[1024,576]{0,1:T(8,128)(2,1)S(1)} %bitcast_select_fusion), channel_id=1, source_target_pairs={{0,16},{8,24},{16,0},{24,8},{1,17},{9,25},{17,1},{25,9},{2,18},{10... | collective-permute-start | bytes 3538952 | tf_op jit(solution)/shard_map/ppermute | solution.py:326
  21.6 1.6 collective-permute-start
  23.2 25.1 %collective-permute-done.15 = bf16[1024,576]{0,1:T(8,128)(2,1)} collective-permute-done((bf16[1024,576]{0,1:T(8,128)(2,1)S(1)}, bf16[1024,576]{0,1:T(8,128)(2,1)}, u32[]{:S(2)}, u32[]{:S(2)}) %collective-permute-start.15) | collective-permute-done | bytes 1179680 | tf_op jit(solution)/shard_map/ppermute | solution.py:326
  48.3 1.8 collective-permute-start.1
  50.4 6.3 %collective-permute-done.1.refs_2_ = bf16[192,576]{1,0:T(8,128)(2,1)S(1)} collective-permute-done((bf16[192,576]{1,0:T(8,128)(2,1)S(1)}, bf16[192,576]{1,0:T(8,128)(2,1)S(1)}, u32[]{:S(2)}, u32[]{:S(2)}) %collective-permute-start.1) | collective-permute-done | bytes 221216 | tf_op jit(solution)/shard_map/ppermute | solution.py:371
  56.7 1.8 collective-permute-start.2
  58.7 0.9 slice.25
  59.6 1.8 collective-permute-start.17
  61.7 4.4 %copy.16 = bf16[1,2048,576]{2,1,0:T(8,128)(2,1)} copy(bf16[1,2048,576]{1,2,0:T(8,128)(2,1)} %param.9) | data formatting | bytes 4718592 | tf_op args[0]
  66.1 1.8 collective-permute-start.3
  67.9 0.6 fusion.1
  68.5 1.6 collective-permute-start.18
  70.1 0.4 collective-permute-start.7
  70.5 1.3 fusion.2
  72.6 1.6 collective-permute-done.18.refs_2_
  74.3 1.7 collective-permute-start.19
  76.0 3.5 %attend_send.2 = bf16[208,512]{1,0:T(8,128)(2,1)S(1)} custom-call(s32[1]{0:T(128)} %bitcast.1.refs_0_, bf16[2048,576]{1,0:T(8,128)(2,1)} %bitcast.21, bf16[192,576]{1,0:T(8,128)(2,1)S(1)} %collective-permute-done.3.refs_2_), custom_call_target="tpu_custom_call" | custom-call | flops 855638016 | bytes 4194304 | tf_op jit(solution)/shard_map/attend_send/pallas_call | solution.py:161
  88.4 1.7 collective-permute-start.24
  90.5 5.0 %attend_keep_send.2 = (f32[192,512]{1,0:T(8,128)S(1)}, f32[8,192]{1,0:T(8,128)S(1)}, bf16[208,512]{1,0:T(8,128)(2,1)S(1)}) custom-call(s32[1]{0:T(128)} %bitcast.1.refs_0_, bf16[2048,576]{1,0:T(8,128)(2,1)} %bitcast.22, bf16[192,576]{1,0:T(8,128)(2,1)S(1)} %collective-permute-done.2.refs_2_, bf16[192,576]{1,0:T(8,128)(2,1)S(1)} %collective-permute-done.7.refs_3_), custom_call_target="tpu_custom_call" | custom-call | flops 1711276032 | bytes 4194304 | tf_op jit(solution)/shard_map/attend_keep_send/pallas_call | solution.py:161
  95.5 1.8 collective-permute-start.9
  97.8 1.8 broadcast_select_fusion.1
  99.6 1.6 pad_maximum_fusion
  101.2 16.0 %conditional.1 = (bf16[2048,576]{1,0:T(8,128)(2,1)}) conditional(s32[]{:T(128)} %convert_element_type.2, (s32[]{:T(128)}, s32[]{:T(128)}, s32[]{:T(128)}, s32[]{:T(128)}, bf16[2048,576]{1,0:T(8,128)(2,1)}, /*index=5*/bf16[2048,576]{0,1:T(8,128)(2,1)}, bf16[2048,576]{0,1:T(8,128)(2,1)}, s32[]{:T(128)}) %tuple.28, (bf16[1,2048,576]{1,2,0:T(8,128)(2,1)}, ...), branch_computations={%region_3.4_spmd, %region_4.5_spmd} | conditional | flops 2359313 | bytes 44826708 | solution.py:333
  104.0 4.4 %copy.18 = bf16[2048,576]{1,0:T(8,128)(2,1)} copy(bf16[2048,576]{0,1:T(8,128)(2,1)} %get-tuple-element.155) | data formatting | bytes 4718592 | tf_op jit(solution)/shard_map
  108.4 4.3 %copy.19 = bf16[2048,576]{1,0:T(8,128)(2,1)} copy(bf16[2048,576]{0,1:T(8,128)(2,1)} %get-tuple-element.156) | data formatting | bytes 4718592 | tf_op jit(solution)/shard_map
  112.7 4.4 %select_select_fusion = bf16[2048,576]{1,0:T(8,128)(2,1)} fusion(bf16[2048,576]{1,0:T(8,128)(2,1)} %copy.19, bf16[2048,576]{1,0:T(8,128)(2,1)} %get-tuple-element.65, bf16[2048,576]{1,0:T(8,128)(2,1)} %copy.18, pred[]{:T(512)S(6)} %eq.27, pred[]{:T(512)S(6)} %eq.26), kind=kLoop, calls=%fused_computation | loop fusion | flops 2359296 | bytes 9437186 | tf_op jit(solution)/shard_map/jit(_where)/select_n | solution.py:332
  117.2 3.3 %attend_send.3 = bf16[80,512]{1,0:T(8,128)(2,1)S(1)} custom-call(s32[1]{0:T(128)} %bitcast.4.refs_0_, bf16[2048,576]{1,0:T(8,128)(2,1)} %get-tuple-element.166.refs_1_, bf16[64,576]{1,0:T(8,128)(2,1)S(1)} %collective-permute-done.20.refs_2_), custom_call_target="tpu_custom_call" | custom-call | flops 285212672 | bytes 4194304 | tf_op jit(solution)/shard_map/attend_send/pallas_call | solution.py:161
  120.5 1.9 collective-permute-start.21
  122.4 3.3 %attend_keep_keep.4 = (f32[192,512]{1,0:T(8,128)S(1)}, f32[8,192]{1,0:T(8,128)S(1)}, f32[192,512]{1,0:T(8,128)S(1)}, f32[8,192]{1,0:T(8,128)S(1)}) custom-call(s32[1]{0:T(128)} %bitcast.1.refs_0_, bf16[2048,576]{1,0:T(8,128)(2,1)S(1)} %bitcast.24, bf16[192,576]{1,0:T(8,128)(2,1)S(1)} %collective-permute-done.1.refs_2_, ...), custom_call_target="tpu_custom_call" | custom-call | flops 1711276032 | bytes 4194304 | tf_op jit(solution)/shard_map/attend_keep_keep/pallas_call | solution.py:161
  126.0 1.6 collective-permute-start.10
  128.1 2.8 %attend_keep_send.3 = (f32[64,512]{1,0:T(8,128)S(1)}, f32[8,64]{1,0:T(8,128)S(1)}, bf16[80,512]{1,0:T(8,128)(2,1)S(1)}) custom-call(s32[1]{0:T(128)} %bitcast.4.refs_0_, bf16[2048,576]{1,0:T(8,128)(2,1)S(1)} %copy-done.2, bf16[64,576]{1,0:T(8,128)(2,1)S(1)} %collective-permute-done.19.refs_2_, bf16[64,576]{1,0:T(8,128)(2,1)S(1)} %collective-permute-done.24.refs_3_), custom_call_target="tpu_custom_call" | custom-call | flops 570425344 | bytes 4194304 | tf_op jit(solution)/shard_map/attend_keep_send/pallas_call | solution.py:161
  131.4 1.7 collective-permute-start.25
  133.1 3.3 %attend_keep_keep.5 = (f32[192,512]{1,0:T(8,128)S(1)}, f32[8,192]{1,0:T(8,128)S(1)}, f32[192,512]{1,0:T(8,128)S(1)}, f32[8,192]{1,0:T(8,128)S(1)}) custom-call(s32[1]{0:T(128)} %bitcast.1.refs_0_, bf16[2048,576]{1,0:T(8,128)(2,1)S(1)} %bitcast.25, bf16[192,576]{1,0:T(8,128)(2,1)S(1)} %collective-permute-done.refs_2_, ...), custom_call_target="tpu_custom_call" | custom-call | flops 1711276032 | bytes 4194304 | tf_op jit(solution)/shard_map/attend_keep_keep/pallas_call | solution.py:161
  136.6 1.6 collective-permute-start.12
  138.7 2.8 %attend_keep_keep.6 = (f32[64,512]{1,0:T(8,128)S(1)}, f32[8,64]{1,0:T(8,128)S(1)}, f32[64,512]{1,0:T(8,128)S(1)}, f32[8,64]{1,0:T(8,128)S(1)}) custom-call(s32[1]{0:T(128)} %bitcast.4.refs_0_, bf16[2048,576]{1,0:T(8,128)(2,1)S(1)} %copy-done.2, bf16[64,576]{1,0:T(8,128)(2,1)S(1)} %collective-permute-done.18.refs_2_, ...), custom_call_target="tpu_custom_call" | custom-call | flops 570425344 | bytes 4194304 | tf_op jit(solution)/shard_map/attend_keep_keep/pallas_call | solution.py:161
  141.7 1.6 collective-permute-start.27
  143.8 4.6 %attend_keep_keep.7 = (f32[64,512]{1,0:T(8,128)S(1)}, f32[8,64]{1,0:T(8,128)S(1)}, f32[64,512]{1,0:T(8,128)S(1)}, f32[8,64]{1,0:T(8,128)S(1)}) custom-call(s32[1]{0:T(128)} %bitcast.4.refs_0_, bf16[2048,576]{1,0:T(8,128)(2,1)} %get-tuple-element.166.refs_1_, bf16[64,576]{1,0:T(8,128)(2,1)S(1)} %collective-permute-done.17.refs_2_, ...), custom_call_target="tpu_custom_call" | custom-call | flops 570425344 | bytes 4194304 | tf_op jit(solution)/shard_map/attend_keep_keep/pallas_call | solution.py:161
  148.6 1.6 collective-permute-start.29
  150.7 2.2 %attend_own.2 = (f32[192,512]{1,0:T(8,128)S(1)}, f32[8,192]{1,0:T(8,128)S(1)}) custom-call(s32[1]{0:T(128)} %bitcast.1.refs_0_, bf16[2048,576]{1,0:T(8,128)(2,1)S(1)} %bitcast.26, bf16[192,576]{1,0:T(8,128)(2,1)S(1)} %bitcast.19, bf16[16,576]{1,0:T(8,128)(2,1)S(1)} %reshape.19.refs_3_), custom_call_target="tpu_custom_call" | custom-call | flops 855638016 | bytes 4194304 | tf_op jit(solution)/shard_map/attend_own/pallas_call | solution.py:161
  152.9 1.8 attend_own.3
  154.8 0.6 finish.1.values_ref
  155.5 9.3 %copy-done = bf16[2048,7168]{1,0:T(8,128)(2,1)S(1)} copy-done((bf16[2048,7168]{1,0:T(8,128)(2,1)S(1)}, bf16[2048,7168]{1,0:T(8,128)(2,1)}, u32[]{:S(2)}) %copy-start) | copy-done | bytes 29360152
  164.8 7.5 %project.1 = bf16[8,16,896]{2,1,0:T(8,128)(2,1)S(1)} custom-call(bf16[16,2048]{1,0:T(8,128)(2,1)S(1)} %finish.1.values_ref, bf16[2048,7168]{1,0:T(8,128)(2,1)S(1)} %copy-done), custom_call_target="tpu_custom_call" | custom-call | flops 469762048 | bytes 29360128 | tf_op jit(solution)/shard_map/project/pallas_call | solution.py:282
  172.3 12.7 %all_to_all.5 = bf16[8,16,896]{2,1,0:T(8,128)(2,1)S(1)} all-to-all(bf16[8,16,896]{2,1,0:T(8,128)(2,1)S(1)} %project.1), channel_id=1, replica_groups=mesh['grp'=4,'ctx'=8] {'ctx'}, dimensions={0} | all-to-all | bytes 458752 | tf_op jit(solution)/shard_map/all_to_all | solution.py:405
  185.0 0.6 reshape.21
  (71 shorter events, 5.4 us)
Async XLA Ops:
  6.5 15.0 %copy-start.7 = (bf16[4,1,4,16,576]{4,3,2,1,0:T(8,128)(2,1)S(1)}, bf16[4,1,4,16,576]{4,3,2,1,0:T(8,128)(2,1)}, u32[]{:S(2)}) copy-start(bf16[4,1,4,16,576]{4,3,2,1,0:T(8,128)(2,1)} %param.10) | copy-start | bytes 884740
  6.5 9.8 %collective-permute-start.14 = (bf16[2048,576]{0,1:T(8,128)(2,1)}, bf16[2048,576]{0,1:T(8,128)(2,1)S(1)}, u32[]{:S(2)}, u32[]{:S(2)}) collective-permute-start(bf16[2048,576]{0,1:T(8,128)(2,1)} %bitcast.20), channel_id=1, source_target_pairs={{0,8},{8,0},{16,24},{24,16},{1,9},{9,1},{17,25},{25,17},{2,10},{10... | collective-permute-start | bytes 7077896 | tf_op jit(solution)/shard_map/ppermute | solution.py:313
  16.4 31.9 %copy-start.6 = (bf16[2048,576]{0,1:T(8,128)(2,1)}, bf16[2048,576]{0,1:T(8,128)(2,1)S(1)}, u32[]{:S(2)}) copy-start(bf16[2048,576]{0,1:T(8,128)(2,1)S(1)} %collective-permute-done.14) | copy-start | bytes 7077892
  19.0 29.3 %collective-permute-start.15 = (bf16[1024,576]{0,1:T(8,128)(2,1)S(1)}, bf16[1024,576]{0,1:T(8,128)(2,1)}, u32[]{:S(2)}, u32[]{:S(2)}) collective-permute-start(bf16[1024,576]{0,1:T(8,128)(2,1)S(1)} %bitcast_select_fusion), channel_id=1, source_target_pairs={{0,16},{8,24},{16,0},{24,8},{1,17},{9,25},{17,1},{25,9},{2,18},{10... | collective-permute-start | bytes 3538952 | tf_op jit(solution)/shard_map/ppermute | solution.py:326
  21.6 26.7 %collective-permute-start = (bf16[192,576]{1,0:T(8,128)(2,1)S(1)}, bf16[192,576]{1,0:T(8,128)(2,1)S(1)}, u32[]{:S(2)}, u32[]{:S(2)}) collective-permute-start(bf16[192,576]{1,0:T(8,128)(2,1)S(1)} %bitcast.17), channel_id=1, source_target_pairs={{0,2},{2,4},{4,6},{6,7},{7,5},{5,3},{3,1},{1,0},{8,10},{10,12},{12... | collective-permute-start | bytes 663560 | tf_op jit(solution)/shard_map/ppermute | solution.py:371
  48.3 49.5 %collective-permute-start.16 = (bf16[1024,576]{0,1:T(8,128)(2,1)}, bf16[1024,576]{0,1:T(8,128)(2,1)}, u32[]{:S(2)}, u32[]{:S(2)}) collective-permute-start(bf16[1024,576]{0,1:T(8,128)(2,1)} %collective-permute-done.15), channel_id=1, source_target_pairs={{0,8},{8,0},{16,24},{24,16},{1,9},{9,1},{17,25},{25,17},{2,10},{10... | collective-permute-start | bytes 3538952 | tf_op jit(solution)/shard_map/ppermute | solution.py:327
  48.3 8.4 %collective-permute-start.1 = (bf16[192,576]{1,0:T(8,128)(2,1)S(1)}, bf16[192,576]{1,0:T(8,128)(2,1)S(1)}, u32[]{:S(2)}, u32[]{:S(2)}) collective-permute-start(bf16[192,576]{1,0:T(8,128)(2,1)S(1)} %collective-permute-done.refs_2_), channel_id=1, source_target_pairs={{0,2},{2,4},{4,6},{6,7},{7,5},{5,3},{3,1},{1,0},{8,10},{10,12},{12... | collective-permute-start | bytes 663560 | tf_op jit(solution)/shard_map/ppermute | solution.py:371
  50.2 8.3 %collective-permute-start.5 = (bf16[192,576]{1,0:T(8,128)(2,1)S(1)}, bf16[192,576]{1,0:T(8,128)(2,1)S(1)}, u32[]{:S(2)}, u32[]{:S(2)}) collective-permute-start(bf16[192,576]{1,0:T(8,128)(2,1)S(1)} %bitcast.18), channel_id=1, source_target_pairs={{2,0},{4,2},{6,4},{7,6},{5,7},{3,5},{1,3},{0,1},{10,8},{12,10},{14... | collective-permute-start | bytes 663560 | tf_op jit(solution)/shard_map/ppermute | solution.py:373
  56.7 9.4 %collective-permute-start.2 = (bf16[192,576]{1,0:T(8,128)(2,1)S(1)}, bf16[192,576]{1,0:T(8,128)(2,1)S(1)}, u32[]{:S(2)}, u32[]{:S(2)}) collective-permute-start(bf16[192,576]{1,0:T(8,128)(2,1)S(1)} %collective-permute-done.1.refs_2_), channel_id=1, source_target_pairs={{0,2},{2,4},{4,6},{6,7},{7,5},{5,3},{3,1},{1,0},{8,10},{10,12},{12... | collective-permute-start | bytes 663560 | tf_op jit(solution)/shard_map/ppermute | solution.py:371
  58.5 11.6 %collective-permute-start.6 = (bf16[192,576]{1,0:T(8,128)(2,1)S(1)}, bf16[192,576]{1,0:T(8,128)(2,1)S(1)}, u32[]{:S(2)}, u32[]{:S(2)}) collective-permute-start(bf16[192,576]{1,0:T(8,128)(2,1)S(1)} %collective-permute-done.5.refs_3_), channel_id=1, source_target_pairs={{2,0},{4,2},{6,4},{7,6},{5,7},{3,5},{1,3},{0,1},{10,8},{12,10},{14... | collective-permute-start | bytes 663560 | tf_op jit(solution)/shard_map/ppermute | solution.py:373
  59.6 8.3 %copy-start.9 = (s32[4]{0:T(128)S(1)}, s32[4]{0:T(128)}, u32[]{:S(2)}) copy-start(s32[4]{0:T(128)} %param.13) | copy-start | bytes 52
  59.6 10.9 %copy-start.10 = (s32[4]{0:T(128)S(1)}, s32[4]{0:T(128)}, u32[]{:S(2)}) copy-start(s32[4]{0:T(128)} %param.12) | copy-start | bytes 52
  59.6 8.9 %collective-permute-start.17 = (bf16[64,576]{1,0:T(8,128)(2,1)S(1)}, bf16[64,576]{1,0:T(8,128)(2,1)S(1)}, u32[]{:S(2)}, u32[]{:S(2)}) collective-permute-start(bf16[64,576]{1,0:T(8,128)(2,1)S(1)} %bitcast.14), channel_id=1, source_target_pairs={{0,2},{2,4},{4,6},{6,7},{7,5},{5,3},{3,1},{1,0},{8,10},{10,12},{12... | collective-permute-start | bytes 221192 | tf_op jit(solution)/shard_map/ppermute | solution.py:371
  61.5 10.9 %collective-permute-start.22 = (bf16[64,576]{1,0:T(8,128)(2,1)S(1)}, bf16[64,576]{1,0:T(8,128)(2,1)S(1)}, u32[]{:S(2)}, u32[]{:S(2)}) collective-permute-start(bf16[64,576]{1,0:T(8,128)(2,1)S(1)} %bitcast.15), channel_id=1, source_target_pairs={{2,0},{4,2},{6,4},{7,6},{5,7},{3,5},{1,3},{0,1},{10,8},{12,10},{14... | collective-permute-start | bytes 221192 | tf_op jit(solution)/shard_map/ppermute | solution.py:373
  66.1 10.0 %collective-permute-start.3 = (bf16[192,576]{1,0:T(8,128)(2,1)S(1)}, bf16[192,576]{1,0:T(8,128)(2,1)S(1)}, u32[]{:S(2)}, u32[]{:S(2)}) collective-permute-start(bf16[192,576]{1,0:T(8,128)(2,1)S(1)} %collective-permute-done.2.refs_2_), channel_id=1, source_target_pairs={{0,2},{2,4},{4,6},{6,7},{7,5},{5,3},{3,1},{1,0},{8,10},{10,12},{12... | collective-permute-start | bytes 663560 | tf_op jit(solution)/shard_map/ppermute | solution.py:371
  68.5 5.8 %collective-permute-start.18 = (bf16[64,576]{1,0:T(8,128)(2,1)S(1)}, bf16[64,576]{1,0:T(8,128)(2,1)S(1)}, u32[]{:S(2)}, u32[]{:S(2)}) collective-permute-start(bf16[64,576]{1,0:T(8,128)(2,1)S(1)} %collective-permute-done.17.refs_2_), channel_id=1, source_target_pairs={{0,2},{2,4},{4,6},{6,7},{7,5},{5,3},{3,1},{1,0},{8,10},{10,12},{12... | collective-permute-start | bytes 221192 | tf_op jit(solution)/shard_map/ppermute | solution.py:371
  70.1 20.4 %collective-permute-start.7 = (bf16[192,576]{1,0:T(8,128)(2,1)S(1)}, bf16[192,576]{1,0:T(8,128)(2,1)S(1)}, u32[]{:S(2)}, u32[]{:S(2)}) collective-permute-start(bf16[192,576]{1,0:T(8,128)(2,1)S(1)} %collective-permute-done.6.refs_3_), channel_id=1, source_target_pairs={{2,0},{4,2},{6,4},{7,6},{5,7},{3,5},{1,3},{0,1},{10,8},{12,10},{14... | collective-permute-start | bytes 663560 | tf_op jit(solution)/shard_map/ppermute | solution.py:373
  72.4 16.0 %collective-permute-start.23 = (bf16[64,576]{1,0:T(8,128)(2,1)S(1)}, bf16[64,576]{1,0:T(8,128)(2,1)S(1)}, u32[]{:S(2)}, u32[]{:S(2)}) collective-permute-start(bf16[64,576]{1,0:T(8,128)(2,1)S(1)} %collective-permute-done.22.refs_3_), channel_id=1, source_target_pairs={{2,0},{4,2},{6,4},{7,6},{5,7},{3,5},{1,3},{0,1},{10,8},{12,10},{14... | collective-permute-start | bytes 221192 | tf_op jit(solution)/shard_map/ppermute | solution.py:373
  74.3 15.8 %collective-permute-start.19 = (bf16[64,576]{1,0:T(8,128)(2,1)S(1)}, bf16[64,576]{1,0:T(8,128)(2,1)S(1)}, u32[]{:S(2)}, u32[]{:S(2)}) collective-permute-start(bf16[64,576]{1,0:T(8,128)(2,1)S(1)} %collective-permute-done.18.refs_2_), channel_id=1, source_target_pairs={{0,2},{2,4},{4,6},{6,7},{7,5},{5,3},{3,1},{1,0},{8,10},{10,12},{12... | collective-permute-start | bytes 221192 | tf_op jit(solution)/shard_map/ppermute | solution.py:371
  79.5 17.7 %collective-permute-start.4 = (bf16[208,512]{1,0:T(8,128)(2,1)S(1)}, bf16[208,512]{1,0:T(8,128)(2,1)S(1)}, u32[]{:S(2)}, u32[]{:S(2)}) collective-permute-start(bf16[208,512]{1,0:T(8,128)(2,1)S(1)} %attend_send.2), channel_id=1, source_target_pairs={{2,0},{4,2},{6,4},{7,6},{5,7},{3,5},{1,3},{0,1},{10,8},{12,10},{14... | collective-permute-start | bytes 638984 | tf_op jit(solution)/shard_map/ppermute | solution.py:391
  88.4 39.7 %collective-permute-start.24 = (bf16[64,576]{1,0:T(8,128)(2,1)S(1)}, bf16[64,576]{1,0:T(8,128)(2,1)S(1)}, u32[]{:S(2)}, u32[]{:S(2)}) collective-permute-start(bf16[64,576]{1,0:T(8,128)(2,1)S(1)} %collective-permute-done.23.refs_3_), channel_id=1, source_target_pairs={{2,0},{4,2},{6,4},{7,6},{5,7},{3,5},{1,3},{0,1},{10,8},{12,10},{14... | collective-permute-start | bytes 221192 | tf_op jit(solution)/shard_map/ppermute | solution.py:373
  90.1 27.1 %collective-permute-start.20 = (bf16[64,576]{1,0:T(8,128)(2,1)S(1)}, bf16[64,576]{1,0:T(8,128)(2,1)S(1)}, u32[]{:S(2)}, u32[]{:S(2)}) collective-permute-start(bf16[64,576]{1,0:T(8,128)(2,1)S(1)} %collective-permute-done.19.refs_2_), channel_id=1, source_target_pairs={{0,2},{2,4},{4,6},{6,7},{7,5},{5,3},{3,1},{1,0},{8,10},{10,12},{12... | collective-permute-start | bytes 221192 | tf_op jit(solution)/shard_map/ppermute | solution.py:371
  95.5 30.2 %collective-permute-start.9 = (bf16[208,512]{1,0:T(8,128)(2,1)S(1)}, bf16[208,512]{1,0:T(8,128)(2,1)S(1)}, u32[]{:S(2)}, u32[]{:S(2)}) collective-permute-start(bf16[208,512]{1,0:T(8,128)(2,1)S(1)} %get-tuple-element.108), channel_id=1, source_target_pairs={{0,2},{2,4},{4,6},{6,7},{7,5},{5,3},{3,1},{1,0},{8,10},{10,12},{12... | collective-permute-start | bytes 638984 | tf_op jit(solution)/shard_map/ppermute | solution.py:396
  97.4 28.3 %collective-permute-start.8 = (bf16[208,512]{1,0:T(8,128)(2,1)S(1)}, bf16[208,512]{1,0:T(8,128)(2,1)S(1)}, u32[]{:S(2)}, u32[]{:S(2)}) collective-permute-start(bf16[208,512]{1,0:T(8,128)(2,1)S(1)} %merge.6), channel_id=1, source_target_pairs={{2,0},{4,2},{6,4},{7,6},{5,7},{3,5},{1,3},{0,1},{10,8},{12,10},{14... | collective-permute-start | bytes 638984 | tf_op jit(solution)/shard_map/ppermute | solution.py:391
  117.2 5.2 %copy-start.4 = (bf16[1,2048,576]{2,1,0:T(8,128)(2,1)S(1)}, bf16[1,2048,576]{2,1,0:T(8,128)(2,1)}, u32[]{:S(2)}) copy-start(bf16[1,2048,576]{2,1,0:T(8,128)(2,1)} %copy.16) | copy-start | bytes 7077892
  120.5 7.5 %copy-start.2 = (bf16[2048,576]{1,0:T(8,128)(2,1)S(1)}, bf16[2048,576]{1,0:T(8,128)(2,1)}, u32[]{:S(2)}) copy-start(bf16[2048,576]{1,0:T(8,128)(2,1)} %get-tuple-element.166.refs_1_) | copy-start | bytes 7077892
  120.5 10.7 %collective-permute-start.21 = (bf16[80,512]{1,0:T(8,128)(2,1)S(1)}, bf16[80,512]{1,0:T(8,128)(2,1)S(1)}, u32[]{:S(2)}, u32[]{:S(2)}) collective-permute-start(bf16[80,512]{1,0:T(8,128)(2,1)S(1)} %attend_send.3), channel_id=1, source_target_pairs={{2,0},{4,2},{6,4},{7,6},{5,7},{3,5},{1,3},{0,1},{10,8},{12,10},{14... | collective-permute-start | bytes 245768 | tf_op jit(solution)/shard_map/ppermute | solution.py:391
  126.0 10.4 %collective-permute-start.10 = (bf16[208,512]{1,0:T(8,128)(2,1)S(1)}, bf16[208,512]{1,0:T(8,128)(2,1)S(1)}, u32[]{:S(2)}, u32[]{:S(2)}) collective-permute-start(bf16[208,512]{1,0:T(8,128)(2,1)S(1)} %get-tuple-element.111), channel_id=1, source_target_pairs={{2,0},{4,2},{6,4},{7,6},{5,7},{3,5},{1,3},{0,1},{10,8},{12,10},{14... | collective-permute-start | bytes 638984 | tf_op jit(solution)/shard_map/ppermute | solution.py:391
  127.6 8.8 %collective-permute-start.11 = (bf16[208,512]{1,0:T(8,128)(2,1)S(1)}, bf16[208,512]{1,0:T(8,128)(2,1)S(1)}, u32[]{:S(2)}, u32[]{:S(2)}) collective-permute-start(bf16[208,512]{1,0:T(8,128)(2,1)S(1)} %get-tuple-element.114), channel_id=1, source_target_pairs={{0,2},{2,4},{4,6},{6,7},{7,5},{5,3},{3,1},{1,0},{8,10},{10,12},{12... | collective-permute-start | bytes 638984 | tf_op jit(solution)/shard_map/ppermute | solution.py:396
  130.8 10.7 %collective-permute-start.26 = (bf16[80,512]{1,0:T(8,128)(2,1)S(1)}, bf16[80,512]{1,0:T(8,128)(2,1)S(1)}, u32[]{:S(2)}, u32[]{:S(2)}) collective-permute-start(bf16[80,512]{1,0:T(8,128)(2,1)S(1)} %get-tuple-element.125), channel_id=1, source_target_pairs={{0,2},{2,4},{4,6},{6,7},{7,5},{5,3},{3,1},{1,0},{8,10},{10,12},{12... | collective-permute-start | bytes 245768 | tf_op jit(solution)/shard_map/ppermute | solution.py:396
  131.4 10.1 %collective-permute-start.25 = (bf16[80,512]{1,0:T(8,128)(2,1)S(1)}, bf16[80,512]{1,0:T(8,128)(2,1)S(1)}, u32[]{:S(2)}, u32[]{:S(2)}) collective-permute-start(bf16[80,512]{1,0:T(8,128)(2,1)S(1)} %merge.9), channel_id=1, source_target_pairs={{2,0},{4,2},{6,4},{7,6},{5,7},{3,5},{1,3},{0,1},{10,8},{12,10},{14... | collective-permute-start | bytes 245768 | tf_op jit(solution)/shard_map/ppermute | solution.py:391
  136.4 7.4 %copy-start.8 = (bf16[4,1,4,576]{3,2,1,0:T(4,128)(2,1)S(1)}, bf16[4,1,4,576]{3,2,1,0:T(4,128)(2,1)}, u32[]{:S(2)}) copy-start(bf16[4,1,4,576]{3,2,1,0:T(4,128)(2,1)} %param.11) | copy-start | bytes 55300
  136.6 18.1 %collective-permute-start.12 = (bf16[208,512]{1,0:T(8,128)(2,1)S(1)}, bf16[208,512]{1,0:T(8,128)(2,1)S(1)}, u32[]{:S(2)}, u32[]{:S(2)}) collective-permute-start(bf16[208,512]{1,0:T(8,128)(2,1)S(1)} %get-tuple-element.117), channel_id=1, source_target_pairs={{2,0},{4,2},{6,4},{7,6},{5,7},{3,5},{1,3},{0,1},{10,8},{12,10},{14... | collective-permute-start | bytes 638984 | tf_op jit(solution)/shard_map/ppermute | solution.py:391
  138.3 16.5 %collective-permute-start.13 = (bf16[208,512]{1,0:T(8,128)(2,1)S(1)}, bf16[208,512]{1,0:T(8,128)(2,1)S(1)}, u32[]{:S(2)}, u32[]{:S(2)}) collective-permute-start(bf16[208,512]{1,0:T(8,128)(2,1)S(1)} %get-tuple-element.118), channel_id=1, source_target_pairs={{0,2},{2,4},{4,6},{6,7},{7,5},{5,3},{3,1},{1,0},{8,10},{10,12},{12... | collective-permute-start | bytes 638984 | tf_op jit(solution)/shard_map/ppermute | solution.py:396
  141.7 6.8 %collective-permute-start.27 = (bf16[80,512]{1,0:T(8,128)(2,1)S(1)}, bf16[80,512]{1,0:T(8,128)(2,1)S(1)}, u32[]{:S(2)}, u32[]{:S(2)}) collective-permute-start(bf16[80,512]{1,0:T(8,128)(2,1)S(1)} %get-tuple-element.128), channel_id=1, source_target_pairs={{2,0},{4,2},{6,4},{7,6},{5,7},{3,5},{1,3},{0,1},{10,8},{12,10},{14... | collective-permute-start | bytes 245768 | tf_op jit(solution)/shard_map/ppermute | solution.py:391
  143.3 5.2 %collective-permute-start.28 = (bf16[80,512]{1,0:T(8,128)(2,1)S(1)}, bf16[80,512]{1,0:T(8,128)(2,1)S(1)}, u32[]{:S(2)}, u32[]{:S(2)}) collective-permute-start(bf16[80,512]{1,0:T(8,128)(2,1)S(1)} %get-tuple-element.131), channel_id=1, source_target_pairs={{0,2},{2,4},{4,6},{6,7},{7,5},{5,3},{3,1},{1,0},{8,10},{10,12},{12... | collective-permute-start | bytes 245768 | tf_op jit(solution)/shard_map/ppermute | solution.py:396
  143.8 6.9 %copy-start.5 = (bf16[1,2048,576]{2,1,0:T(8,128)(2,1)S(1)}, bf16[1,2048,576]{2,1,0:T(8,128)(2,1)}, u32[]{:S(2)}) copy-start(bf16[1,2048,576]{2,1,0:T(8,128)(2,1)} %copy.16) | copy-start | bytes 7077892
  148.4 4.5 %copy-start.3 = (bf16[2048,576]{1,0:T(8,128)(2,1)S(1)}, bf16[2048,576]{1,0:T(8,128)(2,1)}, u32[]{:S(2)}) copy-start(bf16[2048,576]{1,0:T(8,128)(2,1)} %get-tuple-element.166.refs_1_) | copy-start | bytes 7077892
  148.6 6.2 %collective-permute-start.29 = (bf16[80,512]{1,0:T(8,128)(2,1)S(1)}, bf16[80,512]{1,0:T(8,128)(2,1)S(1)}, u32[]{:S(2)}, u32[]{:S(2)}) collective-permute-start(bf16[80,512]{1,0:T(8,128)(2,1)S(1)} %get-tuple-element.134), channel_id=1, source_target_pairs={{2,0},{4,2},{6,4},{7,6},{5,7},{3,5},{1,3},{0,1},{10,8},{12,10},{14... | collective-permute-start | bytes 245768 | tf_op jit(solution)/shard_map/ppermute | solution.py:391
  150.2 4.6 %copy-start.1 = (bf16[16,512,128]{2,1,0:T(8,128)(2,1)S(1)}, bf16[16,512,128]{2,1,0:T(8,128)(2,1)}, u32[]{:S(2)}) copy-start(bf16[16,512,128]{2,1,0:T(8,128)(2,1)} %refs_8_.1) | copy-start | bytes 6291460
  150.2 4.6 %collective-permute-start.30 = (bf16[80,512]{1,0:T(8,128)(2,1)S(1)}, bf16[80,512]{1,0:T(8,128)(2,1)S(1)}, u32[]{:S(2)}, u32[]{:S(2)}) collective-permute-start(bf16[80,512]{1,0:T(8,128)(2,1)S(1)} %get-tuple-element.135), channel_id=1, source_target_pairs={{0,2},{2,4},{4,6},{6,7},{7,5},{5,3},{3,1},{1,0},{8,10},{10,12},{12... | collective-permute-start | bytes 245768 | tf_op jit(solution)/shard_map/ppermute | solution.py:396
  155.5 9.4 %copy-start = (bf16[2048,7168]{1,0:T(8,128)(2,1)S(1)}, bf16[2048,7168]{1,0:T(8,128)(2,1)}, u32[]{:S(2)}) copy-start(bf16[2048,7168]{1,0:T(8,128)(2,1)} %weight_ref.1) | copy-start | bytes 88080384

commit v2 on v0

v2 whole, which is shorter than its diff:
```python
import functools

import jax
import jax.numpy as jnp
from jax import lax
from jax.experimental import pallas as pl
from jax.experimental.pallas import tpu as pltpu
from jax.sharding import PartitionSpec as P

HANDOVER = 3
EXTRA = 16
MIB = 1 << 20

score_scale = 192.0 ** (-0.5)
far_below = -1e30

ROWS_BY_ROWS = (((1,), (1,)), ((), ()))


def diagonal(n):
    return lax.broadcasted_iota(jnp.int32, (n, n), 0) == lax.broadcasted_iota(jnp.int32, (n, n), 1)


def to_row(column):
    n = column.shape[0]
    return jnp.sum(jnp.where(diagonal(n), column, 0.0), axis=0, keepdims=True)


def to_column(row):
    n = row.shape[1]
    return jnp.sum(jnp.where(diagonal(n), row, 0.0), axis=1, keepdims=True)


def split_three(value):
    high = value.astype(jnp.bfloat16).astype(jnp.float32)
    rest = value - high
    middle = rest.astype(jnp.bfloat16).astype(jnp.float32)
    return high, middle, rest - middle


def sections_of(rows):
    return 2 if rows % 32 == 0 else 1


def store_packed(out_ref, sections):
    rows, width = sections[0][0].shape
    end = rows * len(sections)
    line = lax.broadcasted_iota(jnp.int32, (EXTRA, rows), 0)
    block = jnp.zeros((EXTRA, rows), jnp.float32)
    for at, (part, peak, total) in enumerate(sections):
        out_ref[at * rows : (at + 1) * rows, :] = part.astype(jnp.bfloat16)
        for index, piece in enumerate(split_three(peak) + split_three(total)):
            block = jnp.where(line == 6 * at + index, piece, block)
    if rows < width:
        out_ref[end : end + EXTRA, :] = jnp.zeros((EXTRA, width), jnp.bfloat16)
    out_ref[end : end + EXTRA, 0:rows] = block.astype(jnp.bfloat16)


def load_packed(ref, rows, at):
    end = ref.shape[0] - EXTRA
    block = ref[end : end + EXTRA, 0:rows].astype(jnp.float32)
    line = [block[6 * at + i : 6 * at + i + 1] for i in range(6)]
    part = ref[at * rows : (at + 1) * rows, :].astype(jnp.float32)
    return part, line[0] + line[1] + line[2], line[3] + line[4] + line[5]


def load_kept(part_ref, stats_ref, at):
    rows = stats_ref.shape[1]
    part = part_ref[at * rows : (at + 1) * rows, :]
    return part, stats_ref[2 * at : 2 * at + 1, :], stats_ref[2 * at + 1 : 2 * at + 2, :]


def combine(*parts):
    peak = functools.reduce(jnp.maximum, [part[1] for part in parts])
    factors = [jnp.exp(part[1] - peak) for part in parts]
    total = sum(part[2] * factor for part, factor in zip(parts, factors))
    merged = sum(part[0] * to_column(factor) for part, factor in zip(parts, factors))
    return merged, peak, total


def attend_block(query, cache_ref, limit, score_ref, latent):
    rows = query.shape[0]
    length = cache_ref.shape[1]
    tile = min(512, length)
    peak = jnp.full((rows, 1), far_below, jnp.float32)
    for start in range(0, length, tile):
        scores = (
            jnp.dot(
                query, cache_ref[:, start : start + tile], preferred_element_type=jnp.float32
            )
            * score_scale
        )
        position = start + lax.broadcasted_iota(jnp.int32, (1, tile), 1)
        scores = jnp.where(position < limit, scores, far_below)
        score_ref[0:rows, start : start + tile] = scores
        peak = jnp.maximum(peak, jnp.max(scores, axis=1, keepdims=True))
    total = jnp.zeros((rows, 1), jnp.float32)
    part = jnp.zeros((rows, latent), jnp.float32)
    for start in range(0, length, tile):
        weights = jnp.exp(score_ref[0:rows, start : start + tile] - peak)
        total = total + jnp.sum(weights, axis=1, keepdims=True)
        part = part + lax.dot_general(
            weights.astype(jnp.bfloat16),
            cache_ref[0:latent, start : start + tile],
            ROWS_BY_ROWS,
            preferred_element_type=jnp.float32,
        )
    some = limit > 0
    return peak, jnp.where(some, total, 0.0), jnp.where(some, part, 0.0)


def fresh_block(query, fresh_ref, rows_ref, first_step, heads, latent):
    steps, samples, _ = fresh_ref.shape
    for step in range(steps):
        rows_ref[step * samples : (step + 1) * samples, :] = fresh_ref[step].astype(jnp.float32)
    fresh = rows_ref[...].astype(jnp.bfloat16)
    rows, columns = query.shape[0], fresh.shape[0]
    scores = (
        lax.dot_general(query, fresh, ROWS_BY_ROWS, preferred_element_type=jnp.float32)
        * score_scale
    )
    row = lax.broadcasted_iota(jnp.int32, (rows, columns), 0) // heads
    column = lax.broadcasted_iota(jnp.int32, (rows, columns), 1)
    seen = (column % samples == row % samples) & (column // samples <= row // samples + first_step)
    scores = jnp.where(seen, scores, far_below)
    peak = jnp.max(scores, axis=1, keepdims=True)
    weights = jnp.where(seen, jnp.exp(scores - peak), 0.0)
    total = jnp.sum(weights, axis=1, keepdims=True)
    part = jnp.dot(
        weights,
        rows_ref[:, 0:latent],
        precision=lax.Precision.HIGHEST,
        preferred_element_type=jnp.float32,
    )
    return peak, total, part


def fetch_rows(info_ref, near, halves, cache_ref, sem):
    me, source = info_ref[2], info_ref[3]
    half = halves[0].shape[0]

    def whole_copy(ref):
        copy = pltpu.make_async_copy(ref, cache_ref, sem.at[0])
        copy.start()
        copy.wait()

    @pl.when(source == me)
    def _():
        whole_copy(near[0])

    @pl.when((source != me) & ((source >> 1) == (me >> 1)))
    def _():
        whole_copy(near[1])

    @pl.when((source >> 1) != (me >> 1))
    def _():
        core = me & 1
        copies = [
            pltpu.make_async_copy(
                ref, cache_ref.at[pl.ds(pl.multiple_of(at * half, 16), half), :], sem.at[slot]
            )
            for slot, (ref, at) in enumerate(zip(halves, (core, 1 - core)))
        ]
        for copy in copies:
            copy.start()
        for copy in copies:
            copy.wait()


def attend_kernel(kinds, rows, takes, caches, limit_at, latent, fresh_info, *refs):
    refs = list(refs)
    info_ref = refs.pop(0)
    cache_refs, refs = refs[:caches], refs[caches:]
    queries, rest = refs[: len(takes)], refs[len(takes) :]
    fresh_ref = rest.pop(0) if fresh_info else None
    fresh_rows = rest.pop() if fresh_info else None
    if caches > 1:
        sem, cache_ref = rest.pop(), rest.pop(-3)
        fetch_rows(info_ref, cache_refs[:2], cache_refs[2:], cache_ref, sem)
    else:
        cache_ref = cache_refs[0]
    score_ref, query_ref = rest.pop(-2), rest.pop()
    limit = info_ref[limit_at]
    sections = sections_of(rows)
    at = 0
    for ref, (start, stop) in zip(queries, takes):
        query_ref[at : at + stop - start, :] = ref[start:stop, :]
        at += stop - start
    peaks, totals, blocks = attend_block(query_ref[...], cache_ref, limit, score_ref, latent)
    for at, kind in enumerate(kinds):
        mine = slice(at * rows, (at + 1) * rows)
        peak, total, part = peaks[mine], totals[mine], blocks[mine]
        if kind == "own":
            query = query_ref[mine, :]
            other = fresh_block(query, fresh_ref, fresh_rows, *fresh_info, latent)
            top = jnp.maximum(peak, other[0])
            one, two = jnp.exp(peak - top), jnp.exp(other[0] - top)
            total = total * one + other[1] * two
            part = part * one + other[2] * two
            peak = top
        size = rows // sections
        cut = [slice(i * size, (i + 1) * size) for i in range(sections)]
        pieces = [(part[c], to_row(peak[c]), to_row(total[c])) for c in cut]
        if kind == "ends":
            for piece in pieces:
                store_packed(rest.pop(0), [piece])
            continue
        rest.pop(0)[...] = part
        stats_ref = rest.pop(0)
        line = lax.broadcasted_iota(jnp.int32, stats_ref.shape, 0)
        stats = jnp.zeros(stats_ref.shape, jnp.float32)
        for index, piece in enumerate(pieces):
            stats = jnp.where(line == 2 * index, piece[1], stats)
            stats = jnp.where(line == 2 * index + 1, piece[2], stats)
        stats_ref[...] = stats


def whole(memory=pltpu.VMEM):
    return pl.BlockSpec(memory_space=memory)


def attend(kinds, pieces, cache_parts, info, limit_at, latent, fresh=None, fresh_info=None):
    out_shape = []
    queries = [piece[0] for piece in pieces]
    takes = tuple(piece[1:] for piece in pieces)
    key_width = queries[0].shape[1]
    total = sum(stop - start for start, stop in takes)
    rows = total // len(kinds)
    sections = sections_of(rows)
    length = cache_parts[0].shape[1]
    flops = 2 * total * length * (key_width + latent)
    for kind in kinds:
        if kind == "ends":
            shape = (rows // sections + EXTRA, latent)
            out_shape += [jax.ShapeDtypeStruct(shape, jnp.bfloat16)] * sections
        else:
            out_shape.append(jax.ShapeDtypeStruct((rows, latent), jnp.float32))
            out_shape.append(jax.ShapeDtypeStruct((8, rows // sections), jnp.float32))
    operands = [info, *cache_parts, *queries] + ([fresh] if fresh_info else [])
    caches = len(cache_parts)
    scratch = [
        pltpu.VMEM((total, length), jnp.float32),
        pltpu.VMEM((total, key_width), jnp.bfloat16),
    ]
    if caches > 1:
        out_shape.append(jax.ShapeDtypeStruct((key_width, length), jnp.bfloat16))
        scratch.append(pltpu.SemaphoreType.DMA((2,)))
    if fresh_info:
        scratch.append(pltpu.VMEM((fresh.shape[0] * fresh.shape[1], key_width), jnp.float32))
    outs = pl.pallas_call(
        functools.partial(
            attend_kernel, tuple(kinds), rows, takes, caches, limit_at, latent, fresh_info
        ),
        out_shape=out_shape,
        in_specs=[whole(pltpu.SMEM)]
        + [whole(pl.ANY if caches > 1 else pltpu.VMEM)] * caches
        + [whole()] * (len(operands) - 1 - caches),
        out_specs=[whole()] * len(out_shape),
        scratch_shapes=scratch,
        compiler_params=pltpu.CompilerParams(vmem_limit_bytes=20 * MIB),
        cost_estimate=pl.CostEstimate(
            flops=flops, bytes_accessed=4 * MIB, transcendentals=total * length
        ),
        name="attend_" + "_".join(kinds),
    )(*operands)
    outs = list(outs)
    results = []
    for kind in kinds:
        size = sections if kind == "ends" else 2
        results.append(tuple(outs[:size]))
        outs = outs[size:]
    return results + outs


def merge_kernel(covers, *refs):
    refs = list(refs)
    outs = refs[len(refs) - len(covers) :]
    for cover, out_ref in zip(covers, outs):
        packed_ref = refs.pop(0) if cover else None
        part_ref, stats_ref = refs.pop(0), refs.pop(0)
        rows = stats_ref.shape[1]
        merged = []
        for at in range(part_ref.shape[0] // rows):
            piece = load_kept(part_ref, stats_ref, at)
            if at in cover:
                piece = combine(load_packed(packed_ref, rows, cover.index(at)), piece)
            merged.append(piece)
        store_packed(out_ref, merged)


def merge(items):
    operands, out_shape = [], []
    for packed, cover, (part, stats) in items:
        operands += ([packed] if cover else []) + [part, stats]
        shape = (part.shape[0] + EXTRA, part.shape[1])
        out_shape.append(jax.ShapeDtypeStruct(shape, jnp.bfloat16))
    return pl.pallas_call(
        functools.partial(merge_kernel, tuple(cover for _, cover, _ in items)),
        grid=(1,),
        out_shape=out_shape,
        in_specs=[pl.BlockSpec(operand.shape, lambda i: (0, 0)) for operand in operands],
        out_specs=[pl.BlockSpec(shape.shape, lambda i: (0, 0)) for shape in out_shape],
        compiler_params=pltpu.CompilerParams(vmem_limit_bytes=12 * MIB),
        cost_estimate=pl.CostEstimate(flops=1 << 20, bytes_accessed=2 * MIB, transcendentals=1024),
        name="merge",
    )(*operands)


def finish_kernel(chunks, heads, tile, *refs):
    value_ref, weight_ref, out_ref, rows_ref, values_ref, tiles_ref, sem = refs[-7:]
    copies = [
        pltpu.make_async_copy(
            weight_ref.at[:, at * tile : (at + 1) * tile], tiles_ref.at[at], sem.at[at]
        )
        for at in range(tiles_ref.shape[0])
    ]
    for copy in copies:
        copy.start()
    lanes = rows_ref.shape[0]
    end = 0
    for index in range(chunks):
        left_ref, right_ref, part_ref, stats_ref = refs[4 * index : 4 * index + 4]
        rows = stats_ref.shape[1]
        for at in range(part_ref.shape[0] // rows):
            merged, _, total = combine(
                load_packed(left_ref, rows, at),
                load_packed(right_ref, rows, at),
                load_kept(part_ref, stats_ref, at),
            )
            merged = merged / to_column(total)
            for lane in range(lanes):
                rows_ref[lane, end : end + rows, :] = merged[:, lane * 128 : (lane + 1) * 128]
            end += rows
    width = value_ref.shape[2]
    for head in range(heads):
        picked = pl.ds(head, end // heads, stride=heads)
        attended = jnp.concatenate([rows_ref[lane, picked, :] for lane in range(lanes)], axis=1)
        values = jnp.dot(
            attended.astype(jnp.bfloat16), value_ref[head], preferred_element_type=jnp.float32
        )
        values_ref[:, head * width : (head + 1) * width] = values.astype(jnp.bfloat16)
    values = values_ref[...]
    for at, copy in enumerate(copies):
        copy.wait()
        share = jnp.dot(values, tiles_ref[at], preferred_element_type=jnp.float32)
        if len(out_ref.shape) == 3:
            out_ref[at] = share.astype(out_ref.dtype)
        else:
            out_ref[:, at * tile : (at + 1) * tile] = share.astype(out_ref.dtype)


def finish(chunk_parts, value_up, out_proj, parts):
    heads, latent, width = value_up.shape
    depth, columns = out_proj.shape
    operands = []
    rows = 0
    for left, right, (part, stats) in chunk_parts:
        operands += [left, right, part, stats]
        rows += part.shape[0]
    lines = rows // heads
    share = columns // parts
    if share % 128 == 0:
        tile, shape = share, (parts, lines, share)
    else:
        tile, shape = columns // 8 if columns % 1024 == 0 else columns, (lines, columns)
    out = pl.pallas_call(
        functools.partial(finish_kernel, len(chunk_parts), heads, tile),
        out_shape=jax.ShapeDtypeStruct(shape, jnp.bfloat16),
        in_specs=[whole()] * (len(operands) + 1) + [whole(pltpu.HBM)],
        out_specs=whole(),
        scratch_shapes=[
            pltpu.VMEM((latent // 128, rows, 128), jnp.float32),
            pltpu.VMEM((lines, depth), jnp.bfloat16),
            pltpu.VMEM((columns // tile, depth, tile), jnp.bfloat16),
            pltpu.SemaphoreType.DMA((columns // tile,)),
        ],
        compiler_params=pltpu.CompilerParams(vmem_limit_bytes=44 * MIB),
        cost_estimate=pl.CostEstimate(
            flops=2 * lines * depth * columns,
            bytes_accessed=2 * depth * columns,
            transcendentals=1024,
        ),
        name="finish",
    )(*operands, value_up, out_proj)
    if share % 128:
        out = out.reshape(lines, parts, share).transpose(1, 0, 2)
    return out


def plan_kernel(group_ref, place_ref, lengths_ref, donor_ref, info_ref, *, local_len, half):
    group, place = group_ref[0], place_ref[0]
    source = donor_ref[group]
    first = place * local_len
    info_ref[0] = jnp.clip(lengths_ref[group] - first, 0, local_len)
    info_ref[1] = jnp.clip(lengths_ref[source] - first, 0, local_len)
    info_ref[2] = group
    info_ref[3] = source
    core, plane = group & 1, group >> 1
    wanted, crowded = [], []
    for at in range(2):
        one, two = donor_ref[2 * at], donor_ref[2 * at + 1]
        one_far, two_far = (one >> 1) != at, (two >> 1) != at
        wanted.append(jnp.where(one_far, one, two))
        crowded.append(one_far & two_far & (one != two))
    asked = jnp.where(plane == 0, wanted[1], wanted[0])
    info_ref[4] = jnp.where((asked & 1) == core, 1, 0)
    info_ref[5] = core * half
    info_ref[6] = jnp.where(crowded[0] | crowded[1], 1, 0)
    info_ref[7] = (1 - core) * half


def plan(lengths, donor, local_len, half):
    return pl.pallas_call(
        functools.partial(plan_kernel, local_len=local_len, half=half),
        out_shape=jax.ShapeDtypeStruct((8,), jnp.int32),
        in_specs=[whole(pltpu.SMEM)] * 4,
        out_specs=whole(pltpu.SMEM),
        name="plan",
    )(
        lax.axis_index("grp").reshape(1),
        lax.axis_index("ctx").reshape(1),
        lengths,
        donor,
    )


def offer_kernel(info_ref, own_ref, beside_ref, out_ref, sem):
    half = out_ref.shape[0]
    start = pl.multiple_of((info_ref[2] & 1) * half, 16)

    @pl.when(info_ref[4] == 1)
    def _():
        copy = pltpu.make_async_copy(own_ref.at[pl.ds(start, half), :], out_ref, sem)
        copy.start()
        copy.wait()

    @pl.when(info_ref[4] != 1)
    def _():
        copy = pltpu.make_async_copy(beside_ref.at[pl.ds(start, half), :], out_ref, sem)
        copy.start()
        copy.wait()


def offer(info, own, beside):
    half = own.shape[0] // 2
    return pl.pallas_call(
        offer_kernel,
        out_shape=jax.ShapeDtypeStruct((half, own.shape[1]), own.dtype),
        in_specs=[whole(pltpu.SMEM), whole(pl.ANY), whole(pl.ANY)],
        out_specs=whole(),
        scratch_shapes=[pltpu.SemaphoreType.DMA],
        cost_estimate=pl.CostEstimate(flops=0, bytes_accessed=2 * MIB, transcendentals=0),
        name="offer",
    )(info, own, beside)


core_swap = functools.partial(lax.ppermute, axis_name="grp", perm=[(g, g ^ 1) for g in range(4)])
plane_swap = functools.partial(lax.ppermute, axis_name="grp", perm=[(g, g ^ 2) for g in range(4)])


def exchange_all(cache_t, info):
    half = cache_t.shape[0] // 2
    across = plane_swap(cache_t)
    corner = core_swap(across)
    rows = jnp.where(info[3] == info[2] ^ 2, across, corner)
    return (
        lax.dynamic_slice_in_dim(rows, info[5], half, 0),
        lax.dynamic_slice_in_dim(rows, info[7], half, 0),
    )


def tie(came, other):
    values, other = lax.optimization_barrier(([value for value, _ in came], other))
    return [(value, cover) for value, (_, cover) in zip(values, came)], other


def body(cache, queries, new_latent, lengths, donor, value_up, out_proj):
    parts = lax.axis_size("ctx")
    steps, _, samples, heads, key_width = queries.shape
    latent = value_up.shape[1]
    cache_t = jnp.swapaxes(cache[0], 0, 1)
    local_len = cache_t.shape[1]
    info = plan(lengths, donor, local_len, key_width // 2)
    fresh = new_latent.reshape(steps, samples, key_width)

    ring = list(range(0, parts, 2)) + list(range(parts - 1, 0, -2))
    to_right = [(ring[i], ring[(i + 1) % parts]) for i in range(parts)]
    to_left = [(b, a) for a, b in to_right]
    right = functools.partial(lax.ppermute, axis_name="ctx", perm=to_right)
    left = functools.partial(lax.ppermute, axis_name="ctx", perm=to_left)
    reach = parts // 2

    step_rows = samples * heads
    mine_rows = queries.reshape(steps * step_rows, key_width)
    rows, cut = steps * step_rows, HANDOVER * step_rows
    half = rows // 2 if rows % 32 == 0 else rows
    four = lax.axis_size("grp") == 4
    if four:
        beside = core_swap(cache_t)

    lefts, rights = [mine_rows], [mine_rows]

    def pieces_of(hop, start, stop):
        if hop == 0:
            return [(mine_rows, start, stop)]
        if hop < reach:
            return [(lefts[hop], start, stop), (rights[hop], start, stop)]
        found = []
        for block, first in ((lefts[hop], 0), (rights[hop], half)):
            low, high = max(start, first), min(stop, first + half)
            if low < high and block is not None:
                found.append((block, low - first, high - first))
        return found

    def attend_early(hop):
        pieces = pieces_of(hop, 0, cut)
        if hop == 0:
            return attend(["own"], pieces, [cache_t], info, 0, latent, fresh, (0, heads))
        kinds = ["ends"] if hop == reach else ["keep", "keep"]
        return attend(kinds, pieces, [cache_t], info, 0, latent)

    early_parts = []
    for hop in range(1, reach + 1):
        if hop < reach:
            came = (right(lefts[-1]), left(rights[-1]))
        else:
            came = (
                right(lefts[-1][:half]),
                left(rights[-1][half:]) if half < rows else None,
            )
        extra = offer(info, cache_t, beside) if hop == 1 and four else None
        came, extra, parts_now = lax.optimization_barrier((came, extra, attend_early(hop - 1)))
        if hop == 1 and four:
            far_half = plane_swap(extra)
        lefts.append(came[0])
        rights.append(came[1])
        early_parts.append(parts_now)
    early_parts.append(attend_early(reach))

    if four:
        far_half, lefts[reach] = lax.optimization_barrier((far_half, lefts[reach]))
        far_rest = core_swap(far_half)
        far_half, far_rest = lax.cond(
            info[6] != 0, exchange_all, lambda *_: (far_half, far_rest), cache_t, info
        )
        moved = [cache_t, beside, far_half, far_rest]
    else:
        shards = lax.all_gather(cache_t, "grp", axis=0, tiled=False)
        found = lax.dynamic_index_in_dim(shards, info[3], 0, keepdims=False)
        moved = [found, found, found[: key_width // 2], found[key_width // 2 :]]
    *late_ends, moved_rows = attend(["ends"], pieces_of(reach, cut, rows), moved, info, 1, latent)

    def start_back(ends):
        ends = ends[0]
        sections = tuple(range(len(ends)))
        return [(ends[0], (0,)), (ends[1], (1,)) if len(ends) > 1 else (None, ())], sections

    def hop_back(going):
        (to_the_left, cover_left), (to_the_right, cover_right) = going
        return [
            (left(to_the_left), cover_left),
            (right(to_the_right) if cover_right else None, cover_right),
        ]

    def merge_back(came, kept, sections):
        merged = merge([(*item, block) for item, block in zip(came, kept)])
        return [(block, sections) for block in merged]

    early_going, sections = start_back(early_parts[reach])
    early_came = hop_back(early_going)
    early_came, late_ends = tie(early_came, late_ends)
    late_going, late_sections = start_back(late_ends)
    kinds, pieces = ["own"], pieces_of(0, cut, rows)
    for hop in range(1, reach):
        kinds += ["keep", "keep"]
        pieces += pieces_of(hop, cut, rows)
    results = attend(kinds, pieces, [moved_rows], info, 1, latent, fresh, (HANDOVER, heads))
    late_came = hop_back(late_going)
    for hop in range(reach - 1, 0, -1):
        early_came = hop_back(merge_back(early_came, early_parts[hop], sections))
        if hop == reach - 1:
            values = [value for value, _ in late_came]
            early_came, (results, values) = tie(early_came, (results, values))
            late_came = [(value, cover) for value, (_, cover) in zip(values, late_came)]
    late_parts = [[results[0]]]
    for hop in range(1, reach):
        late_parts.append(results[2 * hop - 1 : 2 * hop + 1])
    for hop in range(reach - 1, 0, -1):
        late_came = hop_back(merge_back(late_came, late_parts[hop], late_sections))
    finals = [
        (came[0][0], came[1][0], own[0])
        for came, own in ((early_came, early_parts[0]), (late_came, late_parts[0]))
    ]

    term = finish(finals, value_up, out_proj, parts)
    shares = lax.all_to_all(term, "ctx", split_axis=0, concat_axis=0, tiled=True)
    mixed = jnp.sum(shares.astype(jnp.float32), axis=0).astype(jnp.bfloat16)
    return mixed.reshape(steps, 1, samples, mixed.shape[-1])


def solution(mesh):
    return jax.shard_map(
        body,
        mesh=mesh,
        in_specs=(
            P("grp", "ctx", None),
            P(None, "grp", None, "ctx", None),
            P(None, "grp", None, None),
            P(),
            P(),
            P("ctx", None, None),
            P("ctx", None),
        ),
        out_specs=P(None, "grp", None, "ctx"),
        check_vma=False,
    )
```

time: 667 us -> 113 us (0.17); the launches traced: 657 us -> 112 us
  waiting for transfers between devices: 301 us -> 21 us
  blocking collectives: 131 us -> 10.4 us
  matrix products: 100 us -> 0 us
  Pallas kernels: 0 us -> 42.7 us
  starting transfers between devices: 55.4 us -> 27.8 us
  local copies, waits for them, and re-layouts: 30.2 us -> 9.01 us
  other arithmetic: 20.6 us -> 0.04 us
  between operations: 18 us -> 1.24 us
    unnamed x9 -> x0, waiting for transfers between devices: 227 us -> none
    all_gather x4 -> x0, blocking collectives: 131 us -> none  [serve(): gathered = lax.all_gather(query_part, 'ctx', axis=2, tiled=True)]
    all_to_all x12 -> x0, waiting for transfers between devices: 73.9 us -> none  [the longest x4 45.2 us: serve(): lax.all_to_all(partial_out[None], 'ctx', split_axis=3, concat_axis=0, til...]
    unnamed x4 -> x0, matrix products: 68.3 us -> none
    all_to_all x12 -> x0, starting transfers between devices: 54.7 us -> none  [the longest x4 20.1 us: serve(): lax.all_to_all(partial_out[None], 'ctx', split_axis=3, concat_axis=0, til...]
    pallas_call x0 -> x16, Pallas kernels: none -> 42.7 us  [the longest x7 25.8 us: attend(): pl.pallas_call(functools.partial(attend_kernel, tuple(kinds), rows, takes...]
    dot_general x15 -> x0, matrix products: 31.9 us -> none  [the longest x4 13.6 us: block_partial(): jnp.dot(weights.astype(jnp.bfloat16), cache_rows[:, :latent_width], prefe...]
    ppermute x0 -> x27, starting transfers between devices: none -> 27.8 us  [the longest x8 13.4 us: hop_back(): left(to_the_left)]
  transfers between devices with their start and end apart: 17 -> 27, of which waited for: 13 -> 13; matrix products, arithmetic and copies ran while one was open for 22% -> 1% of each run, Pallas kernels for 0% -> 27%
where the time goes in v2:
time: 113 us; the launch traced here: 112 us
  Pallas kernels  42.7 us (38%)
  starting transfers between devices  27.8 us (25%)
  waiting for transfers between devices  21 us (19%)
  blocking collectives  10.4 us (9%)
  local copies, waits for them, and re-layouts  9.01 us (8%)
  between operations  1.24 us (1%)
    pallas_call x7, Pallas kernels, attend(): pl.pallas_call(functools.partial(attend_kernel, tuple(kinds), rows, takes...  25.8 us
    ppermute x8, starting transfers between devices, hop_back(): left(to_the_left)  13.4 us
    pallas_call x1, Pallas kernels, finish(): pl.pallas_call(functools.partial(finish_kernel, len(chunk_parts), heads,...  10.8 us
    all_to_all x1, blocking collectives, body(): lax.all_to_all(term, 'ctx', split_axis=0, concat_axis=0, tiled=True)  10.4 us
    unnamed x68, local copies, waits for them, and re-layouts  7.69 us
    ppermute x8, waiting for transfers between devices, hop_back(): left(to_the_left)  7.49 us
    ppermute x6, waiting for transfers between devices, body(): came = (right(lefts[-1]), left(rights[-1]))  7 us
    ppermute x6, starting transfers between devices, body(): came = (right(lefts[-1]), left(rights[-1]))  6.63 us
  transfers between devices with their start and end apart: 27, of which 13 were waited for; matrix products, arithmetic and copies ran while one was open for 1% of the time, Pallas kernels for 27%

profile of v2, /device:TPU:0, one launch (start us, length us, event | category | flops | bytes accessed | tf_op | source)
XLA Modules:
  0.0 112.4 jit_solution(15177989545049139577)
XLA Ops:
  0.5 2.6 %collective-permute-start.2 = (bf16[256,576]{1,0:T(8,128)(2,1)}, bf16[256,576]{1,0:T(8,128)(2,1)}, u32[]{:S(2)}, u32[]{:S(2)}) collective-permute-start(bf16[256,576]{1,0:T(8,128)(2,1)} %bitcast.11), channel_id=1, source_target_pairs={{0,2},{2,4},{4,6},{6,7},{7,5},{5,3},{3,1},{1,0},{8,10},{10,12},{12... | collective-permute-start | bytes 884744 | tf_op jit(solution)/shard_map/ppermute | solution.py:525
  3.0 1.3 %plan.1.info_ref.refs_0_ = s32[8]{0:T(128)S(1)} custom-call(s32[1]{0:T(128)} %bitcast.3.group_ref, s32[1]{0:T(128)} %bitcast.4.place_ref, s32[4]{0:T(128)} %lengths_ref.1, s32[4]{0:T(128)} %donor_ref.1), custom_call_target="tpu_custom_call" | custom-call | tf_op jit(solution)/shard_map/plan/pallas_call | solution.py:413
  4.3 1.0 copy-done.23
  5.3 0.7 copy-done.29
  6.0 3.9 %attend_own.1 = (f32[192,512]{1,0:T(8,128)S(1)}, f32[8,96]{1,0:T(8,128)S(1)}) custom-call(s32[8]{0:T(128)S(1)} %plan.1.info_ref.refs_0_, bf16[576,2048]{1,0:T(8,128)(2,1)} %bitcast.18, bf16[256,576]{1,0:T(8,128)(2,1)S(1)} %bitcast.13, bf16[4,4,576]{2,1,0:T(4,128)(2,1)S(1)} %bitcast.15), custom_call_target="tpu_custom_call" | custom-call | flops 855638016 | bytes 4194304 | tf_op jit(solution)/shard_map/attend_own/pallas_call | solution.py:250
  10.0 0.6 copy-done.21
  10.6 1.4 %copy-done = bf16[576,2048]{1,0:T(8,128)(2,1)} copy-done((bf16[576,2048]{1,0:T(8,128)(2,1)}, bf16[576,2048]{1,0:T(8,128)(2,1)S(1)}, u32[]{:S(2)}) %copy-start) | copy-done | bytes 2359320
  12.0 2.8 %offer.1 = bf16[288,2048]{1,0:T(8,128)(2,1)} custom-call(s32[8]{0:T(128)S(1)} %plan.1.info_ref.refs_0_, bf16[576,2048]{1,0:T(8,128)(2,1)} %bitcast.19, bf16[576,2048]{1,0:T(8,128)(2,1)} %copy-done), custom_call_target="tpu_custom_call" | custom-call | bytes 2097152 | tf_op jit(solution)/shard_map/offer/pallas_call | solution.py:446
  14.8 2.0 %collective-permute-start.13 = (bf16[288,2048]{1,0:T(8,128)(2,1)}, bf16[288,2048]{1,0:T(8,128)(2,1)}, u32[]{:S(2)}, u32[]{:S(2)}) collective-permute-start(bf16[288,2048]{1,0:T(8,128)(2,1)} %offer.1), channel_id=1, source_target_pairs={{0,16},{8,24},{16,0},{24,8},{1,17},{9,25},{17,1},{25,9},{2,18},{10... | collective-permute-start | bytes 3538952 | tf_op jit(solution)/shard_map/ppermute | solution.py:534
  16.9 1.6 %collective-permute-start.5 = (bf16[256,576]{1,0:T(8,128)(2,1)}, bf16[256,576]{1,0:T(8,128)(2,1)S(1)}, u32[]{:S(2)}, u32[]{:S(2)}) collective-permute-start(bf16[256,576]{1,0:T(8,128)(2,1)} %collective-permute-done.2.refs_2_.refs_3_), channel_id=1, source_target_pairs={{0,2},{2,4},{4,6},{6,7},{7,5},{5,3},{3,1},{1,0},{8,10},{10,12},{12... | collective-permute-start | bytes 884744 | tf_op jit(solution)/shard_map/ppermute | solution.py:525
  18.9 4.4 %attend_keep_keep.3 = (f32[192,512]{1,0:T(8,128)S(1)}, f32[8,96]{1,0:T(8,128)S(1)}, f32[192,512]{1,0:T(8,128)S(1)}, f32[8,96]{1,0:T(8,128)S(1)}) custom-call(s32[8]{0:T(128)S(1)} %plan.1.info_ref.refs_0_, bf16[576,2048]{1,0:T(8,128)(2,1)} %bitcast.20, bf16[256,576]{1,0:T(8,128)(2,1)} %collective-permute-done.2.refs_2_.refs_3_, ...), custom_call_target="tpu_custom_call" | custom-call | flops 1711276032 | bytes 4194304 | tf_op jit(solution)/shard_map/attend_keep_keep/pallas_call | solution.py:250
  23.3 3.0 %collective-permute-done.5.refs_2_.refs_5_ = bf16[256,576]{1,0:T(8,128)(2,1)S(1)} collective-permute-done((bf16[256,576]{1,0:T(8,128)(2,1)}, bf16[256,576]{1,0:T(8,128)(2,1)S(1)}, u32[]{:S(2)}, u32[]{:S(2)}) %collective-permute-start.5) | collective-permute-done | bytes 294944 | tf_op jit(solution)/shard_map/ppermute | solution.py:525
  26.4 1.3 %collective-permute-done.6.refs_3_.refs_6_ = bf16[256,576]{1,0:T(8,128)(2,1)S(1)} collective-permute-done((bf16[256,576]{1,0:T(8,128)(2,1)}, bf16[256,576]{1,0:T(8,128)(2,1)S(1)}, u32[]{:S(2)}, u32[]{:S(2)}) %collective-permute-start.6) | collective-permute-done | bytes 294944 | tf_op jit(solution)/shard_map/ppermute | solution.py:525
  27.7 1.6 %collective-permute-start.7 = (bf16[256,576]{1,0:T(8,128)(2,1)S(1)}, bf16[256,576]{1,0:T(8,128)(2,1)S(1)}, u32[]{:S(2)}, u32[]{:S(2)}) collective-permute-start(bf16[256,576]{1,0:T(8,128)(2,1)S(1)} %collective-permute-done.5.refs_2_.refs_5_), channel_id=1, source_target_pairs={{0,2},{2,4},{4,6},{6,7},{7,5},{5,3},{3,1},{1,0},{8,10},{10,12},{12... | collective-permute-start | bytes 884744 | tf_op jit(solution)/shard_map/ppermute | solution.py:525
  29.7 3.2 %attend_keep_keep.4 = (f32[192,512]{1,0:T(8,128)S(1)}, f32[8,96]{1,0:T(8,128)S(1)}, f32[192,512]{1,0:T(8,128)S(1)}, f32[8,96]{1,0:T(8,128)S(1)}) custom-call(s32[8]{0:T(128)S(1)} %plan.1.info_ref.refs_0_, bf16[576,2048]{1,0:T(8,128)(2,1)S(1)} %bitcast.22, bf16[256,576]{1,0:T(8,128)(2,1)S(1)} %collective-permute-done.5.refs_2_.refs_5_, ...), custom_call_target="tpu_custom_call" | custom-call | flops 1711276032 | bytes 4194304 | tf_op jit(solution)/shard_map/attend_keep_keep/pallas_call | solution.py:250
  32.9 0.8 copy-done.3
  33.7 0.8 copy-done.5
  34.5 1.4 %collective-permute-done.7.refs_2_.refs_7_ = bf16[256,576]{1,0:T(8,128)(2,1)S(1)} collective-permute-done((bf16[256,576]{1,0:T(8,128)(2,1)S(1)}, bf16[256,576]{1,0:T(8,128)(2,1)S(1)}, u32[]{:S(2)}, u32[]{:S(2)}) %collective-permute-start.7) | collective-permute-done | bytes 294944 | tf_op jit(solution)/shard_map/ppermute | solution.py:525
  35.8 1.3 %collective-permute-done.8.refs_3_.refs_8_ = bf16[256,576]{1,0:T(8,128)(2,1)S(1)} collective-permute-done((bf16[256,576]{1,0:T(8,128)(2,1)S(1)}, bf16[256,576]{1,0:T(8,128)(2,1)S(1)}, u32[]{:S(2)}, u32[]{:S(2)}) %collective-permute-start.8) | collective-permute-done | bytes 294944 | tf_op jit(solution)/shard_map/ppermute | solution.py:525
  37.2 0.5 collective-permute-start.10
  37.7 1.6 %collective-permute-start.9 = (bf16[128,576]{1,0:T(8,128)(2,1)S(1)}, bf16[128,576]{1,0:T(8,128)(2,1)S(1)}, u32[]{:S(2)}, u32[]{:S(2)}) collective-permute-start(bf16[128,576]{1,0:T(8,128)(2,1)S(1)} %slice.21), channel_id=1, source_target_pairs={{0,2},{2,4},{4,6},{6,7},{7,5},{5,3},{3,1},{1,0},{8,10},{10,12},{12... | collective-permute-start | bytes 442376 | tf_op jit(solution)/shard_map/ppermute | solution.py:528
  39.3 3.2 %attend_keep_keep.5 = (f32[192,512]{1,0:T(8,128)S(1)}, f32[8,96]{1,0:T(8,128)S(1)}, f32[192,512]{1,0:T(8,128)S(1)}, f32[8,96]{1,0:T(8,128)S(1)}) custom-call(s32[8]{0:T(128)S(1)} %plan.1.info_ref.refs_0_, bf16[576,2048]{1,0:T(8,128)(2,1)S(1)} %bitcast.23, bf16[256,576]{1,0:T(8,128)(2,1)S(1)} %collective-permute-done.7.refs_2_.refs_7_, ...), custom_call_target="tpu_custom_call" | custom-call | flops 1711276032 | bytes 4194304 | tf_op jit(solution)/shard_map/attend_keep_keep/pallas_call | solution.py:250
  42.6 0.5 collective-permute-done.9.refs_2_
  43.3 2.9 %attend_ends.2 = (bf16[112,512]{1,0:T(8,128)(2,1)}, bf16[112,512]{1,0:T(8,128)(2,1)}) custom-call(s32[8]{0:T(128)S(1)} %plan.1.info_ref.refs_0_, bf16[576,2048]{1,0:T(8,128)(2,1)S(1)} %bitcast.24, bf16[128,576]{1,0:T(8,128)(2,1)S(1)} %collective-permute-done.9.refs_2_, bf16[128,576]{1,0:T(8,128)(2,1)S(1)} %collective-permute-done.10.refs_3_.refs_5_), custom_call_target="tpu_custom_call" | custom-call | flops 855638016 | bytes 4194304 | tf_op jit(solution)/shard_map/attend_ends/pallas_call | solution.py:250
  46.2 1.7 %collective-permute-start.11 = (bf16[112,512]{1,0:T(8,128)(2,1)}, bf16[112,512]{1,0:T(8,128)(2,1)}, u32[]{:S(2)}, u32[]{:S(2)}) collective-permute-start(bf16[112,512]{1,0:T(8,128)(2,1)} %get-tuple-element.130), channel_id=1, source_target_pairs={{2,0},{4,2},{6,4},{7,6},{5,7},{3,5},{1,3},{0,1},{10,8},{12,10},{14... | collective-permute-start | bytes 344072 | tf_op jit(solution)/shard_map/ppermute | solution.py:561
  48.3 0.7 slice.23
  49.9 1.5 %copy-done.1 = bf16[576,2048]{1,0:T(8,128)(2,1)S(1)} copy-done((bf16[576,2048]{1,0:T(8,128)(2,1)S(1)}, bf16[576,2048]{1,0:T(8,128)(2,1)}, u32[]{:S(2)}) %copy-start.1) | copy-done | bytes 2359320
  51.4 0.9 copy-done.12
  52.4 3.8 %attend_ends.3 = (bf16[48,512]{1,0:T(8,128)(2,1)S(1)}, bf16[48,512]{1,0:T(8,128)(2,1)S(1)}, bf16[576,2048]{1,0:T(8,128)(2,1)S(1)}) custom-call(s32[8]{0:T(128)} %copy-done.32, bf16[576,2048]{1,0:T(8,128)(2,1)} %bitcast.21, bf16[576,2048]{1,0:T(8,128)(2,1)S(1)} %copy-done.1, bf16[288,2048]{1,0:T(8,128)(2,1)} %get-tuple-element.134.refs_3_, ...), custom_call_target="tpu_custom_call" | custom-call | flops 285212672 | bytes 4194304 | tf_op jit(solution)/shard_map/attend_ends/pallas_call | solution.py:250
  56.2 1.1 %merge.6 = (bf16[208,512]{1,0:T(8,128)(2,1)S(1)}, bf16[208,512]{1,0:T(8,128)(2,1)S(1)}) custom-call(bf16[112,512]{1,0:T(8,128)(2,1)} %collective-permute-done.11.refs_0_, f32[192,512]{1,0:T(8,128)S(1)} %copy-done.8, f32[8,96]{1,0:T(8,128)S(1)} %copy-done.18, bf16[112,512]{1,0:T(8,128)(2,1)} %collective-permute-done.12.refs_3_, f32[192,512]{1,0:T(8,128)S(1)} %copy-done.10, ...), custom_call_target="tpu_custom_call" | custom-call | flops 1048576 | bytes 2097152 | tf_op jit(solution)/shard_map/merge/pallas_call | solution.py:297
  57.4 1.7 %collective-permute-start.15 = (bf16[208,512]{1,0:T(8,128)(2,1)S(1)}, bf16[208,512]{1,0:T(8,128)(2,1)S(1)}, u32[]{:S(2)}, u32[]{:S(2)}) collective-permute-start(bf16[208,512]{1,0:T(8,128)(2,1)S(1)} %get-tuple-element.144), channel_id=1, source_target_pairs={{2,0},{4,2},{6,4},{7,6},{5,7},{3,5},{1,3},{0,1},{10,8},{12,10},{14... | collective-permute-start | bytes 638984 | tf_op jit(solution)/shard_map/ppermute | solution.py:561
  59.4 1.7 %collective-permute-start.17 = (bf16[48,512]{1,0:T(8,128)(2,1)S(1)}, bf16[48,512]{1,0:T(8,128)(2,1)S(1)}, u32[]{:S(2)}, u32[]{:S(2)}) collective-permute-start(bf16[48,512]{1,0:T(8,128)(2,1)S(1)} %get-tuple-element.161), channel_id=1, source_target_pairs={{2,0},{4,2},{6,4},{7,6},{5,7},{3,5},{1,3},{0,1},{10,8},{12,10},{14... | collective-permute-start | bytes 147464 | tf_op jit(solution)/shard_map/ppermute | solution.py:561
  61.5 4.3 %attend_own_keep_keep_keep_keep_keep_keep.1 = (f32[64,512]{1,0:T(8,128)S(1)}, f32[8,32]{1,0:T(8,128)S(1)}, f32[64,512]{1,0:T(8,128)S(1)}, f32[8,32]{1,0:T(8,128)...) custom-call(s32[8]{0:T(128)S(1)} %copy-done.33, ...), custom_call_target="tpu_custom_call" | custom-call | flops 1996488704 | bytes 4194304 | tf_op jit(solution)/shard_map/attend_own_keep_keep_keep_keep_keep_keep/pallas_call | solution.py:250
  65.9 1.1 collective-permute-done.18.refs_3_
  67.2 1.6 %collective-permute-start.19 = (bf16[208,512]{1,0:T(8,128)(2,1)S(1)}, bf16[208,512]{1,0:T(8,128)(2,1)S(1)}, u32[]{:S(2)}, u32[]{:S(2)}) collective-permute-start(bf16[208,512]{1,0:T(8,128)(2,1)S(1)} %get-tuple-element.169), channel_id=1, source_target_pairs={{2,0},{4,2},{6,4},{7,6},{5,7},{3,5},{1,3},{0,1},{10,8},{12,10},{14... | collective-permute-start | bytes 638984 | tf_op jit(solution)/shard_map/ppermute | solution.py:561
  69.4 1.6 %collective-permute-start.23 = (bf16[80,512]{1,0:T(8,128)(2,1)S(1)}, bf16[80,512]{1,0:T(8,128)(2,1)S(1)}, u32[]{:S(2)}, u32[]{:S(2)}) collective-permute-start(bf16[80,512]{1,0:T(8,128)(2,1)S(1)} %get-tuple-element.185), channel_id=1, source_target_pairs={{2,0},{4,2},{6,4},{7,6},{5,7},{3,5},{1,3},{0,1},{10,8},{12,10},{14... | collective-permute-start | bytes 245768 | tf_op jit(solution)/shard_map/ppermute | solution.py:561
  71.5 2.6 %collective-permute-done.19.refs_0_ = bf16[208,512]{1,0:T(8,128)(2,1)S(1)} collective-permute-done((bf16[208,512]{1,0:T(8,128)(2,1)S(1)}, bf16[208,512]{1,0:T(8,128)(2,1)S(1)}, u32[]{:S(2)}, u32[]{:S(2)}) %collective-permute-start.19) | collective-permute-done | bytes 213024 | tf_op jit(solution)/shard_map/ppermute | solution.py:561
  74.1 1.3 %collective-permute-done.20.refs_3_ = bf16[208,512]{1,0:T(8,128)(2,1)S(1)} collective-permute-done((bf16[208,512]{1,0:T(8,128)(2,1)S(1)}, bf16[208,512]{1,0:T(8,128)(2,1)S(1)}, u32[]{:S(2)}, u32[]{:S(2)}) %collective-permute-start.20) | collective-permute-done | bytes 213024 | tf_op jit(solution)/shard_map/ppermute | solution.py:562
  75.6 1.6 %collective-permute-start.21 = (bf16[208,512]{1,0:T(8,128)(2,1)S(1)}, bf16[208,512]{1,0:T(8,128)(2,1)S(1)}, u32[]{:S(2)}, u32[]{:S(2)}) collective-permute-start(bf16[208,512]{1,0:T(8,128)(2,1)S(1)} %get-tuple-element.175), channel_id=1, source_target_pairs={{2,0},{4,2},{6,4},{7,6},{5,7},{3,5},{1,3},{0,1},{10,8},{12,10},{14... | collective-permute-start | bytes 638984 | tf_op jit(solution)/shard_map/ppermute | solution.py:561
  77.8 1.6 %collective-permute-start.25 = (bf16[80,512]{1,0:T(8,128)(2,1)S(1)}, bf16[80,512]{1,0:T(8,128)(2,1)S(1)}, u32[]{:S(2)}, u32[]{:S(2)}) collective-permute-start(bf16[80,512]{1,0:T(8,128)(2,1)S(1)} %get-tuple-element.191), channel_id=1, source_target_pairs={{2,0},{4,2},{6,4},{7,6},{5,7},{3,5},{1,3},{0,1},{10,8},{12,10},{14... | collective-permute-start | bytes 245768 | tf_op jit(solution)/shard_map/ppermute | solution.py:561
  79.9 2.5 %collective-permute-done.25.refs_0_ = bf16[80,512]{1,0:T(8,128)(2,1)S(1)} collective-permute-done((bf16[80,512]{1,0:T(8,128)(2,1)S(1)}, bf16[80,512]{1,0:T(8,128)(2,1)S(1)}, u32[]{:S(2)}, u32[]{:S(2)}) %collective-permute-start.25) | collective-permute-done | bytes 81952 | tf_op jit(solution)/shard_map/ppermute | solution.py:561
  82.4 1.6 %collective-permute-done.26.refs_3_ = bf16[80,512]{1,0:T(8,128)(2,1)S(1)} collective-permute-done((bf16[80,512]{1,0:T(8,128)(2,1)S(1)}, bf16[80,512]{1,0:T(8,128)(2,1)S(1)}, u32[]{:S(2)}, u32[]{:S(2)}) %collective-permute-start.26) | collective-permute-done | bytes 81952 | tf_op jit(solution)/shard_map/ppermute | solution.py:562
  84.1 1.9 %collective-permute-start.27 = (bf16[80,512]{1,0:T(8,128)(2,1)S(1)}, bf16[80,512]{1,0:T(8,128)(2,1)S(1)}, u32[]{:S(2)}, u32[]{:S(2)}) collective-permute-start(bf16[80,512]{1,0:T(8,128)(2,1)S(1)} %get-tuple-element.197), channel_id=1, source_target_pairs={{2,0},{4,2},{6,4},{7,6},{5,7},{3,5},{1,3},{0,1},{10,8},{12,10},{14... | collective-permute-start | bytes 245768 | tf_op jit(solution)/shard_map/ppermute | solution.py:561
  86.2 2.4 %collective-permute-done.27.refs_4_ = bf16[80,512]{1,0:T(8,128)(2,1)S(1)} collective-permute-done((bf16[80,512]{1,0:T(8,128)(2,1)S(1)}, bf16[80,512]{1,0:T(8,128)(2,1)S(1)}, u32[]{:S(2)}, u32[]{:S(2)}) %collective-permute-start.27) | collective-permute-done | bytes 81952 | tf_op jit(solution)/shard_map/ppermute | solution.py:561
  88.6 1.8 %collective-permute-done.28.refs_5_ = bf16[80,512]{1,0:T(8,128)(2,1)S(1)} collective-permute-done((bf16[80,512]{1,0:T(8,128)(2,1)S(1)}, bf16[80,512]{1,0:T(8,128)(2,1)S(1)}, u32[]{:S(2)}, u32[]{:S(2)}) %collective-permute-start.28) | collective-permute-done | bytes 81952 | tf_op jit(solution)/shard_map/ppermute | solution.py:562
  90.5 10.8 %finish.1 = bf16[8,16,896]{2,1,0:T(8,128)(2,1)S(1)} custom-call(bf16[208,512]{1,0:T(8,128)(2,1)S(1)} %collective-permute-done.21.refs_0_, bf16[208,512]{1,0:T(8,128)(2,1)S(1)} %collective-permute-done.22.refs_1_, f32[192,512]{1,0:T(8,128)S(1)} %get-tuple-element.177.refs_2_, f32[8,96]{1,0:T(8,128)S(1)} %copy-done.22, ...), custom_call_target="tpu_custom_call" | custom-call | flops 469762048 | bytes 29360128 | tf_op jit(solution)/shard_map/finish/pallas_call | solution.py:366
  101.3 10.4 %all_to_all.5 = bf16[8,16,896]{2,1,0:T(8,128)(2,1)S(1)} all-to-all(bf16[8,16,896]{2,1,0:T(8,128)(2,1)S(1)} %finish.1), channel_id=1, replica_groups=mesh['grp'=4,'ctx'=8] {'ctx'}, dimensions={0} | all-to-all | bytes 458752 | tf_op jit(solution)/shard_map/all_to_all | solution.py:596
  111.7 0.6 reshape.26
  (97 shorter events, 6.0 us)
Async XLA Ops:
  0.0 10.6 %collective-permute-start.4 = (bf16[576,2048]{1,0:T(8,128)(2,1)}, bf16[576,2048]{1,0:T(8,128)(2,1)S(1)}, u32[]{:S(2)}, u32[]{:S(2)}) collective-permute-start(bf16[576,2048]{1,0:T(8,128)(2,1)} %bitcast.17), channel_id=1, source_target_pairs={{0,8},{8,0},{16,24},{24,16},{1,9},{9,1},{17,25},{25,17},{2,10},{10... | collective-permute-start | bytes 7077896 | tf_op jit(solution)/shard_map/ppermute | solution.py:499
  0.5 14.4 %collective-permute-start.2 = (bf16[256,576]{1,0:T(8,128)(2,1)}, bf16[256,576]{1,0:T(8,128)(2,1)}, u32[]{:S(2)}, u32[]{:S(2)}) collective-permute-start(bf16[256,576]{1,0:T(8,128)(2,1)} %bitcast.11), channel_id=1, source_target_pairs={{0,2},{2,4},{4,6},{6,7},{7,5},{5,3},{3,1},{1,0},{8,10},{10,12},{12... | collective-permute-start | bytes 884744 | tf_op jit(solution)/shard_map/ppermute | solution.py:525
  3.0 11.8 %collective-permute-start.3 = (bf16[256,576]{1,0:T(8,128)(2,1)}, bf16[256,576]{1,0:T(8,128)(2,1)}, u32[]{:S(2)}, u32[]{:S(2)}) collective-permute-start(bf16[256,576]{1,0:T(8,128)(2,1)} %bitcast.12), channel_id=1, source_target_pairs={{2,0},{4,2},{6,4},{7,6},{5,7},{3,5},{1,3},{0,1},{10,8},{12,10},{14... | collective-permute-start | bytes 884744 | tf_op jit(solution)/shard_map/ppermute | solution.py:525
  4.3 44.0 %copy-start.32 = (s32[8]{0:T(128)}, s32[8]{0:T(128)S(1)}, u32[]{:S(2)}) copy-start(s32[8]{0:T(128)S(1)} %plan.1.info_ref.refs_0_) | copy-start | bytes 100
  14.8 14.9 %copy-start.31 = (bf16[1,2048,576]{1,2,0:T(8,128)(2,1)S(1)}, bf16[1,2048,576]{1,2,0:T(8,128)(2,1)}, u32[]{:S(2)}) copy-start(bf16[1,2048,576]{1,2,0:T(8,128)(2,1)} %param.9) | copy-start | bytes 7077892
  14.8 28.5 %collective-permute-start.13 = (bf16[288,2048]{1,0:T(8,128)(2,1)}, bf16[288,2048]{1,0:T(8,128)(2,1)}, u32[]{:S(2)}, u32[]{:S(2)}) collective-permute-start(bf16[288,2048]{1,0:T(8,128)(2,1)} %offer.1), channel_id=1, source_target_pairs={{0,16},{8,24},{16,0},{24,8},{1,17},{9,25},{17,1},{25,9},{2,18},{10... | collective-permute-start | bytes 3538952 | tf_op jit(solution)/shard_map/ppermute | solution.py:534
  16.9 9.5 %collective-permute-start.5 = (bf16[256,576]{1,0:T(8,128)(2,1)}, bf16[256,576]{1,0:T(8,128)(2,1)S(1)}, u32[]{:S(2)}, u32[]{:S(2)}) collective-permute-start(bf16[256,576]{1,0:T(8,128)(2,1)} %collective-permute-done.2.refs_2_.refs_3_), channel_id=1, source_target_pairs={{0,2},{2,4},{4,6},{6,7},{7,5},{5,3},{3,1},{1,0},{8,10},{10,12},{12... | collective-permute-start | bytes 884744 | tf_op jit(solution)/shard_map/ppermute | solution.py:525
  18.5 9.2 %collective-permute-start.6 = (bf16[256,576]{1,0:T(8,128)(2,1)}, bf16[256,576]{1,0:T(8,128)(2,1)S(1)}, u32[]{:S(2)}, u32[]{:S(2)}) collective-permute-start(bf16[256,576]{1,0:T(8,128)(2,1)} %collective-permute-done.3.refs_3_.refs_4_), channel_id=1, source_target_pairs={{2,0},{4,2},{6,4},{7,6},{5,7},{3,5},{1,3},{0,1},{10,8},{12,10},{14... | collective-permute-start | bytes 884744 | tf_op jit(solution)/shard_map/ppermute | solution.py:525
  26.4 6.5 %copy-start.25 = (bf16[256,576]{1,0:T(8,128)(2,1)}, bf16[256,576]{1,0:T(8,128)(2,1)S(1)}, u32[]{:S(2)}) copy-start(bf16[256,576]{1,0:T(8,128)(2,1)S(1)} %collective-permute-done.5.refs_2_.refs_5_) | copy-start | bytes 884740
  27.7 8.2 %collective-permute-start.7 = (bf16[256,576]{1,0:T(8,128)(2,1)S(1)}, bf16[256,576]{1,0:T(8,128)(2,1)S(1)}, u32[]{:S(2)}, u32[]{:S(2)}) collective-permute-start(bf16[256,576]{1,0:T(8,128)(2,1)S(1)} %collective-permute-done.5.refs_2_.refs_5_), channel_id=1, source_target_pairs={{0,2},{2,4},{4,6},{6,7},{7,5},{5,3},{3,1},{1,0},{8,10},{10,12},{12... | collective-permute-start | bytes 884744 | tf_op jit(solution)/shard_map/ppermute | solution.py:525
  29.2 7.9 %collective-permute-start.8 = (bf16[256,576]{1,0:T(8,128)(2,1)S(1)}, bf16[256,576]{1,0:T(8,128)(2,1)S(1)}, u32[]{:S(2)}, u32[]{:S(2)}) collective-permute-start(bf16[256,576]{1,0:T(8,128)(2,1)S(1)} %collective-permute-done.6.refs_3_.refs_6_), channel_id=1, source_target_pairs={{2,0},{4,2},{6,4},{7,6},{5,7},{3,5},{1,3},{0,1},{10,8},{12,10},{14... | collective-permute-start | bytes 884744 | tf_op jit(solution)/shard_map/ppermute | solution.py:525
  35.8 6.7 %copy-start.13 = (bf16[256,576]{1,0:T(8,128)(2,1)}, bf16[256,576]{1,0:T(8,128)(2,1)S(1)}, u32[]{:S(2)}) copy-start(bf16[256,576]{1,0:T(8,128)(2,1)S(1)} %collective-permute-done.7.refs_2_.refs_7_) | copy-start | bytes 884740
  37.1 5.4 %copy-start.15 = (bf16[256,576]{1,0:T(8,128)(2,1)}, bf16[256,576]{1,0:T(8,128)(2,1)S(1)}, u32[]{:S(2)}) copy-start(bf16[256,576]{1,0:T(8,128)(2,1)S(1)} %collective-permute-done.8.refs_3_.refs_8_) | copy-start | bytes 884740
  37.2 5.4 %collective-permute-start.10 = (bf16[128,576]{1,0:T(8,128)(2,1)S(1)}, bf16[128,576]{1,0:T(8,128)(2,1)S(1)}, u32[]{:S(2)}, u32[]{:S(2)}) collective-permute-start(bf16[128,576]{1,0:T(8,128)(2,1)S(1)} %slice.22), channel_id=1, source_target_pairs={{2,0},{4,2},{6,4},{7,6},{5,7},{3,5},{1,3},{0,1},{10,8},{12,10},{14... | collective-permute-start | bytes 442376 | tf_op jit(solution)/shard_map/ppermute | solution.py:529
  37.7 5.4 %collective-permute-start.9 = (bf16[128,576]{1,0:T(8,128)(2,1)S(1)}, bf16[128,576]{1,0:T(8,128)(2,1)S(1)}, u32[]{:S(2)}, u32[]{:S(2)}) collective-permute-start(bf16[128,576]{1,0:T(8,128)(2,1)S(1)} %slice.21), channel_id=1, source_target_pairs={{0,2},{2,4},{4,6},{6,7},{7,5},{5,3},{3,1},{1,0},{8,10},{10,12},{12... | collective-permute-start | bytes 442376 | tf_op jit(solution)/shard_map/ppermute | solution.py:528
  42.5 7.1 %copy-start.7 = (f32[192,512]{1,0:T(8,128)}, f32[192,512]{1,0:T(8,128)S(1)}, u32[]{:S(2)}) copy-start(f32[192,512]{1,0:T(8,128)S(1)} %get-tuple-element.139.refs_1_) | copy-start | bytes 1179652
  42.5 7.1 %copy-start.9 = (f32[192,512]{1,0:T(8,128)}, f32[192,512]{1,0:T(8,128)S(1)}, u32[]{:S(2)}) copy-start(f32[192,512]{1,0:T(8,128)S(1)} %get-tuple-element.142.refs_4_) | copy-start | bytes 1179652
  42.6 7.1 %copy-start.17 = (f32[8,96]{1,0:T(8,128)}, f32[8,96]{1,0:T(8,128)S(1)}, u32[]{:S(2)}) copy-start(f32[8,96]{1,0:T(8,128)S(1)} %get-tuple-element.140.refs_2_) | copy-start | bytes 9220
  42.6 7.1 %copy-start.19 = (f32[8,96]{1,0:T(8,128)}, f32[8,96]{1,0:T(8,128)S(1)}, u32[]{:S(2)}) copy-start(f32[8,96]{1,0:T(8,128)S(1)} %get-tuple-element.143.refs_5_) | copy-start | bytes 9220
  42.6 7.1 %copy-start.11 = (bf16[128,576]{1,0:T(8,128)(2,1)}, bf16[128,576]{1,0:T(8,128)(2,1)S(1)}, u32[]{:S(2)}) copy-start(bf16[128,576]{1,0:T(8,128)(2,1)S(1)} %collective-permute-done.10.refs_3_.refs_5_) | copy-start | bytes 442372
  43.3 6.3 %collective-permute-start.14 = (bf16[288,2048]{1,0:T(8,128)(2,1)}, bf16[288,2048]{1,0:T(8,128)(2,1)}, u32[]{:S(2)}, u32[]{:S(2)}) collective-permute-start(bf16[288,2048]{1,0:T(8,128)(2,1)} %collective-permute-done.13), channel_id=1, source_target_pairs={{0,8},{8,0},{16,24},{24,16},{1,9},{9,1},{17,25},{25,17},{2,10},{10... | collective-permute-start | bytes 3538952 | tf_op jit(solution)/shard_map/ppermute | solution.py:542
  46.2 9.9 %collective-permute-start.11 = (bf16[112,512]{1,0:T(8,128)(2,1)}, bf16[112,512]{1,0:T(8,128)(2,1)}, u32[]{:S(2)}, u32[]{:S(2)}) collective-permute-start(bf16[112,512]{1,0:T(8,128)(2,1)} %get-tuple-element.130), channel_id=1, source_target_pairs={{2,0},{4,2},{6,4},{7,6},{5,7},{3,5},{1,3},{0,1},{10,8},{12,10},{14... | collective-permute-start | bytes 344072 | tf_op jit(solution)/shard_map/ppermute | solution.py:561
  47.9 8.3 %collective-permute-start.12 = (bf16[112,512]{1,0:T(8,128)(2,1)}, bf16[112,512]{1,0:T(8,128)(2,1)}, u32[]{:S(2)}, u32[]{:S(2)}) collective-permute-start(bf16[112,512]{1,0:T(8,128)(2,1)} %get-tuple-element.131), channel_id=1, source_target_pairs={{0,2},{2,4},{4,6},{6,7},{7,5},{5,3},{3,1},{1,0},{8,10},{10,12},{12... | collective-permute-start | bytes 344072 | tf_op jit(solution)/shard_map/ppermute | solution.py:562
  52.3 9.2 %copy-start.14 = (bf16[256,576]{1,0:T(8,128)(2,1)S(1)}, bf16[256,576]{1,0:T(8,128)(2,1)}, u32[]{:S(2)}) copy-start(bf16[256,576]{1,0:T(8,128)(2,1)} %copy-done.13) | copy-start | bytes 884740
  52.3 9.2 %copy-start.16 = (bf16[256,576]{1,0:T(8,128)(2,1)S(1)}, bf16[256,576]{1,0:T(8,128)(2,1)}, u32[]{:S(2)}) copy-start(bf16[256,576]{1,0:T(8,128)(2,1)} %copy-done.15) | copy-start | bytes 884740
  52.3 9.2 %copy-start.24 = (bf16[4,1,4,16,576]{4,3,2,1,0:T(8,128)(2,1)S(1)}, bf16[4,1,4,16,576]{4,3,2,1,0:T(8,128)(2,1)}, u32[]{:S(2)}) copy-start(bf16[4,1,4,16,576]{4,3,2,1,0:T(8,128)(2,1)} %param.10) | copy-start | bytes 884740
  52.3 9.2 %copy-start.26 = (bf16[256,576]{1,0:T(8,128)(2,1)S(1)}, bf16[256,576]{1,0:T(8,128)(2,1)}, u32[]{:S(2)}) copy-start(bf16[256,576]{1,0:T(8,128)(2,1)} %copy-done.25) | copy-start | bytes 884740
  52.3 9.1 %copy-start.28 = (bf16[256,576]{1,0:T(8,128)(2,1)S(1)}, bf16[256,576]{1,0:T(8,128)(2,1)}, u32[]{:S(2)}) copy-start(bf16[256,576]{1,0:T(8,128)(2,1)} %copy-done.27) | copy-start | bytes 884740
  52.3 9.1 %copy-start.30 = (bf16[4,1,4,576]{3,2,1,0:T(4,128)(2,1)S(1)}, bf16[4,1,4,576]{3,2,1,0:T(4,128)(2,1)}, u32[]{:S(2)}) copy-start(bf16[4,1,4,576]{3,2,1,0:T(4,128)(2,1)} %param.11) | copy-start | bytes 55300
  52.3 9.1 %copy-start.33 = (s32[8]{0:T(128)S(1)}, s32[8]{0:T(128)}, u32[]{:S(2)}) copy-start(s32[8]{0:T(128)} %copy-done.32) | copy-start | bytes 100
  57.4 9.6 %collective-permute-start.15 = (bf16[208,512]{1,0:T(8,128)(2,1)S(1)}, bf16[208,512]{1,0:T(8,128)(2,1)S(1)}, u32[]{:S(2)}, u32[]{:S(2)}) collective-permute-start(bf16[208,512]{1,0:T(8,128)(2,1)S(1)} %get-tuple-element.144), channel_id=1, source_target_pairs={{2,0},{4,2},{6,4},{7,6},{5,7},{3,5},{1,3},{0,1},{10,8},{12,10},{14... | collective-permute-start | bytes 638984 | tf_op jit(solution)/shard_map/ppermute | solution.py:561
  59.1 7.9 %collective-permute-start.16 = (bf16[208,512]{1,0:T(8,128)(2,1)S(1)}, bf16[208,512]{1,0:T(8,128)(2,1)S(1)}, u32[]{:S(2)}, u32[]{:S(2)}) collective-permute-start(bf16[208,512]{1,0:T(8,128)(2,1)S(1)} %get-tuple-element.145), channel_id=1, source_target_pairs={{0,2},{2,4},{4,6},{6,7},{7,5},{5,3},{3,1},{1,0},{8,10},{10,12},{12... | collective-permute-start | bytes 638984 | tf_op jit(solution)/shard_map/ppermute | solution.py:562
  59.4 6.5 %collective-permute-start.17 = (bf16[48,512]{1,0:T(8,128)(2,1)S(1)}, bf16[48,512]{1,0:T(8,128)(2,1)S(1)}, u32[]{:S(2)}, u32[]{:S(2)}) collective-permute-start(bf16[48,512]{1,0:T(8,128)(2,1)S(1)} %get-tuple-element.161), channel_id=1, source_target_pairs={{2,0},{4,2},{6,4},{7,6},{5,7},{3,5},{1,3},{0,1},{10,8},{12,10},{14... | collective-permute-start | bytes 147464 | tf_op jit(solution)/shard_map/ppermute | solution.py:561
  61.1 5.9 %collective-permute-start.18 = (bf16[48,512]{1,0:T(8,128)(2,1)S(1)}, bf16[48,512]{1,0:T(8,128)(2,1)S(1)}, u32[]{:S(2)}, u32[]{:S(2)}) collective-permute-start(bf16[48,512]{1,0:T(8,128)(2,1)S(1)} %get-tuple-element.162), channel_id=1, source_target_pairs={{0,2},{2,4},{4,6},{6,7},{7,5},{5,3},{3,1},{1,0},{8,10},{10,12},{12... | collective-permute-start | bytes 147464 | tf_op jit(solution)/shard_map/ppermute | solution.py:562
  61.5 5.5 %copy-start.4 = (f32[192,512]{1,0:T(8,128)S(1)}, f32[192,512]{1,0:T(8,128)}, u32[]{:S(2)}) copy-start(f32[192,512]{1,0:T(8,128)} %copy-done.3) | copy-start | bytes 1179652
  61.5 5.4 %copy-start.6 = (f32[192,512]{1,0:T(8,128)S(1)}, f32[192,512]{1,0:T(8,128)}, u32[]{:S(2)}) copy-start(f32[192,512]{1,0:T(8,128)} %copy-done.5) | copy-start | bytes 1179652
  65.9 24.6 %copy-start.2 = (bf16[16,512,128]{2,1,0:T(8,128)(2,1)S(1)}, bf16[16,512,128]{2,1,0:T(8,128)(2,1)}, u32[]{:S(2)}) copy-start(bf16[16,512,128]{2,1,0:T(8,128)(2,1)} %refs_8_.1) | copy-start | bytes 6291460
  65.9 24.6 %copy-start.22 = (f32[8,96]{1,0:T(8,128)S(1)}, f32[8,96]{1,0:T(8,128)}, u32[]{:S(2)}) copy-start(f32[8,96]{1,0:T(8,128)} %copy-done.21) | copy-start | bytes 9220
  67.2 6.9 %collective-permute-start.19 = (bf16[208,512]{1,0:T(8,128)(2,1)S(1)}, bf16[208,512]{1,0:T(8,128)(2,1)S(1)}, u32[]{:S(2)}, u32[]{:S(2)}) collective-permute-start(bf16[208,512]{1,0:T(8,128)(2,1)S(1)} %get-tuple-element.169), channel_id=1, source_target_pairs={{2,0},{4,2},{6,4},{7,6},{5,7},{3,5},{1,3},{0,1},{10,8},{12,10},{14... | collective-permute-start | bytes 638984 | tf_op jit(solution)/shard_map/ppermute | solution.py:561
  68.8 6.5 %collective-permute-start.20 = (bf16[208,512]{1,0:T(8,128)(2,1)S(1)}, bf16[208,512]{1,0:T(8,128)(2,1)S(1)}, u32[]{:S(2)}, u32[]{:S(2)}) collective-permute-start(bf16[208,512]{1,0:T(8,128)(2,1)S(1)} %get-tuple-element.172), channel_id=1, source_target_pairs={{0,2},{2,4},{4,6},{6,7},{7,5},{5,3},{3,1},{1,0},{8,10},{10,12},{12... | collective-permute-start | bytes 638984 | tf_op jit(solution)/shard_map/ppermute | solution.py:562
  69.4 8.3 %collective-permute-start.23 = (bf16[80,512]{1,0:T(8,128)(2,1)S(1)}, bf16[80,512]{1,0:T(8,128)(2,1)S(1)}, u32[]{:S(2)}, u32[]{:S(2)}) collective-permute-start(bf16[80,512]{1,0:T(8,128)(2,1)S(1)} %get-tuple-element.185), channel_id=1, source_target_pairs={{2,0},{4,2},{6,4},{7,6},{5,7},{3,5},{1,3},{0,1},{10,8},{12,10},{14... | collective-permute-start | bytes 245768 | tf_op jit(solution)/shard_map/ppermute | solution.py:561
  71.0 6.7 %collective-permute-start.24 = (bf16[80,512]{1,0:T(8,128)(2,1)S(1)}, bf16[80,512]{1,0:T(8,128)(2,1)S(1)}, u32[]{:S(2)}, u32[]{:S(2)}) collective-permute-start(bf16[80,512]{1,0:T(8,128)(2,1)S(1)} %get-tuple-element.188), channel_id=1, source_target_pairs={{0,2},{2,4},{4,6},{6,7},{7,5},{5,3},{3,1},{1,0},{8,10},{10,12},{12... | collective-permute-start | bytes 245768 | tf_op jit(solution)/shard_map/ppermute | solution.py:562
  75.6 14.8 %collective-permute-start.21 = (bf16[208,512]{1,0:T(8,128)(2,1)S(1)}, bf16[208,512]{1,0:T(8,128)(2,1)S(1)}, u32[]{:S(2)}, u32[]{:S(2)}) collective-permute-start(bf16[208,512]{1,0:T(8,128)(2,1)S(1)} %get-tuple-element.175), channel_id=1, source_target_pairs={{2,0},{4,2},{6,4},{7,6},{5,7},{3,5},{1,3},{0,1},{10,8},{12,10},{14... | collective-permute-start | bytes 638984 | tf_op jit(solution)/shard_map/ppermute | solution.py:561
  77.2 13.2 %collective-permute-start.22 = (bf16[208,512]{1,0:T(8,128)(2,1)S(1)}, bf16[208,512]{1,0:T(8,128)(2,1)S(1)}, u32[]{:S(2)}, u32[]{:S(2)}) collective-permute-start(bf16[208,512]{1,0:T(8,128)(2,1)S(1)} %get-tuple-element.176), channel_id=1, source_target_pairs={{0,2},{2,4},{4,6},{6,7},{7,5},{5,3},{3,1},{1,0},{8,10},{10,12},{12... | collective-permute-start | bytes 638984 | tf_op jit(solution)/shard_map/ppermute | solution.py:562
  77.8 4.6 %collective-permute-start.25 = (bf16[80,512]{1,0:T(8,128)(2,1)S(1)}, bf16[80,512]{1,0:T(8,128)(2,1)S(1)}, u32[]{:S(2)}, u32[]{:S(2)}) collective-permute-start(bf16[80,512]{1,0:T(8,128)(2,1)S(1)} %get-tuple-element.191), channel_id=1, source_target_pairs={{2,0},{4,2},{6,4},{7,6},{5,7},{3,5},{1,3},{0,1},{10,8},{12,10},{14... | collective-permute-start | bytes 245768 | tf_op jit(solution)/shard_map/ppermute | solution.py:561
  79.4 4.5 %collective-permute-start.26 = (bf16[80,512]{1,0:T(8,128)(2,1)S(1)}, bf16[80,512]{1,0:T(8,128)(2,1)S(1)}, u32[]{:S(2)}, u32[]{:S(2)}) collective-permute-start(bf16[80,512]{1,0:T(8,128)(2,1)S(1)} %get-tuple-element.194), channel_id=1, source_target_pairs={{0,2},{2,4},{4,6},{6,7},{7,5},{5,3},{3,1},{1,0},{8,10},{10,12},{12... | collective-permute-start | bytes 245768 | tf_op jit(solution)/shard_map/ppermute | solution.py:562
  84.1 4.5 %collective-permute-start.27 = (bf16[80,512]{1,0:T(8,128)(2,1)S(1)}, bf16[80,512]{1,0:T(8,128)(2,1)S(1)}, u32[]{:S(2)}, u32[]{:S(2)}) collective-permute-start(bf16[80,512]{1,0:T(8,128)(2,1)S(1)} %get-tuple-element.197), channel_id=1, source_target_pairs={{2,0},{4,2},{6,4},{7,6},{5,7},{3,5},{1,3},{0,1},{10,8},{12,10},{14... | collective-permute-start | bytes 245768 | tf_op jit(solution)/shard_map/ppermute | solution.py:561
  86.0 4.4 %collective-permute-start.28 = (bf16[80,512]{1,0:T(8,128)(2,1)S(1)}, bf16[80,512]{1,0:T(8,128)(2,1)S(1)}, u32[]{:S(2)}, u32[]{:S(2)}) collective-permute-start(bf16[80,512]{1,0:T(8,128)(2,1)S(1)} %get-tuple-element.198), channel_id=1, source_target_pairs={{0,2},{2,4},{4,6},{6,7},{7,5},{5,3},{3,1},{1,0},{8,10},{10,12},{12... | collective-permute-start | bytes 245768 | tf_op jit(solution)/shard_map/ppermute | solution.py:562
  (13 other events, 28.7 us)

commit v3 on v2

--- a/solution.py
+++ b/solution.py
@@ -135,9 +135,11 @@
     return peak, total, part
 
 
-def fetch_rows(info_ref, near, halves, cache_ref, sem):
-    me, source = info_ref[2], info_ref[3]
-    half = halves[0].shape[0]
+def fetch_rows(info_ref, sources, cache_ref, sem):
+    own_ref, beside_ref, half_ref, rest_ref, spare_ref = sources
+    me, source, crowded = info_ref[2], info_ref[3], info_ref[5] != 0
+    half = half_ref.shape[0]
+    near = (source >> 1) == (me >> 1)
 
     def whole_copy(ref):
         copy = pltpu.make_async_copy(ref, cache_ref, sem.at[0])
@@ -146,20 +148,24 @@
 
     @pl.when(source == me)
     def _():
-        whole_copy(near[0])
-
-    @pl.when((source != me) & ((source >> 1) == (me >> 1)))
+        whole_copy(own_ref)
+
+    @pl.when(near & (source != me))
     def _():
-        whole_copy(near[1])
-
-    @pl.when((source >> 1) != (me >> 1))
+        whole_copy(beside_ref)
+
+    @pl.when(jnp.logical_not(near) & crowded)
+    def _():
+        whole_copy(spare_ref)
+
+    @pl.when(jnp.logical_not(near | crowded))
     def _():
         core = me & 1
         copies = [
             pltpu.make_async_copy(
                 ref, cache_ref.at[pl.ds(pl.multiple_of(at * half, 16), half), :], sem.at[slot]
             )
-            for slot, (ref, at) in enumerate(zip(halves, (core, 1 - core)))
+            for slot, (ref, at) in enumerate(((half_ref, core), (rest_ref, 1 - core)))
         ]
         for copy in copies:
             copy.start()
@@ -167,8 +173,14 @@
             copy.wait()
 
 
-def attend_kernel(kinds, rows, takes, caches, limit_at, latent, fresh_info, *refs):
+def attend_kernel(kinds, rows, takes, caches, limit_at, latent, fresh_info, load, *refs):
     refs = list(refs)
+    if load:
+        load_sem, loaded_ref, weight_ref = refs.pop(), refs.pop(load[0]), refs.pop(load[1])
+        loading = pltpu.make_async_copy(
+            weight_ref.at[:, load[2] : load[3]], loaded_ref, load_sem
+        )
+        loading.start()
     info_ref = refs.pop(0)
     cache_refs, refs = refs[:caches], refs[caches:]
     queries, rest = refs[: len(takes)], refs[len(takes) :]
@@ -176,7 +188,7 @@
     fresh_rows = rest.pop() if fresh_info else None
     if caches > 1:
         sem, cache_ref = rest.pop(), rest.pop(-3)
-        fetch_rows(info_ref, cache_refs[:2], cache_refs[2:], cache_ref, sem)
+        fetch_rows(info_ref, cache_refs, cache_ref, sem)
     else:
         cache_ref = cache_refs[0]
     score_ref, query_ref = rest.pop(-2), rest.pop()
@@ -213,13 +225,21 @@
             stats = jnp.where(line == 2 * index, piece[1], stats)
             stats = jnp.where(line == 2 * index + 1, piece[2], stats)
         stats_ref[...] = stats
+    if load:
+        loading.wait()
 
 
 def whole(memory=pltpu.VMEM):
     return pl.BlockSpec(memory_space=memory)
 
 
-def attend(kinds, pieces, cache_parts, info, limit_at, latent, fresh=None, fresh_info=None):
+def in_hbm(array):
+    return pltpu.with_memory_space_constraint(array, pltpu.HBM)
+
+
+def attend(
+    kinds, pieces, cache_parts, info, limit_at, latent, fresh=None, fresh_info=None, load=None
+):
     out_shape = []
     queries = [piece[0] for piece in pieces]
     takes = tuple(piece[1:] for piece in pieces)
@@ -236,8 +256,10 @@
         else:
             out_shape.append(jax.ShapeDtypeStruct((rows, latent), jnp.float32))
             out_shape.append(jax.ShapeDtypeStruct((8, rows // sections), jnp.float32))
+    caches = len(cache_parts)
+    if caches > 1:
+        cache_parts = [in_hbm(part) for part in cache_parts]
     operands = [info, *cache_parts, *queries] + ([fresh] if fresh_info else [])
-    caches = len(cache_parts)
     scratch = [
         pltpu.VMEM((total, length), jnp.float32),
         pltpu.VMEM((total, key_width), jnp.bfloat16),
@@ -247,17 +269,30 @@
         scratch.append(pltpu.SemaphoreType.DMA((2,)))
     if fresh_info:
         scratch.append(pltpu.VMEM((fresh.shape[0] * fresh.shape[1], key_width), jnp.float32))
+    in_specs = (
+        [whole(pltpu.SMEM)]
+        + [whole(pltpu.HBM if caches > 1 else pltpu.VMEM)] * caches
+        + [whole()] * (len(operands) - 1 - caches)
+    )
+    out_specs = [whole()] * len(out_shape)
+    span = None
+    if load:
+        weight, start, stop = load
+        operands.append(in_hbm(weight))
+        in_specs.append(whole(pltpu.HBM))
+        out_shape.append(pltpu.VMEM((weight.shape[0], stop - start), weight.dtype))
+        out_specs.append(whole())
+        scratch.append(pltpu.SemaphoreType.DMA)
+        span = (len(operands) + len(out_shape) - 1, len(operands) - 1, start, stop)
     outs = pl.pallas_call(
         functools.partial(
-            attend_kernel, tuple(kinds), rows, takes, caches, limit_at, latent, fresh_info
+            attend_kernel, tuple(kinds), rows, takes, caches, limit_at, latent, fresh_info, span
         ),
         out_shape=out_shape,
-        in_specs=[whole(pltpu.SMEM)]
-        + [whole(pl.ANY if caches > 1 else pltpu.VMEM)] * caches
-        + [whole()] * (len(operands) - 1 - caches),
-        out_specs=[whole()] * len(out_shape),
+        in_specs=in_specs,
+        out_specs=out_specs,
         scratch_shapes=scratch,
-        compiler_params=pltpu.CompilerParams(vmem_limit_bytes=20 * MIB),
+        compiler_params=pltpu.CompilerParams(vmem_limit_bytes=14 * MIB),
         cost_estimate=pl.CostEstimate(
             flops=flops, bytes_accessed=4 * MIB, transcendentals=total * length
         ),
@@ -307,15 +342,9 @@
 
 
 def finish_kernel(chunks, heads, tile, *refs):
-    value_ref, weight_ref, out_ref, rows_ref, values_ref, tiles_ref, sem = refs[-7:]
-    copies = [
-        pltpu.make_async_copy(
-            weight_ref.at[:, at * tile : (at + 1) * tile], tiles_ref.at[at], sem.at[at]
-        )
-        for at in range(tiles_ref.shape[0])
-    ]
-    for copy in copies:
-        copy.start()
+    value_ref = refs[4 * chunks]
+    weight_refs = refs[4 * chunks + 1 : -3]
+    out_ref, rows_ref, values_ref = refs[-3:]
     lanes = rows_ref.shape[0]
     end = 0
     for index in range(chunks):
@@ -340,18 +369,23 @@
         )
         values_ref[:, head * width : (head + 1) * width] = values.astype(jnp.bfloat16)
     values = values_ref[...]
-    for at, copy in enumerate(copies):
-        copy.wait()
-        share = jnp.dot(values, tiles_ref[at], preferred_element_type=jnp.float32)
-        if len(out_ref.shape) == 3:
-            out_ref[at] = share.astype(out_ref.dtype)
-        else:
-            out_ref[:, at * tile : (at + 1) * tile] = share.astype(out_ref.dtype)
-
-
-def finish(chunk_parts, value_up, out_proj, parts):
+    at = 0
+    for weight_ref in weight_refs:
+        for start in range(0, weight_ref.shape[1], tile):
+            share = jnp.dot(
+                values, weight_ref[:, start : start + tile], preferred_element_type=jnp.float32
+            )
+            if len(out_ref.shape) == 3:
+                out_ref[at] = share.astype(out_ref.dtype)
+            else:
+                out_ref[:, at * tile : (at + 1) * tile] = share.astype(out_ref.dtype)
+            at += 1
+
+
+def finish(chunk_parts, value_up, weights, parts):
     heads, latent, width = value_up.shape
-    depth, columns = out_proj.shape
+    depth = weights[0].shape[0]
+    columns = sum(weight.shape[1] for weight in weights)
     operands = []
     rows = 0
     for left, right, (part, stats) in chunk_parts:
@@ -362,32 +396,30 @@
     if share % 128 == 0:
         tile, shape = share, (parts, lines, share)
     else:
-        tile, shape = columns // 8 if columns % 1024 == 0 else columns, (lines, columns)
+        tile, shape = columns // 8, (lines, columns)
     out = pl.pallas_call(
         functools.partial(finish_kernel, len(chunk_parts), heads, tile),
         out_shape=jax.ShapeDtypeStruct(shape, jnp.bfloat16),
-        in_specs=[whole()] * (len(operands) + 1) + [whole(pltpu.HBM)],
+        in_specs=[whole()] * (len(operands) + 1 + len(weights)),
         out_specs=whole(),
         scratch_shapes=[
             pltpu.VMEM((latent // 128, rows, 128), jnp.float32),
             pltpu.VMEM((lines, depth), jnp.bfloat16),
-            pltpu.VMEM((columns // tile, depth, tile), jnp.bfloat16),
-            pltpu.SemaphoreType.DMA((columns // tile,)),
         ],
-        compiler_params=pltpu.CompilerParams(vmem_limit_bytes=44 * MIB),
+        compiler_params=pltpu.CompilerParams(vmem_limit_bytes=10 * MIB),
         cost_estimate=pl.CostEstimate(
             flops=2 * lines * depth * columns,
             bytes_accessed=2 * depth * columns,
             transcendentals=1024,
         ),
         name="finish",
-    )(*operands, value_up, out_proj)
+    )(*operands, value_up, *weights)
     if share % 128:
         out = out.reshape(lines, parts, share).transpose(1, 0, 2)
     return out
 
 
-def plan_kernel(group_ref, place_ref, lengths_ref, donor_ref, info_ref, *, local_len, half):
+def plan_kernel(group_ref, place_ref, lengths_ref, donor_ref, info_ref, flag_ref, *, local_len):
     group, place = group_ref[0], place_ref[0]
     source = donor_ref[group]
     first = place * local_len
@@ -404,17 +436,18 @@
         crowded.append(one_far & two_far & (one != two))
     asked = jnp.where(plane == 0, wanted[1], wanted[0])
     info_ref[4] = jnp.where((asked & 1) == core, 1, 0)
-    info_ref[5] = core * half
-    info_ref[6] = jnp.where(crowded[0] | crowded[1], 1, 0)
-    info_ref[7] = (1 - core) * half
-
-
-def plan(lengths, donor, local_len, half):
+    flag = jnp.where(crowded[0] | crowded[1], 1, 0)
+    info_ref[5] = flag
+    flag_ref[0] = flag
+
+
+def plan(lengths, donor, local_len):
     return pl.pallas_call(
-        functools.partial(plan_kernel, local_len=local_len, half=half),
-        out_shape=jax.ShapeDtypeStruct((8,), jnp.int32),
+        functools.partial(plan_kernel, local_len=local_len),
+        out_shape=[jax.ShapeDtypeStruct((6,), jnp.int32), jax.ShapeDtypeStruct((1,), jnp.int32)],
         in_specs=[whole(pltpu.SMEM)] * 4,
-        out_specs=whole(pltpu.SMEM),
+        out_specs=[whole(pltpu.SMEM)] * 2,
+        compiler_params=pltpu.CompilerParams(vmem_limit_bytes=MIB),
         name="plan",
     )(
         lax.axis_index("grp").reshape(1),
@@ -445,13 +478,14 @@
     half = own.shape[0] // 2
     return pl.pallas_call(
         offer_kernel,
-        out_shape=jax.ShapeDtypeStruct((half, own.shape[1]), own.dtype),
-        in_specs=[whole(pltpu.SMEM), whole(pl.ANY), whole(pl.ANY)],
+        out_shape=pltpu.VMEM((half, own.shape[1]), own.dtype),
+        in_specs=[whole(pltpu.SMEM), whole(pltpu.HBM), whole(pltpu.HBM)],
         out_specs=whole(),
         scratch_shapes=[pltpu.SemaphoreType.DMA],
+        compiler_params=pltpu.CompilerParams(vmem_limit_bytes=4 * MIB),
         cost_estimate=pl.CostEstimate(flops=0, bytes_accessed=2 * MIB, transcendentals=0),
         name="offer",
-    )(info, own, beside)
+    )(info, in_hbm(own), in_hbm(beside))
 
 
 core_swap = functools.partial(lax.ppermute, axis_name="grp", perm=[(g, g ^ 1) for g in range(4)])
@@ -459,14 +493,19 @@
 
 
 def exchange_all(cache_t, info):
-    half = cache_t.shape[0] // 2
     across = plane_swap(cache_t)
     corner = core_swap(across)
-    rows = jnp.where(info[3] == info[2] ^ 2, across, corner)
-    return (
-        lax.dynamic_slice_in_dim(rows, info[5], half, 0),
-        lax.dynamic_slice_in_dim(rows, info[7], half, 0),
-    )
+    return jnp.where(info[3] == info[2] ^ 2, across, corner)
+
+
+def blank(like):
+    return pl.pallas_call(
+        lambda out_ref: None,
+        out_shape=jax.ShapeDtypeStruct(like.shape, like.dtype),
+        out_specs=whole(pl.ANY),
+        compiler_params=pltpu.CompilerParams(vmem_limit_bytes=MIB),
+        name="blank",
+    )()
 
 
 def tie(came, other):
@@ -480,7 +519,7 @@
     latent = value_up.shape[1]
     cache_t = jnp.swapaxes(cache[0], 0, 1)
     local_len = cache_t.shape[1]
-    info = plan(lengths, donor, local_len, key_width // 2)
+    info, crowded = plan(lengths, donor, local_len)
     fresh = new_latent.reshape(steps, samples, key_width)
 
     ring = list(range(0, parts, 2)) + list(range(parts - 1, 0, -2))
@@ -512,12 +551,22 @@
                 found.append((block, low - first, high - first))
         return found
 
+    width = out_proj.shape[1]
+    quarter = width // 4 if width % 512 == 0 else width
+    loaded = []
+
     def attend_early(hop):
         pieces = pieces_of(hop, 0, cut)
         if hop == 0:
-            return attend(["own"], pieces, [cache_t], info, 0, latent, fresh, (0, heads))
+            return None
         kinds = ["ends"] if hop == reach else ["keep", "keep"]
-        return attend(kinds, pieces, [cache_t], info, 0, latent)
+        start = (hop - 1) * quarter
+        if hop == reach or start >= width or hop > 2:
+            return attend(kinds, pieces, [cache_t], info, 0, latent)
+        load = (out_proj, start, start + quarter)
+        *results, piece = attend(kinds, pieces, [cache_t], info, 0, latent, load=load)
+        loaded.append(piece)
+        return results
 
     early_parts = []
     for hop in range(1, reach + 1):
@@ -528,10 +577,18 @@
                 right(lefts[-1][:half]),
                 left(rights[-1][half:]) if half < rows else None,
             )
-        extra = offer(info, cache_t, beside) if hop == 1 and four else None
+        extra = None
+        if hop == 1 and four:
+            extra = offer(info, cache_t, beside)
+        elif hop == 2 and four:
+            extra = lax.cond(
+                crowded.reshape(()) != 0, exchange_all, lambda rows, _: blank(rows), cache_t, info
+            )
         came, extra, parts_now = lax.optimization_barrier((came, extra, attend_early(hop - 1)))
         if hop == 1 and four:
             far_half = plane_swap(extra)
+        elif hop == 2 and four:
+            spare = extra
         lefts.append(came[0])
         rights.append(came[1])
         early_parts.append(parts_now)
@@ -539,15 +596,11 @@
 
     if four:
         far_half, lefts[reach] = lax.optimization_barrier((far_half, lefts[reach]))
-        far_rest = core_swap(far_half)
-        far_half, far_rest = lax.cond(
-            info[6] != 0, exchange_all, lambda *_: (far_half, far_rest), cache_t, info
-        )
-        moved = [cache_t, beside, far_half, far_rest]
+        moved = [cache_t, beside, far_half, core_swap(far_half), spare]
     else:
         shards = lax.all_gather(cache_t, "grp", axis=0, tiled=False)
         found = lax.dynamic_index_in_dim(shards, info[3], 0, keepdims=False)
-        moved = [found, found, found[: key_width // 2], found[key_width // 2 :]]
+        moved = [found, found, found[: key_width // 2], found[key_width // 2 :], found]
     *late_ends, moved_rows = attend(["ends"], pieces_of(reach, cut, rows), moved, info, 1, latent)
 
     def start_back(ends):
@@ -574,7 +627,24 @@
     for hop in range(1, reach):
         kinds += ["keep", "keep"]
         pieces += pieces_of(hop, cut, rows)
-    results = attend(kinds, pieces, [moved_rows], info, 1, latent, fresh, (HANDOVER, heads))
+
+    def load_more(limit):
+        start = quarter * len(loaded)
+        stop = min(start + quarter, width) if limit else width
+        return (out_proj, start, stop) if start < width else None
+
+    load = load_more(True)
+    results = attend(
+        kinds, pieces, [moved_rows], info, 1, latent, fresh, (HANDOVER, heads), load
+    )
+    if load:
+        loaded.append(results.pop())
+    load = load_more(False)
+    early_parts[0] = attend(
+        ["own"], pieces_of(0, 0, cut), [cache_t], info, 0, latent, fresh, (0, heads), load
+    )
+    if load:
+        loaded.append(early_parts[0].pop())
     late_came = hop_back(late_going)
     for hop in range(reach - 1, 0, -1):
         early_came = hop_back(merge_back(early_came, early_parts[hop], sections))
@@ -592,7 +662,7 @@
         for came, own in ((early_came, early_parts[0]), (late_came, late_parts[0]))
     ]
 
-    term = finish(finals, value_up, out_proj, parts)
+    term = finish(finals, value_up, loaded, parts)
     shares = lax.all_to_all(term, "ctx", split_axis=0, concat_axis=0, tiled=True)
     mixed = jnp.sum(shares.astype(jnp.float32), axis=0).astype(jnp.bfloat16)
     return mixed.reshape(steps, 1, samples, mixed.shape[-1])

time: 113 us -> 100 us (0.88)
  waiting for transfers between devices: 21 us -> 14.3 us
  local copies, waits for them, and re-layouts: 9.01 us -> 4.39 us
  Pallas kernels: 42.7 us -> 40.4 us
  blocking collectives: 10.4 us -> 12.5 us
    pallas_call x1, Pallas kernels: 10.8 us -> 4.48 us  [finish(): pl.pallas_call(functools.partial(finish_kernel, len(chunk_parts), heads,...]
    pallas_call x7, Pallas kernels: 25.8 us -> 31.9 us  [attend(): pl.pallas_call(functools.partial(attend_kernel, tuple(kinds), rows, takes...]
    ppermute x8, starting transfers between devices: 3.09 us -> 8.08 us  [hop_back(): right(to_the_right)]
    ppermute x8, starting transfers between devices: 13.4 us -> 8.49 us  [hop_back(): left(to_the_left)]
    unnamed x68 -> x18, local copies, waits for them, and re-layouts: 7.69 us -> 3.73 us
    ppermute x8, waiting for transfers between devices: 5.8 us -> 2.14 us  [hop_back(): right(to_the_right)]
    ppermute x8, waiting for transfers between devices: 7.49 us -> 5.12 us  [hop_back(): left(to_the_left)]
    all_to_all x1, blocking collectives: 10.4 us -> 12.5 us  [body(): lax.all_to_all(term, 'ctx', split_axis=0, concat_axis=0, tiled=True)]
  transfers between devices with their start and end apart: 27 -> 27, of which waited for: 13 -> 11; matrix products, arithmetic and copies ran while one was open for 1% -> 0% of each run, Pallas kernels for 27% -> 36%
where the time goes in v3:
time: 100 us; the launch traced here: 99.9 us
  Pallas kernels  40.4 us (40%)
  starting transfers between devices  27.3 us (27%)
  waiting for transfers between devices  14.3 us (14%)
  blocking collectives  12.5 us (12%)
  local copies, waits for them, and re-layouts  4.39 us (4%)
    pallas_call x7, Pallas kernels, attend(): pl.pallas_call(functools.partial(attend_kernel, tuple(kinds), rows, takes...  31.9 us
    all_to_all x1, blocking collectives, body(): lax.all_to_all(term, 'ctx', split_axis=0, concat_axis=0, tiled=True)  12.5 us
    ppermute x8, starting transfers between devices, hop_back(): left(to_the_left)  8.49 us
    ppermute x8, starting transfers between devices, hop_back(): right(to_the_right)  8.08 us
    ppermute x6, starting transfers between devices, body(): came = (right(lefts[-1]), left(rights[-1]))  6.63 us
    ppermute x6, waiting for transfers between devices, body(): came = (right(lefts[-1]), left(rights[-1]))  5.85 us
    ppermute x8, waiting for transfers between devices, hop_back(): left(to_the_left)  5.12 us
    pallas_call x1, Pallas kernels, finish(): pl.pallas_call(functools.partial(finish_kernel, len(chunk_parts), heads,...  4.48 us
  transfers between devices with their start and end apart: 27, of which 11 were waited for; matrix products, arithmetic and copies ran while one was open for 0% of the time, Pallas kernels for 36%

profile of v3, /device:TPU:0, one launch (start us, length us, event | category | flops | bytes accessed | tf_op | source)
XLA Modules:
  0.0 99.9 jit_solution(18267763363460250449)
XLA Ops:
  0.0 0.5 collective-permute-start.4
  0.5 2.6 %collective-permute-start.2 = (bf16[256,576]{1,0:T(8,128)(2,1)}, bf16[256,576]{1,0:T(8,128)(2,1)S(1)}, u32[]{:S(2)}, u32[]{:S(2)}) collective-permute-start(bf16[256,576]{1,0:T(8,128)(2,1)} %bitcast.9), channel_id=1, source_target_pairs={{0,2},{2,4},{4,6},{6,7},{7,5},{5,3},{3,1},{1,0},{8,10},{10,12},{12... | collective-permute-start | bytes 884744 | tf_op jit(solution)/shard_map/ppermute | solution.py:574
  3.0 0.7 copy-done.3
  3.7 0.7 copy-done.4
  4.3 1.2 %plan.1 = (s32[6]{0:T(128)S(1)}, s32[1]{0:T(128)}) custom-call(s32[1]{0:T(128)} %bitcast.1.group_ref, s32[1]{0:T(128)} %bitcast.2.place_ref, s32[4]{0:T(128)S(1)} %copy-done.3, s32[4]{0:T(128)S(1)} %copy-done.4), custom_call_target="tpu_custom_call" | custom-call | tf_op jit(solution)/shard_map/plan/pallas_call | solution.py:445
  5.5 1.4 %copy-done.7 = bf16[576,2048]{1,0:T(8,128)(2,1)} copy-done((bf16[576,2048]{1,0:T(8,128)(2,1)}, bf16[576,2048]{1,0:T(8,128)(2,1)S(1)}, u32[]{:S(2)}) %copy-start.7) | copy-done | bytes 2359320
  6.9 1.8 %offer.1 = bf16[288,2048]{1,0:T(8,128)(2,1)S(1)} custom-call(s32[6]{0:T(128)S(1)} %get-tuple-element.110.info_ref.refs_0_, bf16[576,2048]{1,0:T(8,128)(2,1)} %bitcast.16, bf16[576,2048]{1,0:T(8,128)(2,1)} %copy-done.7), custom_call_target="tpu_custom_call" | custom-call | bytes 2097152 | tf_op jit(solution)/shard_map/offer/pallas_call | solution.py:479
  8.8 2.8 %collective-permute-done.2.refs_2_.refs_3_ = bf16[256,576]{1,0:T(8,128)(2,1)S(1)} collective-permute-done((bf16[256,576]{1,0:T(8,128)(2,1)}, bf16[256,576]{1,0:T(8,128)(2,1)S(1)}, u32[]{:S(2)}, u32[]{:S(2)}) %collective-permute-start.2) | collective-permute-done | bytes 294944 | tf_op jit(solution)/shard_map/ppermute | solution.py:574
  11.5 1.5 %collective-permute-done.3.refs_3_.refs_4_ = bf16[256,576]{1,0:T(8,128)(2,1)S(1)} collective-permute-done((bf16[256,576]{1,0:T(8,128)(2,1)}, bf16[256,576]{1,0:T(8,128)(2,1)S(1)}, u32[]{:S(2)}, u32[]{:S(2)}) %collective-permute-start.3) | collective-permute-done | bytes 294944 | tf_op jit(solution)/shard_map/ppermute | solution.py:574
  13.1 1.5 %collective-permute-start.13 = (bf16[288,2048]{1,0:T(8,128)(2,1)S(1)}, bf16[288,2048]{1,0:T(8,128)(2,1)}, u32[]{:S(2)}, u32[]{:S(2)}) collective-permute-start(bf16[288,2048]{1,0:T(8,128)(2,1)S(1)} %offer.1), channel_id=1, source_target_pairs={{0,16},{8,24},{16,0},{24,8},{1,17},{9,25},{17,1},{25,9},{2,18},{10... | collective-permute-start | bytes 3538952 | tf_op jit(solution)/shard_map/ppermute | solution.py:589
  14.6 1.6 %collective-permute-start.5 = (bf16[256,576]{1,0:T(8,128)(2,1)S(1)}, bf16[256,576]{1,0:T(8,128)(2,1)S(1)}, u32[]{:S(2)}, u32[]{:S(2)}) collective-permute-start(bf16[256,576]{1,0:T(8,128)(2,1)S(1)} %collective-permute-done.2.refs_2_.refs_3_), channel_id=1, source_target_pairs={{0,2},{2,4},{4,6},{6,7},{7,5},{5,3},{3,1},{1,0},{8,10},{10,12},{12... | collective-permute-start | bytes 884744 | tf_op jit(solution)/shard_map/ppermute | solution.py:574
  16.2 0.4 collective-permute-start.6
  17.3 6.9 %attend_keep_keep.3 = (f32[192,512]{1,0:T(8,128)S(1)}, f32[8,96]{1,0:T(8,128)S(1)}, f32[192,512]{1,0:T(8,128)S(1)}, f32[8,96]{1,0:T(8,128)S(1)}, bf16[2048,1792]{1,0:T(8,128)(2,1)S(1)}) custom-call(s32[6]{0:T(128)S(1)} %get-tuple-element.110.info_ref.refs_0_, bf16[576,2048]{1,0:T(8,128)(2,1)} %bitcast.18, ...), custom_call_target="tpu_custom_call" | custom-call | flops 1711276032 | bytes 4194304 | tf_op jit(solution)/shard_map/attend_keep_keep/pallas_call | solution.py:287
  24.6 1.6 %collective-permute-start.7 = (bf16[256,576]{1,0:T(8,128)(2,1)S(1)}, bf16[256,576]{1,0:T(8,128)(2,1)S(1)}, u32[]{:S(2)}, u32[]{:S(2)}) collective-permute-start(bf16[256,576]{1,0:T(8,128)(2,1)S(1)} %collective-permute-done.5.refs_2_.refs_5_), channel_id=1, source_target_pairs={{0,2},{2,4},{4,6},{6,7},{7,5},{5,3},{3,1},{1,0},{8,10},{10,12},{12... | collective-permute-start | bytes 884744 | tf_op jit(solution)/shard_map/ppermute | solution.py:574
  26.2 0.4 collective-permute-start.8
  26.7 6.0 %attend_keep_keep.4 = (f32[192,512]{1,0:T(8,128)S(1)}, f32[8,96]{1,0:T(8,128)S(1)}, f32[192,512]{1,0:T(8,128)S(1)}, f32[8,96]{1,0:T(8,128)S(1)}, bf16[2048,1792]{1,0:T(8,128)(2,1)S(1)}) custom-call(s32[6]{0:T(128)S(1)} %get-tuple-element.110.info_ref.refs_0_, bf16[576,2048]{1,0:T(8,128)(2,1)S(1)} %bitcast.20, ...), custom_call_target="tpu_custom_call" | custom-call | flops 1711276032 | bytes 4194304 | tf_op jit(solution)/shard_map/attend_keep_keep/pallas_call | solution.py:287
  32.7 1.2 %collective-permute-done.8.refs_3_.refs_8_ = bf16[256,576]{1,0:T(8,128)(2,1)S(1)} collective-permute-done((bf16[256,576]{1,0:T(8,128)(2,1)S(1)}, bf16[256,576]{1,0:T(8,128)(2,1)S(1)}, u32[]{:S(2)}, u32[]{:S(2)}) %collective-permute-start.8) | collective-permute-done | bytes 294944 | tf_op jit(solution)/shard_map/ppermute | solution.py:574
  33.9 0.5 collective-permute-start.10
  34.5 1.6 %collective-permute-start.9 = (bf16[128,576]{1,0:T(8,128)(2,1)S(1)}, bf16[128,576]{1,0:T(8,128)(2,1)S(1)}, u32[]{:S(2)}, u32[]{:S(2)}) collective-permute-start(bf16[128,576]{1,0:T(8,128)(2,1)S(1)} %slice.12), channel_id=1, source_target_pairs={{0,2},{2,4},{4,6},{6,7},{7,5},{5,3},{3,1},{1,0},{8,10},{10,12},{12... | collective-permute-start | bytes 442376 | tf_op jit(solution)/shard_map/ppermute | solution.py:577
  36.1 3.2 %attend_keep_keep.5 = (f32[192,512]{1,0:T(8,128)S(1)}, f32[8,96]{1,0:T(8,128)S(1)}, f32[192,512]{1,0:T(8,128)S(1)}, f32[8,96]{1,0:T(8,128)S(1)}) custom-call(s32[6]{0:T(128)S(1)} %get-tuple-element.110.info_ref.refs_0_, bf16[576,2048]{1,0:T(8,128)(2,1)S(1)} %bitcast.21, bf16[256,576]{1,0:T(8,128)(2,1)S(1)} %collective-permute-done.7.refs_2_.refs_7_, ...), custom_call_target="tpu_custom_call" | custom-call | flops 1711276032 | bytes 4194304 | tf_op jit(solution)/shard_map/attend_keep_keep/pallas_call | solution.py:287
  39.3 0.5 collective-permute-done.9.refs_2_
  39.8 0.6 collective-permute-done.13.refs_3_
  40.5 2.3 %attend_ends.2 = (bf16[112,512]{1,0:T(8,128)(2,1)S(1)}, bf16[112,512]{1,0:T(8,128)(2,1)S(1)}) custom-call(s32[6]{0:T(128)S(1)} %get-tuple-element.110.info_ref.refs_0_, bf16[576,2048]{1,0:T(8,128)(2,1)S(1)} %bitcast.22, bf16[128,576]{1,0:T(8,128)(2,1)S(1)} %collective-permute-done.9.refs_2_, bf16[128,576]{1,0:T(8,128)(2,1)S(1)} %collective-permute-done.10.refs_3_.refs_6_), custom_call_target="tpu_custom_call" | custom-call | flops 855638016 | bytes 4194304 | tf_op jit(solution)/shard_map/attend_ends/pallas_call | solution.py:287
  42.8 0.7 collective-permute-start.11
  43.5 1.4 %collective-permute-start.12 = (bf16[112,512]{1,0:T(8,128)(2,1)S(1)}, bf16[112,512]{1,0:T(8,128)(2,1)S(1)}, u32[]{:S(2)}, u32[]{:S(2)}) collective-permute-start(bf16[112,512]{1,0:T(8,128)(2,1)S(1)} %get-tuple-element.133), channel_id=1, source_target_pairs={{0,2},{2,4},{4,6},{6,7},{7,5},{5,3},{3,1},{1,0},{8,10},{10,12},{12... | collective-permute-start | bytes 344072 | tf_op jit(solution)/shard_map/ppermute | solution.py:615
  44.9 1.0 copy-done.8
  45.9 3.5 %attend_ends.3 = (bf16[48,512]{1,0:T(8,128)(2,1)S(1)}, bf16[48,512]{1,0:T(8,128)(2,1)S(1)}, bf16[576,2048]{1,0:T(8,128)(2,1)S(1)}) custom-call(s32[6]{0:T(128)S(1)} %get-tuple-element.110.info_ref.refs_0_, bf16[576,2048]{1,0:T(8,128)(2,1)} %bitcast.19, bf16[576,2048]{1,0:T(8,128)(2,1)} %copy-done.7, bf16[288,2048]{1,0:T(8,128)(2,1)} %collective-permute-done.13.refs_3_, ...), custom_call_target="tpu_custom_call" | custom-call | flops 285212672 | bytes 4194304 | tf_op jit(solution)/shard_map/attend_ends/pallas_call | solution.py:287
  49.6 0.8 collective-permute-start.15
  50.4 1.3 %collective-permute-start.16 = (bf16[208,512]{1,0:T(8,128)(2,1)S(1)}, bf16[208,512]{1,0:T(8,128)(2,1)S(1)}, u32[]{:S(2)}, u32[]{:S(2)}) collective-permute-start(bf16[208,512]{1,0:T(8,128)(2,1)S(1)} %get-tuple-element.146), channel_id=1, source_target_pairs={{0,2},{2,4},{4,6},{6,7},{7,5},{5,3},{3,1},{1,0},{8,10},{10,12},{12... | collective-permute-start | bytes 638984 | tf_op jit(solution)/shard_map/ppermute | solution.py:615
  51.7 0.8 collective-permute-start.17
  52.4 1.3 %collective-permute-start.18 = (bf16[48,512]{1,0:T(8,128)(2,1)S(1)}, bf16[48,512]{1,0:T(8,128)(2,1)S(1)}, u32[]{:S(2)}, u32[]{:S(2)}) collective-permute-start(bf16[48,512]{1,0:T(8,128)(2,1)S(1)} %get-tuple-element.163), channel_id=1, source_target_pairs={{0,2},{2,4},{4,6},{6,7},{7,5},{5,3},{3,1},{1,0},{8,10},{10,12},{12... | collective-permute-start | bytes 147464 | tf_op jit(solution)/shard_map/ppermute | solution.py:615
  53.7 6.2 %attend_own_keep_keep_keep_keep_keep_keep.1 = (f32[64,512]{1,0:T(8,128)S(1)}, f32[8,32]{1,0:T(8,128)S(1)}, f32[64,512]{1,0:T(8,128)S(1)}, f32[8,32]{1,0:T(8,128)...) custom-call(s32[6]{0:T(128)S(1)} %get-tuple-element.110.info_ref.ref, ...), custom_call_target="tpu_custom_call" | custom-call | flops 1996488704 | bytes 4194304 | tf_op jit(solution)/shard_map/attend_own_keep_keep_keep_keep_keep_keep/pallas_call | solution.py:287
  60.2 0.8 collective-permute-start.19
  61.0 1.3 %collective-permute-start.20 = (bf16[208,512]{1,0:T(8,128)(2,1)S(1)}, bf16[208,512]{1,0:T(8,128)(2,1)S(1)}, u32[]{:S(2)}, u32[]{:S(2)}) collective-permute-start(bf16[208,512]{1,0:T(8,128)(2,1)S(1)} %get-tuple-element.173), channel_id=1, source_target_pairs={{0,2},{2,4},{4,6},{6,7},{7,5},{5,3},{3,1},{1,0},{8,10},{10,12},{12... | collective-permute-start | bytes 638984 | tf_op jit(solution)/shard_map/ppermute | solution.py:615
  62.4 0.8 collective-permute-start.23
  63.2 1.3 %collective-permute-start.24 = (bf16[80,512]{1,0:T(8,128)(2,1)S(1)}, bf16[80,512]{1,0:T(8,128)(2,1)S(1)}, u32[]{:S(2)}, u32[]{:S(2)}) collective-permute-start(bf16[80,512]{1,0:T(8,128)(2,1)S(1)} %get-tuple-element.189), channel_id=1, source_target_pairs={{0,2},{2,4},{4,6},{6,7},{7,5},{5,3},{3,1},{1,0},{8,10},{10,12},{12... | collective-permute-start | bytes 245768 | tf_op jit(solution)/shard_map/ppermute | solution.py:615
  64.5 2.6 %collective-permute-done.19.refs_0_ = bf16[208,512]{1,0:T(8,128)(2,1)S(1)} collective-permute-done((bf16[208,512]{1,0:T(8,128)(2,1)S(1)}, bf16[208,512]{1,0:T(8,128)(2,1)S(1)}, u32[]{:S(2)}, u32[]{:S(2)}) %collective-permute-start.19) | collective-permute-done | bytes 213024 | tf_op jit(solution)/shard_map/ppermute | solution.py:614
  67.7 1.5 %collective-permute-start.21 = (bf16[208,512]{1,0:T(8,128)(2,1)S(1)}, bf16[208,512]{1,0:T(8,128)(2,1)S(1)}, u32[]{:S(2)}, u32[]{:S(2)}) collective-permute-start(bf16[208,512]{1,0:T(8,128)(2,1)S(1)} %get-tuple-element.176), channel_id=1, source_target_pairs={{2,0},{4,2},{6,4},{7,6},{5,7},{3,5},{1,3},{0,1},{10,8},{12,10},{14... | collective-permute-start | bytes 638984 | tf_op jit(solution)/shard_map/ppermute | solution.py:614
  69.2 0.6 collective-permute-start.22
  69.9 1.5 %collective-permute-start.25 = (bf16[80,512]{1,0:T(8,128)(2,1)S(1)}, bf16[80,512]{1,0:T(8,128)(2,1)S(1)}, u32[]{:S(2)}, u32[]{:S(2)}) collective-permute-start(bf16[80,512]{1,0:T(8,128)(2,1)S(1)} %get-tuple-element.192), channel_id=1, source_target_pairs={{2,0},{4,2},{6,4},{7,6},{5,7},{3,5},{1,3},{0,1},{10,8},{12,10},{14... | collective-permute-start | bytes 245768 | tf_op jit(solution)/shard_map/ppermute | solution.py:614
  71.4 0.6 collective-permute-start.26
  72.0 2.5 %collective-permute-done.25.refs_0_ = bf16[80,512]{1,0:T(8,128)(2,1)S(1)} collective-permute-done((bf16[80,512]{1,0:T(8,128)(2,1)S(1)}, bf16[80,512]{1,0:T(8,128)(2,1)S(1)}, u32[]{:S(2)}, u32[]{:S(2)}) %collective-permute-start.25) | collective-permute-done | bytes 81952 | tf_op jit(solution)/shard_map/ppermute | solution.py:614
  74.5 1.5 %collective-permute-done.26.refs_3_ = bf16[80,512]{1,0:T(8,128)(2,1)S(1)} collective-permute-done((bf16[80,512]{1,0:T(8,128)(2,1)S(1)}, bf16[80,512]{1,0:T(8,128)(2,1)S(1)}, u32[]{:S(2)}, u32[]{:S(2)}) %collective-permute-start.26) | collective-permute-done | bytes 81952 | tf_op jit(solution)/shard_map/ppermute | solution.py:615
  76.1 1.6 %collective-permute-start.27 = (bf16[80,512]{1,0:T(8,128)(2,1)S(1)}, bf16[80,512]{1,0:T(8,128)(2,1)S(1)}, u32[]{:S(2)}, u32[]{:S(2)}) collective-permute-start(bf16[80,512]{1,0:T(8,128)(2,1)S(1)} %get-tuple-element.198), channel_id=1, source_target_pairs={{2,0},{4,2},{6,4},{7,6},{5,7},{3,5},{1,3},{0,1},{10,8},{12,10},{14... | collective-permute-start | bytes 245768 | tf_op jit(solution)/shard_map/ppermute | solution.py:614
  78.2 3.7 %attend_own.1 = (f32[192,512]{1,0:T(8,128)S(1)}, f32[8,96]{1,0:T(8,128)S(1)}, bf16[2048,1792]{1,0:T(8,128)(2,1)S(1)}) custom-call(s32[6]{0:T(128)S(1)} %get-tuple-element.110.info_ref.refs_0_, bf16[576,2048]{1,0:T(8,128)(2,1)S(1)} %bitcast.23, bf16[256,576]{1,0:T(8,128)(2,1)S(1)} %bitcast.12, bf16[4,4,576]{2,1,0:T(4,128)(2,1)S(1)} %bitcast.14, ...), custom_call_target="tpu_custom_call" | custom-call | flops 855638016 | bytes 4194304 | tf_op jit(solution)/shard_map/attend_own/pallas_call | solution.py:287
  82.2 4.5 %finish.1 = bf16[8,16,896]{2,1,0:T(8,128)(2,1)S(1)} custom-call(bf16[208,512]{1,0:T(8,128)(2,1)S(1)} %collective-permute-done.21.refs_0_, bf16[208,512]{1,0:T(8,128)(2,1)S(1)} %collective-permute-done.22.refs_1_, f32[192,512]{1,0:T(8,128)S(1)} %get-tuple-element.178.refs_2_, f32[8,96]{1,0:T(8,128)S(1)} %get-tuple-element.179.refs_3_, ...), custom_call_target="tpu_custom_call" | custom-call | flops 469762048 | bytes 29360128 | tf_op jit(solution)/shard_map/finish/pallas_call | solution.py:400
  86.7 12.5 %all_to_all.5 = bf16[8,16,896]{2,1,0:T(8,128)(2,1)S(1)} all-to-all(bf16[8,16,896]{2,1,0:T(8,128)(2,1)S(1)} %finish.1), channel_id=1, replica_groups=mesh['grp'=4,'ctx'=8] {'ctx'}, dimensions={0} | all-to-all | bytes 458752 | tf_op jit(solution)/shard_map/all_to_all | solution.py:666
  99.3 0.6 reshape.27
  (47 shorter events, 2.6 us)
Async XLA Ops:
  0.0 5.5 %collective-permute-start.4 = (bf16[576,2048]{1,0:T(8,128)(2,1)}, bf16[576,2048]{1,0:T(8,128)(2,1)S(1)}, u32[]{:S(2)}, u32[]{:S(2)}) collective-permute-start(bf16[576,2048]{1,0:T(8,128)(2,1)} %bitcast.15), channel_id=1, source_target_pairs={{0,8},{8,0},{16,24},{24,16},{1,9},{9,1},{17,25},{25,17},{2,10},{10... | collective-permute-start | bytes 7077896 | tf_op jit(solution)/shard_map/ppermute | solution.py:538
  0.5 11.1 %collective-permute-start.2 = (bf16[256,576]{1,0:T(8,128)(2,1)}, bf16[256,576]{1,0:T(8,128)(2,1)S(1)}, u32[]{:S(2)}, u32[]{:S(2)}) collective-permute-start(bf16[256,576]{1,0:T(8,128)(2,1)} %bitcast.9), channel_id=1, source_target_pairs={{0,2},{2,4},{4,6},{6,7},{7,5},{5,3},{3,1},{1,0},{8,10},{10,12},{12... | collective-permute-start | bytes 884744 | tf_op jit(solution)/shard_map/ppermute | solution.py:574
  3.0 10.1 %collective-permute-start.3 = (bf16[256,576]{1,0:T(8,128)(2,1)}, bf16[256,576]{1,0:T(8,128)(2,1)S(1)}, u32[]{:S(2)}, u32[]{:S(2)}) collective-permute-start(bf16[256,576]{1,0:T(8,128)(2,1)} %bitcast.10), channel_id=1, source_target_pairs={{2,0},{4,2},{6,4},{7,6},{5,7},{3,5},{1,3},{0,1},{10,8},{12,10},{14... | collective-permute-start | bytes 884744 | tf_op jit(solution)/shard_map/ppermute | solution.py:574
  3.0 0.7 copy-start.3
  3.7 0.7 copy-start.4
  5.5 1.4 %copy-start.7 = (bf16[576,2048]{1,0:T(8,128)(2,1)}, bf16[576,2048]{1,0:T(8,128)(2,1)S(1)}, u32[]{:S(2)}) copy-start(bf16[576,2048]{1,0:T(8,128)(2,1)S(1)} %collective-permute-done.4.beside_ref.refs_2_) | copy-start | bytes 7077892
  13.1 27.4 %collective-permute-start.13 = (bf16[288,2048]{1,0:T(8,128)(2,1)S(1)}, bf16[288,2048]{1,0:T(8,128)(2,1)}, u32[]{:S(2)}, u32[]{:S(2)}) collective-permute-start(bf16[288,2048]{1,0:T(8,128)(2,1)S(1)} %offer.1), channel_id=1, source_target_pairs={{0,16},{8,24},{16,0},{24,8},{1,17},{9,25},{17,1},{25,9},{2,18},{10... | collective-permute-start | bytes 3538952 | tf_op jit(solution)/shard_map/ppermute | solution.py:589
  14.6 9.7 %collective-permute-start.5 = (bf16[256,576]{1,0:T(8,128)(2,1)S(1)}, bf16[256,576]{1,0:T(8,128)(2,1)S(1)}, u32[]{:S(2)}, u32[]{:S(2)}) collective-permute-start(bf16[256,576]{1,0:T(8,128)(2,1)S(1)} %collective-permute-done.2.refs_2_.refs_3_), channel_id=1, source_target_pairs={{0,2},{2,4},{4,6},{6,7},{7,5},{5,3},{3,1},{1,0},{8,10},{10,12},{12... | collective-permute-start | bytes 884744 | tf_op jit(solution)/shard_map/ppermute | solution.py:574
  16.2 8.5 %collective-permute-start.6 = (bf16[256,576]{1,0:T(8,128)(2,1)S(1)}, bf16[256,576]{1,0:T(8,128)(2,1)S(1)}, u32[]{:S(2)}, u32[]{:S(2)}) collective-permute-start(bf16[256,576]{1,0:T(8,128)(2,1)S(1)} %collective-permute-done.3.refs_3_.refs_4_), channel_id=1, source_target_pairs={{2,0},{4,2},{6,4},{7,6},{5,7},{3,5},{1,3},{0,1},{10,8},{12,10},{14... | collective-permute-start | bytes 884744 | tf_op jit(solution)/shard_map/ppermute | solution.py:574
  17.3 9.3 %copy-start.5 = (bf16[1,2048,576]{1,2,0:T(8,128)(2,1)S(1)}, bf16[1,2048,576]{1,2,0:T(8,128)(2,1)}, u32[]{:S(2)}) copy-start(bf16[1,2048,576]{1,2,0:T(8,128)(2,1)} %param.9) | copy-start | bytes 7077892
  24.6 8.1 %collective-permute-start.7 = (bf16[256,576]{1,0:T(8,128)(2,1)S(1)}, bf16[256,576]{1,0:T(8,128)(2,1)S(1)}, u32[]{:S(2)}, u32[]{:S(2)}) collective-permute-start(bf16[256,576]{1,0:T(8,128)(2,1)S(1)} %collective-permute-done.5.refs_2_.refs_5_), channel_id=1, source_target_pairs={{0,2},{2,4},{4,6},{6,7},{7,5},{5,3},{3,1},{1,0},{8,10},{10,12},{12... | collective-permute-start | bytes 884744 | tf_op jit(solution)/shard_map/ppermute | solution.py:574
  26.2 7.7 %collective-permute-start.8 = (bf16[256,576]{1,0:T(8,128)(2,1)S(1)}, bf16[256,576]{1,0:T(8,128)(2,1)S(1)}, u32[]{:S(2)}, u32[]{:S(2)}) collective-permute-start(bf16[256,576]{1,0:T(8,128)(2,1)S(1)} %collective-permute-done.6.refs_3_.refs_6_), channel_id=1, source_target_pairs={{2,0},{4,2},{6,4},{7,6},{5,7},{3,5},{1,3},{0,1},{10,8},{12,10},{14... | collective-permute-start | bytes 884744 | tf_op jit(solution)/shard_map/ppermute | solution.py:574
  33.9 5.4 %collective-permute-start.10 = (bf16[128,576]{1,0:T(8,128)(2,1)S(1)}, bf16[128,576]{1,0:T(8,128)(2,1)S(1)}, u32[]{:S(2)}, u32[]{:S(2)}) collective-permute-start(bf16[128,576]{1,0:T(8,128)(2,1)S(1)} %slice.13), channel_id=1, source_target_pairs={{2,0},{4,2},{6,4},{7,6},{5,7},{3,5},{1,3},{0,1},{10,8},{12,10},{14... | collective-permute-start | bytes 442376 | tf_op jit(solution)/shard_map/ppermute | solution.py:578
  34.5 5.4 %collective-permute-start.9 = (bf16[128,576]{1,0:T(8,128)(2,1)S(1)}, bf16[128,576]{1,0:T(8,128)(2,1)S(1)}, u32[]{:S(2)}, u32[]{:S(2)}) collective-permute-start(bf16[128,576]{1,0:T(8,128)(2,1)S(1)} %slice.12), channel_id=1, source_target_pairs={{0,2},{2,4},{4,6},{6,7},{7,5},{5,3},{3,1},{1,0},{8,10},{10,12},{12... | collective-permute-start | bytes 442376 | tf_op jit(solution)/shard_map/ppermute | solution.py:577
  40.5 4.4 %collective-permute-start.14 = (bf16[288,2048]{1,0:T(8,128)(2,1)}, bf16[288,2048]{1,0:T(8,128)(2,1)S(1)}, u32[]{:S(2)}, u32[]{:S(2)}) collective-permute-start(bf16[288,2048]{1,0:T(8,128)(2,1)} %collective-permute-done.13.refs_3_), channel_id=1, source_target_pairs={{0,8},{8,0},{16,24},{24,16},{1,9},{9,1},{17,25},{25,17},{2,10},{10... | collective-permute-start | bytes 3538952 | tf_op jit(solution)/shard_map/ppermute | solution.py:599
  42.8 6.6 %collective-permute-start.11 = (bf16[112,512]{1,0:T(8,128)(2,1)S(1)}, bf16[112,512]{1,0:T(8,128)(2,1)S(1)}, u32[]{:S(2)}, u32[]{:S(2)}) collective-permute-start(bf16[112,512]{1,0:T(8,128)(2,1)S(1)} %get-tuple-element.132), channel_id=1, source_target_pairs={{2,0},{4,2},{6,4},{7,6},{5,7},{3,5},{1,3},{0,1},{10,8},{12,10},{14... | collective-permute-start | bytes 344072 | tf_op jit(solution)/shard_map/ppermute | solution.py:614
  43.4 10.3 %copy-start.1 = (bf16[4,1,4,16,576]{4,3,2,1,0:T(8,128)(2,1)S(1)}, bf16[4,1,4,16,576]{4,3,2,1,0:T(8,128)(2,1)}, u32[]{:S(2)}) copy-start(bf16[4,1,4,16,576]{4,3,2,1,0:T(8,128)(2,1)} %param.10) | copy-start | bytes 884740
  43.4 10.3 %copy-start.2 = (bf16[4,1,4,576]{3,2,1,0:T(4,128)(2,1)S(1)}, bf16[4,1,4,576]{3,2,1,0:T(4,128)(2,1)}, u32[]{:S(2)}) copy-start(bf16[4,1,4,576]{3,2,1,0:T(4,128)(2,1)} %param.11) | copy-start | bytes 55300
  43.5 6.0 %collective-permute-start.12 = (bf16[112,512]{1,0:T(8,128)(2,1)S(1)}, bf16[112,512]{1,0:T(8,128)(2,1)S(1)}, u32[]{:S(2)}, u32[]{:S(2)}) collective-permute-start(bf16[112,512]{1,0:T(8,128)(2,1)S(1)} %get-tuple-element.133), channel_id=1, source_target_pairs={{0,2},{2,4},{4,6},{6,7},{7,5},{5,3},{3,1},{1,0},{8,10},{10,12},{12... | collective-permute-start | bytes 344072 | tf_op jit(solution)/shard_map/ppermute | solution.py:615
  44.9 1.0 %copy-start.8 = (bf16[288,2048]{1,0:T(8,128)(2,1)}, bf16[288,2048]{1,0:T(8,128)(2,1)S(1)}, u32[]{:S(2)}) copy-start(bf16[288,2048]{1,0:T(8,128)(2,1)S(1)} %collective-permute-done.14.refs_4_) | copy-start | bytes 3538948
  49.6 10.4 %collective-permute-start.15 = (bf16[208,512]{1,0:T(8,128)(2,1)S(1)}, bf16[208,512]{1,0:T(8,128)(2,1)S(1)}, u32[]{:S(2)}, u32[]{:S(2)}) collective-permute-start(bf16[208,512]{1,0:T(8,128)(2,1)S(1)} %get-tuple-element.145), channel_id=1, source_target_pairs={{2,0},{4,2},{6,4},{7,6},{5,7},{3,5},{1,3},{0,1},{10,8},{12,10},{14... | collective-permute-start | bytes 638984 | tf_op jit(solution)/shard_map/ppermute | solution.py:614
  50.4 9.6 %collective-permute-start.16 = (bf16[208,512]{1,0:T(8,128)(2,1)S(1)}, bf16[208,512]{1,0:T(8,128)(2,1)S(1)}, u32[]{:S(2)}, u32[]{:S(2)}) collective-permute-start(bf16[208,512]{1,0:T(8,128)(2,1)S(1)} %get-tuple-element.146), channel_id=1, source_target_pairs={{0,2},{2,4},{4,6},{6,7},{7,5},{5,3},{3,1},{1,0},{8,10},{10,12},{12... | collective-permute-start | bytes 638984 | tf_op jit(solution)/shard_map/ppermute | solution.py:615
  51.7 8.3 %collective-permute-start.17 = (bf16[48,512]{1,0:T(8,128)(2,1)S(1)}, bf16[48,512]{1,0:T(8,128)(2,1)S(1)}, u32[]{:S(2)}, u32[]{:S(2)}) collective-permute-start(bf16[48,512]{1,0:T(8,128)(2,1)S(1)} %get-tuple-element.162), channel_id=1, source_target_pairs={{2,0},{4,2},{6,4},{7,6},{5,7},{3,5},{1,3},{0,1},{10,8},{12,10},{14... | collective-permute-start | bytes 147464 | tf_op jit(solution)/shard_map/ppermute | solution.py:614
  52.4 7.5 %collective-permute-start.18 = (bf16[48,512]{1,0:T(8,128)(2,1)S(1)}, bf16[48,512]{1,0:T(8,128)(2,1)S(1)}, u32[]{:S(2)}, u32[]{:S(2)}) collective-permute-start(bf16[48,512]{1,0:T(8,128)(2,1)S(1)} %get-tuple-element.163), channel_id=1, source_target_pairs={{0,2},{2,4},{4,6},{6,7},{7,5},{5,3},{3,1},{1,0},{8,10},{10,12},{12... | collective-permute-start | bytes 147464 | tf_op jit(solution)/shard_map/ppermute | solution.py:615
  59.9 18.3 %copy-start.6 = (bf16[1,2048,576]{1,2,0:T(8,128)(2,1)S(1)}, bf16[1,2048,576]{1,2,0:T(8,128)(2,1)}, u32[]{:S(2)}) copy-start(bf16[1,2048,576]{1,2,0:T(8,128)(2,1)} %param.9) | copy-start | bytes 7077892
  60.2 6.9 %collective-permute-start.19 = (bf16[208,512]{1,0:T(8,128)(2,1)S(1)}, bf16[208,512]{1,0:T(8,128)(2,1)S(1)}, u32[]{:S(2)}, u32[]{:S(2)}) collective-permute-start(bf16[208,512]{1,0:T(8,128)(2,1)S(1)} %get-tuple-element.170), channel_id=1, source_target_pairs={{2,0},{4,2},{6,4},{7,6},{5,7},{3,5},{1,3},{0,1},{10,8},{12,10},{14... | collective-permute-start | bytes 638984 | tf_op jit(solution)/shard_map/ppermute | solution.py:614
  61.0 6.5 %collective-permute-start.20 = (bf16[208,512]{1,0:T(8,128)(2,1)S(1)}, bf16[208,512]{1,0:T(8,128)(2,1)S(1)}, u32[]{:S(2)}, u32[]{:S(2)}) collective-permute-start(bf16[208,512]{1,0:T(8,128)(2,1)S(1)} %get-tuple-element.173), channel_id=1, source_target_pairs={{0,2},{2,4},{4,6},{6,7},{7,5},{5,3},{3,1},{1,0},{8,10},{10,12},{12... | collective-permute-start | bytes 638984 | tf_op jit(solution)/shard_map/ppermute | solution.py:615
  62.4 7.4 %collective-permute-start.23 = (bf16[80,512]{1,0:T(8,128)(2,1)S(1)}, bf16[80,512]{1,0:T(8,128)(2,1)S(1)}, u32[]{:S(2)}, u32[]{:S(2)}) collective-permute-start(bf16[80,512]{1,0:T(8,128)(2,1)S(1)} %get-tuple-element.186), channel_id=1, source_target_pairs={{2,0},{4,2},{6,4},{7,6},{5,7},{3,5},{1,3},{0,1},{10,8},{12,10},{14... | collective-permute-start | bytes 245768 | tf_op jit(solution)/shard_map/ppermute | solution.py:614
  63.2 6.6 %collective-permute-start.24 = (bf16[80,512]{1,0:T(8,128)(2,1)S(1)}, bf16[80,512]{1,0:T(8,128)(2,1)S(1)}, u32[]{:S(2)}, u32[]{:S(2)}) collective-permute-start(bf16[80,512]{1,0:T(8,128)(2,1)S(1)} %get-tuple-element.189), channel_id=1, source_target_pairs={{0,2},{2,4},{4,6},{6,7},{7,5},{5,3},{3,1},{1,0},{8,10},{10,12},{12... | collective-permute-start | bytes 245768 | tf_op jit(solution)/shard_map/ppermute | solution.py:615
  67.7 14.5 %collective-permute-start.21 = (bf16[208,512]{1,0:T(8,128)(2,1)S(1)}, bf16[208,512]{1,0:T(8,128)(2,1)S(1)}, u32[]{:S(2)}, u32[]{:S(2)}) collective-permute-start(bf16[208,512]{1,0:T(8,128)(2,1)S(1)} %get-tuple-element.176), channel_id=1, source_target_pairs={{2,0},{4,2},{6,4},{7,6},{5,7},{3,5},{1,3},{0,1},{10,8},{12,10},{14... | collective-permute-start | bytes 638984 | tf_op jit(solution)/shard_map/ppermute | solution.py:614
  69.2 13.0 %collective-permute-start.22 = (bf16[208,512]{1,0:T(8,128)(2,1)S(1)}, bf16[208,512]{1,0:T(8,128)(2,1)S(1)}, u32[]{:S(2)}, u32[]{:S(2)}) collective-permute-start(bf16[208,512]{1,0:T(8,128)(2,1)S(1)} %get-tuple-element.177), channel_id=1, source_target_pairs={{0,2},{2,4},{4,6},{6,7},{7,5},{5,3},{3,1},{1,0},{8,10},{10,12},{12... | collective-permute-start | bytes 638984 | tf_op jit(solution)/shard_map/ppermute | solution.py:615
  69.9 4.6 %collective-permute-start.25 = (bf16[80,512]{1,0:T(8,128)(2,1)S(1)}, bf16[80,512]{1,0:T(8,128)(2,1)S(1)}, u32[]{:S(2)}, u32[]{:S(2)}) collective-permute-start(bf16[80,512]{1,0:T(8,128)(2,1)S(1)} %get-tuple-element.192), channel_id=1, source_target_pairs={{2,0},{4,2},{6,4},{7,6},{5,7},{3,5},{1,3},{0,1},{10,8},{12,10},{14... | collective-permute-start | bytes 245768 | tf_op jit(solution)/shard_map/ppermute | solution.py:614
  71.4 4.5 %collective-permute-start.26 = (bf16[80,512]{1,0:T(8,128)(2,1)S(1)}, bf16[80,512]{1,0:T(8,128)(2,1)S(1)}, u32[]{:S(2)}, u32[]{:S(2)}) collective-permute-start(bf16[80,512]{1,0:T(8,128)(2,1)S(1)} %get-tuple-element.195), channel_id=1, source_target_pairs={{0,2},{2,4},{4,6},{6,7},{7,5},{5,3},{3,1},{1,0},{8,10},{10,12},{12... | collective-permute-start | bytes 245768 | tf_op jit(solution)/shard_map/ppermute | solution.py:615
  76.1 5.8 %collective-permute-start.27 = (bf16[80,512]{1,0:T(8,128)(2,1)S(1)}, bf16[80,512]{1,0:T(8,128)(2,1)S(1)}, u32[]{:S(2)}, u32[]{:S(2)}) collective-permute-start(bf16[80,512]{1,0:T(8,128)(2,1)S(1)} %get-tuple-element.198), channel_id=1, source_target_pairs={{2,0},{4,2},{6,4},{7,6},{5,7},{3,5},{1,3},{0,1},{10,8},{12,10},{14... | collective-permute-start | bytes 245768 | tf_op jit(solution)/shard_map/ppermute | solution.py:614
  77.7 4.5 %copy-start = (bf16[16,512,128]{2,1,0:T(8,128)(2,1)S(1)}, bf16[16,512,128]{2,1,0:T(8,128)(2,1)}, u32[]{:S(2)}) copy-start(bf16[16,512,128]{2,1,0:T(8,128)(2,1)} %refs_8_.1) | copy-start | bytes 6291460
  77.7 4.4 %collective-permute-start.28 = (bf16[80,512]{1,0:T(8,128)(2,1)S(1)}, bf16[80,512]{1,0:T(8,128)(2,1)S(1)}, u32[]{:S(2)}, u32[]{:S(2)}) collective-permute-start(bf16[80,512]{1,0:T(8,128)(2,1)S(1)} %get-tuple-element.199), channel_id=1, source_target_pairs={{0,2},{2,4},{4,6},{6,7},{7,5},{5,3},{3,1},{1,0},{8,10},{10,12},{12... | collective-permute-start | bytes 245768 | tf_op jit(solution)/shard_map/ppermute | solution.py:615

commit v4 on v3

--- a/solution.py
+++ b/solution.py
@@ -258,7 +258,9 @@
             out_shape.append(jax.ShapeDtypeStruct((8, rows // sections), jnp.float32))
     caches = len(cache_parts)
     if caches > 1:
-        cache_parts = [in_hbm(part) for part in cache_parts]
+        cache_parts = [
+            part if part.shape[0] < key_width else in_hbm(part) for part in cache_parts
+        ]
     operands = [info, *cache_parts, *queries] + ([fresh] if fresh_info else [])
     scratch = [
         pltpu.VMEM((total, length), jnp.float32),
@@ -271,7 +273,7 @@
         scratch.append(pltpu.VMEM((fresh.shape[0] * fresh.shape[1], key_width), jnp.float32))
     in_specs = (
         [whole(pltpu.SMEM)]
-        + [whole(pltpu.HBM if caches > 1 else pltpu.VMEM)] * caches
+        + [whole(pl.ANY if caches > 1 else pltpu.VMEM)] * caches
         + [whole()] * (len(operands) - 1 - caches)
     )
     out_specs = [whole()] * len(out_shape)
@@ -307,30 +309,55 @@
     return results + outs
 
 
+def load_kernel(start, stop, weight_ref, out_ref, sem):
+    copy = pltpu.make_async_copy(weight_ref.at[:, start:stop], out_ref, sem)
+    copy.start()
+    copy.wait()
+
+
+def load_alone(weight, start, stop):
+    return pl.pallas_call(
+        functools.partial(load_kernel, start, stop),
+        out_shape=pltpu.VMEM((weight.shape[0], stop - start), weight.dtype),
+        in_specs=[whole(pltpu.HBM)],
+        out_specs=whole(),
+        scratch_shapes=[pltpu.SemaphoreType.DMA],
+        compiler_params=pltpu.CompilerParams(vmem_limit_bytes=MIB),
+        cost_estimate=pl.CostEstimate(
+            flops=0, bytes_accessed=2 * weight.shape[0] * (stop - start), transcendentals=0
+        ),
+        name="load",
+    )(in_hbm(weight))
+
+
 def merge_kernel(covers, *refs):
     refs = list(refs)
     outs = refs[len(refs) - len(covers) :]
-    for cover, out_ref in zip(covers, outs):
-        packed_ref = refs.pop(0) if cover else None
+    for item, out_ref in zip(covers, outs):
+        packed_refs = [refs.pop(0) for _ in item]
         part_ref, stats_ref = refs.pop(0), refs.pop(0)
         rows = stats_ref.shape[1]
         merged = []
         for at in range(part_ref.shape[0] // rows):
-            piece = load_kept(part_ref, stats_ref, at)
-            if at in cover:
-                piece = combine(load_packed(packed_ref, rows, cover.index(at)), piece)
-            merged.append(piece)
+            pieces = [
+                load_packed(packed_ref, rows, cover.index(at))
+                for packed_ref, cover in zip(packed_refs, item)
+                if at in cover
+            ]
+            kept = load_kept(part_ref, stats_ref, at)
+            merged.append(combine(*pieces, kept) if pieces else kept)
         store_packed(out_ref, merged)
 
 
 def merge(items):
     operands, out_shape = [], []
-    for packed, cover, (part, stats) in items:
-        operands += ([packed] if cover else []) + [part, stats]
+    for packed, (part, stats) in items:
+        operands += [block for block, _ in packed] + [part, stats]
         shape = (part.shape[0] + EXTRA, part.shape[1])
         out_shape.append(jax.ShapeDtypeStruct(shape, jnp.bfloat16))
+    covers = tuple(tuple(cover for _, cover in packed) for packed, _ in items)
     return pl.pallas_call(
-        functools.partial(merge_kernel, tuple(cover for _, cover, _ in items)),
+        functools.partial(merge_kernel, covers),
         grid=(1,),
         out_shape=out_shape,
         in_specs=[pl.BlockSpec(operand.shape, lambda i: (0, 0)) for operand in operands],
@@ -396,7 +423,7 @@
     if share % 128 == 0:
         tile, shape = share, (parts, lines, share)
     else:
-        tile, shape = columns // 8, (lines, columns)
+        tile, shape = columns // 8 if columns % 1024 == 0 else columns, (lines, columns)
     out = pl.pallas_call(
         functools.partial(finish_kernel, len(chunk_parts), heads, tile),
         out_shape=jax.ShapeDtypeStruct(shape, jnp.bfloat16),
@@ -498,6 +525,15 @@
     return jnp.where(info[3] == info[2] ^ 2, across, corner)
 
 
+def tie(*trees):
+    leaves, structure = jax.tree.flatten(trees)
+    places = [at for at, leaf in enumerate(leaves) if isinstance(leaf, jax.Array)]
+    held = lax.optimization_barrier([leaves[at] for at in places])
+    for at, leaf in zip(places, held):
+        leaves[at] = leaf
+    return jax.tree.unflatten(structure, leaves)
+
+
 def blank(like):
     return pl.pallas_call(
         lambda out_ref: None,
@@ -506,11 +542,6 @@
         compiler_params=pltpu.CompilerParams(vmem_limit_bytes=MIB),
         name="blank",
     )()
-
-
-def tie(came, other):
-    values, other = lax.optimization_barrier(([value for value, _ in came], other))
-    return [(value, cover) for value, (_, cover) in zip(values, came)], other
 
 
 def body(cache, queries, new_latent, lengths, donor, value_up, out_proj):
@@ -552,21 +583,28 @@
         return found
 
     width = out_proj.shape[1]
-    quarter = width // 4 if width % 512 == 0 else width
+    unit = width // 8 if width % 1024 == 0 else width
+    loads = (2, 2)
     loaded = []
 
+    def load_next(units):
+        start = sum(piece.shape[1] for piece in loaded)
+        stop = min(start + units * unit, width)
+        return (out_proj, start, stop) if start < stop else None
+
+    def attend_more(kinds, pieces, units, *rest):
+        load = load_next(units)
+        results = attend(kinds, pieces, [cache_t], info, 0, latent, *rest, load=load)
+        if load:
+            loaded.append(results.pop())
+        return results
+
     def attend_early(hop):
-        pieces = pieces_of(hop, 0, cut)
         if hop == 0:
             return None
         kinds = ["ends"] if hop == reach else ["keep", "keep"]
-        start = (hop - 1) * quarter
-        if hop == reach or start >= width or hop > 2:
-            return attend(kinds, pieces, [cache_t], info, 0, latent)
-        load = (out_proj, start, start + quarter)
-        *results, piece = attend(kinds, pieces, [cache_t], info, 0, latent, load=load)
-        loaded.append(piece)
-        return results
+        units = loads[hop - 1] if hop <= len(loads) else 0
+        return attend_more(kinds, pieces_of(hop, 0, cut), units)
 
     early_parts = []
     for hop in range(1, reach + 1):
@@ -584,7 +622,7 @@
             extra = lax.cond(
                 crowded.reshape(()) != 0, exchange_all, lambda rows, _: blank(rows), cache_t, info
             )
-        came, extra, parts_now = lax.optimization_barrier((came, extra, attend_early(hop - 1)))
+        came, extra, parts_now = tie(came, extra, attend_early(hop - 1))
         if hop == 1 and four:
             far_half = plane_swap(extra)
         elif hop == 2 and four:
@@ -595,70 +633,63 @@
     early_parts.append(attend_early(reach))
 
     if four:
-        far_half, lefts[reach] = lax.optimization_barrier((far_half, lefts[reach]))
+        far_half, lefts[reach] = tie(far_half, lefts[reach])
         moved = [cache_t, beside, far_half, core_swap(far_half), spare]
     else:
         shards = lax.all_gather(cache_t, "grp", axis=0, tiled=False)
         found = lax.dynamic_index_in_dim(shards, info[3], 0, keepdims=False)
         moved = [found, found, found[: key_width // 2], found[key_width // 2 :], found]
-    *late_ends, moved_rows = attend(["ends"], pieces_of(reach, cut, rows), moved, info, 1, latent)
-
-    def start_back(ends):
-        ends = ends[0]
-        sections = tuple(range(len(ends)))
-        return [(ends[0], (0,)), (ends[1], (1,)) if len(ends) > 1 else (None, ())], sections
+    near = reach - 1
+    late_ends, *late_near, moved_rows = attend(
+        ["ends", "keep", "keep"],
+        pieces_of(reach, cut, rows) + pieces_of(near, cut, rows),
+        moved,
+        info,
+        1,
+        latent,
+    )
+
+    sections = tuple(range(sections_of(cut)))
+    late_sections = tuple(range(sections_of(rows - cut)))
 
     def hop_back(going):
-        (to_the_left, cover_left), (to_the_right, cover_right) = going
         return [
-            (left(to_the_left), cover_left),
-            (right(to_the_right) if cover_right else None, cover_right),
+            [(send(block), cover) for block, cover in items]
+            for send, items in zip((left, right), going)
         ]
 
     def merge_back(came, kept, sections):
-        merged = merge([(*item, block) for item, block in zip(came, kept)])
-        return [(block, sections) for block in merged]
-
-    early_going, sections = start_back(early_parts[reach])
-    early_came = hop_back(early_going)
-    early_came, late_ends = tie(early_came, late_ends)
-    late_going, late_sections = start_back(late_ends)
+        return [[(block, sections)] for block in merge(list(zip(came, kept)))]
+
+    def ends_back(ends):
+        return [[(ends[0], (0,))], [(ends[1], (1,))] if len(ends) > 1 else []]
+
+    early_came = hop_back(ends_back(early_parts[reach][0]))
+    early_came, late_ends, late_near = tie(early_came, late_ends, late_near)
+    late_came = hop_back(ends_back(late_ends))
+    early_came = hop_back(merge_back(early_came, early_parts[near], sections))
     kinds, pieces = ["own"], pieces_of(0, cut, rows)
-    for hop in range(1, reach):
+    for hop in range(1, near):
         kinds += ["keep", "keep"]
         pieces += pieces_of(hop, cut, rows)
-
-    def load_more(limit):
-        start = quarter * len(loaded)
-        stop = min(start + quarter, width) if limit else width
-        return (out_proj, start, stop) if start < width else None
-
-    load = load_more(True)
-    results = attend(
-        kinds, pieces, [moved_rows], info, 1, latent, fresh, (HANDOVER, heads), load
-    )
+    results = attend(kinds, pieces, [moved_rows], info, 1, latent, fresh, (HANDOVER, heads))
+    late_came, results = tie(late_came, results)
+    late_came = hop_back(merge_back(late_came, late_near, late_sections))
+    early_came, late_came = tie(early_came, late_came)
+
+    early_parts[0] = attend_more(["own"], pieces_of(0, 0, cut), 0, fresh, (0, heads))
+    late_parts = [[results[0]]]
+    for hop in range(1, near):
+        late_parts.append(results[2 * hop - 1 : 2 * hop + 1])
+    for hop in range(near - 1, 0, -1):
+        early_came = hop_back(merge_back(early_came, early_parts[hop], sections))
+        late_came = hop_back(merge_back(late_came, late_parts[hop], late_sections))
+        early_came, late_came, early_parts[0] = tie(early_came, late_came, early_parts[0])
+    load = load_next(8)
     if load:
-        loaded.append(results.pop())
-    load = load_more(False)
-    early_parts[0] = attend(
-        ["own"], pieces_of(0, 0, cut), [cache_t], info, 0, latent, fresh, (0, heads), load
-    )
-    if load:
-        loaded.append(early_parts[0].pop())
-    late_came = hop_back(late_going)
-    for hop in range(reach - 1, 0, -1):
-        early_came = hop_back(merge_back(early_came, early_parts[hop], sections))
-        if hop == reach - 1:
-            values = [value for value, _ in late_came]
-            early_came, (results, values) = tie(early_came, (results, values))
-            late_came = [(value, cover) for value, (_, cover) in zip(values, late_came)]
-    late_parts = [[results[0]]]
-    for hop in range(1, reach):
-        late_parts.append(results[2 * hop - 1 : 2 * hop + 1])
-    for hop in range(reach - 1, 0, -1):
-        late_came = hop_back(merge_back(late_came, late_parts[hop], late_sections))
+        loaded.append(load_alone(*load))
     finals = [
-        (came[0][0], came[1][0], own[0])
+        (came[0][0][0], came[1][0][0], own[0])
         for came, own in ((early_came, early_parts[0]), (late_came, late_parts[0]))
     ]
 

time: 100 us -> 98.1 us (0.981)
  blocking collectives: 12.5 us -> 10.4 us
  Pallas kernels: 40.4 us -> 41.7 us
    pallas_call x6 -> x7, Pallas kernels: 0.99 us -> 6.17 us  [the longest x1 5.18 us: load_alone(): pl.pallas_call(functools.partial(load_kernel, start, stop), out_shape=plt...]
    pallas_call x7, Pallas kernels: 31.9 us -> 28.1 us  [attend(): pl.pallas_call(functools.partial(attend_kernel, tuple(kinds), rows, takes...]
    all_to_all x1, blocking collectives: 12.5 us -> 10.4 us  [body(): lax.all_to_all(term, 'ctx', split_axis=0, concat_axis=0, tiled=True)]
    ppermute x6, waiting for transfers between devices: 5.85 us -> 4.42 us  [body(): came = (right(lefts[-1]), left(rights[-1]))]
    unnamed x18 -> x16, local copies, waits for them, and re-layouts: 3.73 us -> 2.74 us
  transfers between devices with their start and end apart: 27 -> 27, of which waited for: 11 -> 11; matrix products, arithmetic and copies ran while one was open for 0% -> 0% of each run, Pallas kernels for 36% -> 38%
where the time goes in v4:
time: 98.1 us; the launch traced here: 97.7 us
  Pallas kernels  41.7 us (43%)
  starting transfers between devices  27.4 us (28%)
  waiting for transfers between devices  13.9 us (14%)
  blocking collectives  10.4 us (11%)
  local copies, waits for them, and re-layouts  3.39 us (3%)
    pallas_call x7, Pallas kernels, attend(): pl.pallas_call(functools.partial(attend_kernel, tuple(kinds), rows, takes...  28.1 us
    ppermute x16, starting transfers between devices, hop_back(): send(block)  16.6 us
    all_to_all x1, blocking collectives, body(): lax.all_to_all(term, 'ctx', split_axis=0, concat_axis=0, tiled=True)  10.4 us
    ppermute x16, waiting for transfers between devices, hop_back(): send(block)  7.56 us
    ppermute x6, starting transfers between devices, body(): came = (right(lefts[-1]), left(rights[-1]))  6.73 us
    pallas_call x1, Pallas kernels, load_alone(): pl.pallas_call(functools.partial(load_kernel, start, stop), out_shape=plt...  5.18 us
    pallas_call x1, Pallas kernels, finish(): pl.pallas_call(functools.partial(finish_kernel, len(chunk_parts), heads,...  4.48 us
    ppermute x6, waiting for transfers between devices, body(): came = (right(lefts[-1]), left(rights[-1]))  4.42 us
  transfers between devices with their start and end apart: 27, of which 11 were waited for; matrix products, arithmetic and copies ran while one was open for 0% of the time, Pallas kernels for 38%

profile of v4, /device:TPU:0, one launch (start us, length us, event | category | flops | bytes accessed | tf_op | source)
XLA Modules:
  0.0 97.7 jit_solution(610405782340650265)
XLA Ops:
  0.0 0.5 collective-permute-start.4
  0.5 2.5 %collective-permute-start.3 = (bf16[256,576]{1,0:T(8,128)(2,1)}, bf16[256,576]{1,0:T(8,128)(2,1)S(1)}, u32[]{:S(2)}, u32[]{:S(2)}) collective-permute-start(bf16[256,576]{1,0:T(8,128)(2,1)} %bitcast.9), channel_id=1, source_target_pairs={{2,0},{4,2},{6,4},{7,6},{5,7},{3,5},{1,3},{0,1},{10,8},{12,10},{14... | collective-permute-start | bytes 884744 | tf_op jit(solution)/shard_map/ppermute | solution.py:612
  3.1 0.7 copy-done.1
  3.7 0.7 copy-done.2
  4.4 1.2 %plan.1 = (s32[6]{0:T(128)S(1)}, s32[1]{0:T(128)}) custom-call(s32[1]{0:T(128)} %bitcast.1.group_ref, s32[1]{0:T(128)} %bitcast.2.place_ref, s32[4]{0:T(128)S(1)} %copy-done.1, s32[4]{0:T(128)S(1)} %copy-done.2), custom_call_target="tpu_custom_call" | custom-call | tf_op jit(solution)/shard_map/plan/pallas_call | solution.py:472
  5.6 1.4 %copy-done.7 = bf16[576,2048]{1,0:T(8,128)(2,1)} copy-done((bf16[576,2048]{1,0:T(8,128)(2,1)}, bf16[576,2048]{1,0:T(8,128)(2,1)S(1)}, u32[]{:S(2)}) %copy-start.7) | copy-done | bytes 2359320
  7.0 1.8 %offer.1 = bf16[288,2048]{1,0:T(8,128)(2,1)S(1)} custom-call(s32[6]{0:T(128)S(1)} %get-tuple-element.122.info_ref.refs_0_, bf16[576,2048]{1,0:T(8,128)(2,1)} %bitcast.16, bf16[576,2048]{1,0:T(8,128)(2,1)} %copy-done.7), custom_call_target="tpu_custom_call" | custom-call | bytes 2097152 | tf_op jit(solution)/shard_map/offer/pallas_call | solution.py:506
  8.8 2.8 %collective-permute-done.3.refs_3_.refs_4_ = bf16[256,576]{1,0:T(8,128)(2,1)S(1)} collective-permute-done((bf16[256,576]{1,0:T(8,128)(2,1)}, bf16[256,576]{1,0:T(8,128)(2,1)S(1)}, u32[]{:S(2)}, u32[]{:S(2)}) %collective-permute-start.3) | collective-permute-done | bytes 294944 | tf_op jit(solution)/shard_map/ppermute | solution.py:612
  11.6 1.4 %collective-permute-done.2.refs_2_.refs_3_ = bf16[256,576]{1,0:T(8,128)(2,1)S(1)} collective-permute-done((bf16[256,576]{1,0:T(8,128)(2,1)}, bf16[256,576]{1,0:T(8,128)(2,1)S(1)}, u32[]{:S(2)}, u32[]{:S(2)}) %collective-permute-start.2) | collective-permute-done | bytes 294944 | tf_op jit(solution)/shard_map/ppermute | solution.py:612
  13.0 1.5 %collective-permute-start.13 = (bf16[288,2048]{1,0:T(8,128)(2,1)S(1)}, bf16[288,2048]{1,0:T(8,128)(2,1)S(1)}, u32[]{:S(2)}, u32[]{:S(2)}) collective-permute-start(bf16[288,2048]{1,0:T(8,128)(2,1)S(1)} %offer.1), channel_id=1, source_target_pairs={{0,16},{8,24},{16,0},{24,8},{1,17},{9,25},{17,1},{25,9},{2,18},{10... | collective-permute-start | bytes 3538952 | tf_op jit(solution)/shard_map/ppermute | solution.py:627
  14.5 0.5 collective-permute-start.5
  15.1 1.5 %collective-permute-start.6 = (bf16[256,576]{1,0:T(8,128)(2,1)S(1)}, bf16[256,576]{1,0:T(8,128)(2,1)}, u32[]{:S(2)}, u32[]{:S(2)}) collective-permute-start(bf16[256,576]{1,0:T(8,128)(2,1)S(1)} %collective-permute-done.3.refs_3_.refs_4_), channel_id=1, source_target_pairs={{2,0},{4,2},{6,4},{7,6},{5,7},{3,5},{1,3},{0,1},{10,8},{12,10},{14... | collective-permute-start | bytes 884744 | tf_op jit(solution)/shard_map/ppermute | solution.py:612
  17.1 6.9 %attend_keep_keep.3 = (f32[192,512]{1,0:T(8,128)S(1)}, f32[8,96]{1,0:T(8,128)S(1)}, f32[192,512]{1,0:T(8,128)S(1)}, f32[8,96]{1,0:T(8,128)S(1)}, bf16[2048,1792]{1,0:T(8,128)(2,1)S(1)}) custom-call(s32[6]{0:T(128)S(1)} %get-tuple-element.122.info_ref.refs_0_, bf16[576,2048]{1,0:T(8,128)(2,1)} %bitcast.18, ...), custom_call_target="tpu_custom_call" | custom-call | flops 1711276032 | bytes 4194304 | tf_op jit(solution)/shard_map/attend_keep_keep/pallas_call | solution.py:289
  24.1 1.2 %collective-permute-start.7 = (bf16[256,576]{1,0:T(8,128)(2,1)S(1)}, bf16[256,576]{1,0:T(8,128)(2,1)S(1)}, u32[]{:S(2)}, u32[]{:S(2)}) collective-permute-start(bf16[256,576]{1,0:T(8,128)(2,1)S(1)} %collective-permute-done.5.refs_2_.refs_5_), channel_id=1, source_target_pairs={{0,2},{2,4},{4,6},{6,7},{7,5},{5,3},{3,1},{1,0},{8,10},{10,12},{12... | collective-permute-start | bytes 884744 | tf_op jit(solution)/shard_map/ppermute | solution.py:612
  25.4 0.8 collective-permute-start.8
  26.2 6.5 %attend_keep_keep.4 = (f32[192,512]{1,0:T(8,128)S(1)}, f32[8,96]{1,0:T(8,128)S(1)}, f32[192,512]{1,0:T(8,128)S(1)}, f32[8,96]{1,0:T(8,128)S(1)}, bf16[2048,1792]{1,0:T(8,128)(2,1)S(1)}) custom-call(s32[6]{0:T(128)S(1)} %get-tuple-element.122.info_ref.refs_0_, bf16[576,2048]{1,0:T(8,128)(2,1)S(1)} %bitcast.20, ...), custom_call_target="tpu_custom_call" | custom-call | flops 1711276032 | bytes 4194304 | tf_op jit(solution)/shard_map/attend_keep_keep/pallas_call | solution.py:289
  33.0 1.4 %collective-permute-start.10 = (bf16[128,576]{1,0:T(8,128)(2,1)S(1)}, bf16[128,576]{1,0:T(8,128)(2,1)S(1)}, u32[]{:S(2)}, u32[]{:S(2)}) collective-permute-start(bf16[128,576]{1,0:T(8,128)(2,1)S(1)} %slice.13), channel_id=1, source_target_pairs={{2,0},{4,2},{6,4},{7,6},{5,7},{3,5},{1,3},{0,1},{10,8},{12,10},{14... | collective-permute-start | bytes 442376 | tf_op jit(solution)/shard_map/ppermute | solution.py:616
  34.4 0.7 collective-permute-start.9
  35.1 3.2 %attend_keep_keep.5 = (f32[192,512]{1,0:T(8,128)S(1)}, f32[8,96]{1,0:T(8,128)S(1)}, f32[192,512]{1,0:T(8,128)S(1)}, f32[8,96]{1,0:T(8,128)S(1)}) custom-call(s32[6]{0:T(128)S(1)} %get-tuple-element.122.info_ref.refs_0_, bf16[576,2048]{1,0:T(8,128)(2,1)S(1)} %bitcast.21, bf16[256,576]{1,0:T(8,128)(2,1)S(1)} %collective-permute-done.7.refs_2_.refs_7_, ...), custom_call_target="tpu_custom_call" | custom-call | flops 1711276032 | bytes 4194304 | tf_op jit(solution)/shard_map/attend_keep_keep/pallas_call | solution.py:289
  38.4 1.4 %collective-permute-done.9.refs_2_ = bf16[128,576]{1,0:T(8,128)(2,1)S(1)} collective-permute-done((bf16[128,576]{1,0:T(8,128)(2,1)S(1)}, bf16[128,576]{1,0:T(8,128)(2,1)S(1)}, u32[]{:S(2)}, u32[]{:S(2)}) %collective-permute-start.9) | collective-permute-done | bytes 147488 | tf_op jit(solution)/shard_map/ppermute | solution.py:615
  39.7 0.5 collective-permute-done.13.refs_3_
  40.3 2.3 %attend_ends.1 = (bf16[112,512]{1,0:T(8,128)(2,1)S(1)}, bf16[112,512]{1,0:T(8,128)(2,1)S(1)}) custom-call(s32[6]{0:T(128)S(1)} %get-tuple-element.122.info_ref.refs_0_, bf16[576,2048]{1,0:T(8,128)(2,1)S(1)} %bitcast.22, bf16[128,576]{1,0:T(8,128)(2,1)S(1)} %collective-permute-done.9.refs_2_, bf16[128,576]{1,0:T(8,128)(2,1)S(1)} %collective-permute-done.10.refs_3_.refs_6_), custom_call_target="tpu_custom_call" | custom-call | flops 855638016 | bytes 4194304 | tf_op jit(solution)/shard_map/attend_ends/pallas_call | solution.py:289
  42.6 1.6 %collective-permute-start.11 = (bf16[112,512]{1,0:T(8,128)(2,1)S(1)}, bf16[112,512]{1,0:T(8,128)(2,1)S(1)}, u32[]{:S(2)}, u32[]{:S(2)}) collective-permute-start(bf16[112,512]{1,0:T(8,128)(2,1)S(1)} %get-tuple-element.144), channel_id=1, source_target_pairs={{2,0},{4,2},{6,4},{7,6},{5,7},{3,5},{1,3},{0,1},{10,8},{12,10},{14... | collective-permute-start | bytes 344072 | tf_op jit(solution)/shard_map/ppermute | solution.py:657
  44.6 2.8 %attend_ends_keep_keep.1 = (bf16[48,512]{1,0:T(8,128)(2,1)S(1)}, bf16[48,512]{1,0:T(8,128)(2,1)S(1)}, f32[64,512]{1,0:T(8,128)S(1)}, f32[8,32]{1,0:T(8,128)S(1)}...) custom-call(s32[6]{0:T(128)S(1)} %get-tuple-element.122.info_ref.refs_0_, ...), custom_call_target="tpu_custom_call" | custom-call | flops 855638016 | bytes 4194304 | tf_op jit(solution)/shard_map/attend_ends_keep_keep/pallas_call | solution.py:289
  47.4 0.7 collective-permute-done.11.refs_0_
  48.2 1.3 %collective-permute-done.12.refs_3_ = bf16[112,512]{1,0:T(8,128)(2,1)S(1)} collective-permute-done((bf16[112,512]{1,0:T(8,128)(2,1)S(1)}, bf16[112,512]{1,0:T(8,128)(2,1)S(1)}, u32[]{:S(2)}, u32[]{:S(2)}) %collective-permute-start.12) | collective-permute-done | bytes 114720 | tf_op jit(solution)/shard_map/ppermute | solution.py:657
  49.5 1.6 %collective-permute-start.17 = (bf16[48,512]{1,0:T(8,128)(2,1)S(1)}, bf16[48,512]{1,0:T(8,128)(2,1)S(1)}, u32[]{:S(2)}, u32[]{:S(2)}) collective-permute-start(bf16[48,512]{1,0:T(8,128)(2,1)S(1)} %get-tuple-element.163), channel_id=1, source_target_pairs={{2,0},{4,2},{6,4},{7,6},{5,7},{3,5},{1,3},{0,1},{10,8},{12,10},{14... | collective-permute-start | bytes 147464 | tf_op jit(solution)/shard_map/ppermute | solution.py:657
  51.0 0.4 collective-permute-start.18
  51.7 1.6 %collective-permute-start.15 = (bf16[208,512]{1,0:T(8,128)(2,1)S(1)}, bf16[208,512]{1,0:T(8,128)(2,1)S(1)}, u32[]{:S(2)}, u32[]{:S(2)}) collective-permute-start(bf16[208,512]{1,0:T(8,128)(2,1)S(1)} %get-tuple-element.161), channel_id=1, source_target_pairs={{2,0},{4,2},{6,4},{7,6},{5,7},{3,5},{1,3},{0,1},{10,8},{12,10},{14... | collective-permute-start | bytes 638984 | tf_op jit(solution)/shard_map/ppermute | solution.py:657
  53.3 0.4 collective-permute-start.16
  53.7 3.5 %attend_own_keep_keep_keep_keep.1 = (f32[64,512]{1,0:T(8,128)S(1)}, f32[8,32]{1,0:T(8,128)S(1)}, f32[64,512]{1,0:T(8,128)S(1)}, f32[8,32]{1,0:T(8,128)S(1)}, f32...) custom-call(s32[6]{0:T(128)S(1)} %get-tuple-element.122.info_ref.ref, ...), custom_call_target="tpu_custom_call" | custom-call | flops 1426063360 | bytes 4194304 | tf_op jit(solution)/shard_map/attend_own_keep_keep_keep_keep/pallas_call | solution.py:289
  57.4 1.6 %collective-permute-start.19 = (bf16[80,512]{1,0:T(8,128)(2,1)S(1)}, bf16[80,512]{1,0:T(8,128)(2,1)S(1)}, u32[]{:S(2)}, u32[]{:S(2)}) collective-permute-start(bf16[80,512]{1,0:T(8,128)(2,1)S(1)} %get-tuple-element.182), channel_id=1, source_target_pairs={{2,0},{4,2},{6,4},{7,6},{5,7},{3,5},{1,3},{0,1},{10,8},{12,10},{14... | collective-permute-start | bytes 245768 | tf_op jit(solution)/shard_map/ppermute | solution.py:657
  59.1 0.4 collective-permute-start.20
  59.5 2.4 %collective-permute-done.19.refs_0_ = bf16[80,512]{1,0:T(8,128)(2,1)S(1)} collective-permute-done((bf16[80,512]{1,0:T(8,128)(2,1)S(1)}, bf16[80,512]{1,0:T(8,128)(2,1)S(1)}, u32[]{:S(2)}, u32[]{:S(2)}) %collective-permute-start.19) | collective-permute-done | bytes 81952 | tf_op jit(solution)/shard_map/ppermute | solution.py:657
  61.9 1.6 %collective-permute-done.20.refs_3_ = bf16[80,512]{1,0:T(8,128)(2,1)S(1)} collective-permute-done((bf16[80,512]{1,0:T(8,128)(2,1)S(1)}, bf16[80,512]{1,0:T(8,128)(2,1)S(1)}, u32[]{:S(2)}, u32[]{:S(2)}) %collective-permute-start.20) | collective-permute-done | bytes 81952 | tf_op jit(solution)/shard_map/ppermute | solution.py:657
  63.7 1.6 %collective-permute-start.21 = (bf16[208,512]{1,0:T(8,128)(2,1)S(1)}, bf16[208,512]{1,0:T(8,128)(2,1)S(1)}, u32[]{:S(2)}, u32[]{:S(2)}) collective-permute-start(bf16[208,512]{1,0:T(8,128)(2,1)S(1)} %get-tuple-element.190), channel_id=1, source_target_pairs={{2,0},{4,2},{6,4},{7,6},{5,7},{3,5},{1,3},{0,1},{10,8},{12,10},{14... | collective-permute-start | bytes 638984 | tf_op jit(solution)/shard_map/ppermute | solution.py:657
  66.0 1.6 %collective-permute-start.23 = (bf16[80,512]{1,0:T(8,128)(2,1)S(1)}, bf16[80,512]{1,0:T(8,128)(2,1)S(1)}, u32[]{:S(2)}, u32[]{:S(2)}) collective-permute-start(bf16[80,512]{1,0:T(8,128)(2,1)S(1)} %get-tuple-element.198), channel_id=1, source_target_pairs={{2,0},{4,2},{6,4},{7,6},{5,7},{3,5},{1,3},{0,1},{10,8},{12,10},{14... | collective-permute-start | bytes 245768 | tf_op jit(solution)/shard_map/ppermute | solution.py:657
  67.6 0.4 collective-permute-start.24
  68.0 2.8 %attend_own.1 = (f32[192,512]{1,0:T(8,128)S(1)}, f32[8,96]{1,0:T(8,128)S(1)}) custom-call(s32[6]{0:T(128)S(1)} %get-tuple-element.122.info_ref.refs_0_, bf16[576,2048]{1,0:T(8,128)(2,1)S(1)} %bitcast.23, bf16[256,576]{1,0:T(8,128)(2,1)S(1)} %bitcast.12, bf16[4,4,576]{2,1,0:T(4,128)(2,1)S(1)} %bitcast.14), custom_call_target="tpu_custom_call" | custom-call | flops 855638016 | bytes 4194304 | tf_op jit(solution)/shard_map/attend_own/pallas_call | solution.py:289
  70.9 1.5 %collective-permute-done.24.refs_3_ = bf16[80,512]{1,0:T(8,128)(2,1)S(1)} collective-permute-done((bf16[80,512]{1,0:T(8,128)(2,1)S(1)}, bf16[80,512]{1,0:T(8,128)(2,1)S(1)}, u32[]{:S(2)}, u32[]{:S(2)}) %collective-permute-start.24) | collective-permute-done | bytes 81952 | tf_op jit(solution)/shard_map/ppermute | solution.py:657
  72.6 0.7 collective-permute-start.25
  73.3 1.4 %collective-permute-start.26 = (bf16[208,512]{1,0:T(8,128)(2,1)S(1)}, bf16[208,512]{1,0:T(8,128)(2,1)S(1)}, u32[]{:S(2)}, u32[]{:S(2)}) collective-permute-start(bf16[208,512]{1,0:T(8,128)(2,1)S(1)} %get-tuple-element.209), channel_id=1, source_target_pairs={{0,2},{2,4},{4,6},{6,7},{7,5},{5,3},{3,1},{1,0},{8,10},{10,12},{12... | collective-permute-start | bytes 638984 | tf_op jit(solution)/shard_map/ppermute | solution.py:657
  74.8 0.7 collective-permute-start.27
  75.5 1.4 %collective-permute-start.28 = (bf16[80,512]{1,0:T(8,128)(2,1)S(1)}, bf16[80,512]{1,0:T(8,128)(2,1)S(1)}, u32[]{:S(2)}, u32[]{:S(2)}) collective-permute-start(bf16[80,512]{1,0:T(8,128)(2,1)S(1)} %get-tuple-element.217), channel_id=1, source_target_pairs={{0,2},{2,4},{4,6},{6,7},{7,5},{5,3},{3,1},{1,0},{8,10},{10,12},{12... | collective-permute-start | bytes 245768 | tf_op jit(solution)/shard_map/ppermute | solution.py:657
  76.9 5.2 %load.1.refs_11_ = bf16[2048,3584]{1,0:T(8,128)(2,1)S(1)} custom-call(bf16[2048,7168]{1,0:T(8,128)(2,1)} %weight_ref.1), custom_call_target="tpu_custom_call" | custom-call | bytes 14680064 | tf_op jit(solution)/shard_map/load/pallas_call | solution.py:319
  82.2 4.5 %finish.1 = bf16[8,16,896]{2,1,0:T(8,128)(2,1)S(1)} custom-call(bf16[208,512]{1,0:T(8,128)(2,1)S(1)} %collective-permute-done.25.refs_0_, bf16[208,512]{1,0:T(8,128)(2,1)S(1)} %collective-permute-done.26.refs_1_, f32[192,512]{1,0:T(8,128)S(1)} %get-tuple-element.222.refs_2_, f32[8,96]{1,0:T(8,128)S(1)} %get-tuple-element.223.refs_3_, ...), custom_call_target="tpu_custom_call" | custom-call | flops 469762048 | bytes 29360128 | tf_op jit(solution)/shard_map/finish/pallas_call | solution.py:427
  86.6 10.4 %all_to_all.5 = bf16[8,16,896]{2,1,0:T(8,128)(2,1)S(1)} all-to-all(bf16[8,16,896]{2,1,0:T(8,128)(2,1)S(1)} %finish.1), channel_id=1, replica_groups=mesh['grp'=4,'ctx'=8] {'ctx'}, dimensions={0} | all-to-all | bytes 458752 | tf_op jit(solution)/shard_map/all_to_all | solution.py:697
  97.1 0.6 reshape.27
  (46 shorter events, 2.5 us)
Async XLA Ops:
  0.0 5.6 %collective-permute-start.4 = (bf16[576,2048]{1,0:T(8,128)(2,1)}, bf16[576,2048]{1,0:T(8,128)(2,1)S(1)}, u32[]{:S(2)}, u32[]{:S(2)}) collective-permute-start(bf16[576,2048]{1,0:T(8,128)(2,1)} %bitcast.15), channel_id=1, source_target_pairs={{0,8},{8,0},{16,24},{24,16},{1,9},{9,1},{17,25},{25,17},{2,10},{10... | collective-permute-start | bytes 7077896 | tf_op jit(solution)/shard_map/ppermute | solution.py:569
  0.5 11.2 %collective-permute-start.3 = (bf16[256,576]{1,0:T(8,128)(2,1)}, bf16[256,576]{1,0:T(8,128)(2,1)S(1)}, u32[]{:S(2)}, u32[]{:S(2)}) collective-permute-start(bf16[256,576]{1,0:T(8,128)(2,1)} %bitcast.9), channel_id=1, source_target_pairs={{2,0},{4,2},{6,4},{7,6},{5,7},{3,5},{1,3},{0,1},{10,8},{12,10},{14... | collective-permute-start | bytes 884744 | tf_op jit(solution)/shard_map/ppermute | solution.py:612
  2.9 10.1 %collective-permute-start.2 = (bf16[256,576]{1,0:T(8,128)(2,1)}, bf16[256,576]{1,0:T(8,128)(2,1)S(1)}, u32[]{:S(2)}, u32[]{:S(2)}) collective-permute-start(bf16[256,576]{1,0:T(8,128)(2,1)} %bitcast.10), channel_id=1, source_target_pairs={{0,2},{2,4},{4,6},{6,7},{7,5},{5,3},{3,1},{1,0},{8,10},{10,12},{12... | collective-permute-start | bytes 884744 | tf_op jit(solution)/shard_map/ppermute | solution.py:612
  3.1 0.7 copy-start.1
  3.7 0.7 copy-start.2
  5.6 1.4 %copy-start.7 = (bf16[576,2048]{1,0:T(8,128)(2,1)}, bf16[576,2048]{1,0:T(8,128)(2,1)S(1)}, u32[]{:S(2)}) copy-start(bf16[576,2048]{1,0:T(8,128)(2,1)S(1)} %collective-permute-done.4.beside_ref.refs_2_) | copy-start | bytes 7077892
  13.0 27.3 %collective-permute-start.13 = (bf16[288,2048]{1,0:T(8,128)(2,1)S(1)}, bf16[288,2048]{1,0:T(8,128)(2,1)S(1)}, u32[]{:S(2)}, u32[]{:S(2)}) collective-permute-start(bf16[288,2048]{1,0:T(8,128)(2,1)S(1)} %offer.1), channel_id=1, source_target_pairs={{0,16},{8,24},{16,0},{24,8},{1,17},{9,25},{17,1},{25,9},{2,18},{10... | collective-permute-start | bytes 3538952 | tf_op jit(solution)/shard_map/ppermute | solution.py:627
  14.5 9.6 %collective-permute-start.5 = (bf16[256,576]{1,0:T(8,128)(2,1)S(1)}, bf16[256,576]{1,0:T(8,128)(2,1)S(1)}, u32[]{:S(2)}, u32[]{:S(2)}) collective-permute-start(bf16[256,576]{1,0:T(8,128)(2,1)S(1)} %collective-permute-done.2.refs_2_.refs_3_), channel_id=1, source_target_pairs={{0,2},{2,4},{4,6},{6,7},{7,5},{5,3},{3,1},{1,0},{8,10},{10,12},{12... | collective-permute-start | bytes 884744 | tf_op jit(solution)/shard_map/ppermute | solution.py:612
  15.1 9.1 %collective-permute-start.6 = (bf16[256,576]{1,0:T(8,128)(2,1)S(1)}, bf16[256,576]{1,0:T(8,128)(2,1)}, u32[]{:S(2)}, u32[]{:S(2)}) collective-permute-start(bf16[256,576]{1,0:T(8,128)(2,1)S(1)} %collective-permute-done.3.refs_3_.refs_4_), channel_id=1, source_target_pairs={{2,0},{4,2},{6,4},{7,6},{5,7},{3,5},{1,3},{0,1},{10,8},{12,10},{14... | collective-permute-start | bytes 884744 | tf_op jit(solution)/shard_map/ppermute | solution.py:612
  17.1 9.1 %copy-start.5 = (bf16[1,2048,576]{1,2,0:T(8,128)(2,1)S(1)}, bf16[1,2048,576]{1,2,0:T(8,128)(2,1)}, u32[]{:S(2)}) copy-start(bf16[1,2048,576]{1,2,0:T(8,128)(2,1)} %param.9) | copy-start | bytes 7077892
  24.1 8.6 %collective-permute-start.7 = (bf16[256,576]{1,0:T(8,128)(2,1)S(1)}, bf16[256,576]{1,0:T(8,128)(2,1)S(1)}, u32[]{:S(2)}, u32[]{:S(2)}) collective-permute-start(bf16[256,576]{1,0:T(8,128)(2,1)S(1)} %collective-permute-done.5.refs_2_.refs_5_), channel_id=1, source_target_pairs={{0,2},{2,4},{4,6},{6,7},{7,5},{5,3},{3,1},{1,0},{8,10},{10,12},{12... | collective-permute-start | bytes 884744 | tf_op jit(solution)/shard_map/ppermute | solution.py:612
  25.4 7.6 %collective-permute-start.8 = (bf16[256,576]{1,0:T(8,128)(2,1)}, bf16[256,576]{1,0:T(8,128)(2,1)S(1)}, u32[]{:S(2)}, u32[]{:S(2)}) collective-permute-start(bf16[256,576]{1,0:T(8,128)(2,1)} %collective-permute-done.6.refs_3_.refs_6_), channel_id=1, source_target_pairs={{2,0},{4,2},{6,4},{7,6},{5,7},{3,5},{1,3},{0,1},{10,8},{12,10},{14... | collective-permute-start | bytes 884744 | tf_op jit(solution)/shard_map/ppermute | solution.py:612
  33.0 5.4 %collective-permute-start.10 = (bf16[128,576]{1,0:T(8,128)(2,1)S(1)}, bf16[128,576]{1,0:T(8,128)(2,1)S(1)}, u32[]{:S(2)}, u32[]{:S(2)}) collective-permute-start(bf16[128,576]{1,0:T(8,128)(2,1)S(1)} %slice.13), channel_id=1, source_target_pairs={{2,0},{4,2},{6,4},{7,6},{5,7},{3,5},{1,3},{0,1},{10,8},{12,10},{14... | collective-permute-start | bytes 442376 | tf_op jit(solution)/shard_map/ppermute | solution.py:616
  34.4 5.3 %collective-permute-start.9 = (bf16[128,576]{1,0:T(8,128)(2,1)S(1)}, bf16[128,576]{1,0:T(8,128)(2,1)S(1)}, u32[]{:S(2)}, u32[]{:S(2)}) collective-permute-start(bf16[128,576]{1,0:T(8,128)(2,1)S(1)} %slice.12), channel_id=1, source_target_pairs={{0,2},{2,4},{4,6},{6,7},{7,5},{5,3},{3,1},{1,0},{8,10},{10,12},{12... | collective-permute-start | bytes 442376 | tf_op jit(solution)/shard_map/ppermute | solution.py:615
  40.3 4.4 %collective-permute-start.14 = (bf16[288,2048]{1,0:T(8,128)(2,1)S(1)}, bf16[288,2048]{1,0:T(8,128)(2,1)S(1)}, u32[]{:S(2)}, u32[]{:S(2)}) collective-permute-start(bf16[288,2048]{1,0:T(8,128)(2,1)S(1)} %collective-permute-done.13.refs_3_), channel_id=1, source_target_pairs={{0,8},{8,0},{16,24},{24,16},{1,9},{9,1},{17,25},{25,17},{2,10},{10... | collective-permute-start | bytes 3538952 | tf_op jit(solution)/shard_map/ppermute | solution.py:637
  42.6 5.6 %collective-permute-start.11 = (bf16[112,512]{1,0:T(8,128)(2,1)S(1)}, bf16[112,512]{1,0:T(8,128)(2,1)S(1)}, u32[]{:S(2)}, u32[]{:S(2)}) collective-permute-start(bf16[112,512]{1,0:T(8,128)(2,1)S(1)} %get-tuple-element.144), channel_id=1, source_target_pairs={{2,0},{4,2},{6,4},{7,6},{5,7},{3,5},{1,3},{0,1},{10,8},{12,10},{14... | collective-permute-start | bytes 344072 | tf_op jit(solution)/shard_map/ppermute | solution.py:657
  44.2 9.5 %copy-start.3 = (bf16[4,1,4,16,576]{4,3,2,1,0:T(8,128)(2,1)S(1)}, bf16[4,1,4,16,576]{4,3,2,1,0:T(8,128)(2,1)}, u32[]{:S(2)}) copy-start(bf16[4,1,4,16,576]{4,3,2,1,0:T(8,128)(2,1)} %param.10) | copy-start | bytes 884740
  44.2 9.5 %copy-start.4 = (bf16[4,1,4,576]{3,2,1,0:T(4,128)(2,1)S(1)}, bf16[4,1,4,576]{3,2,1,0:T(4,128)(2,1)}, u32[]{:S(2)}) copy-start(bf16[4,1,4,576]{3,2,1,0:T(4,128)(2,1)} %param.11) | copy-start | bytes 55300
  44.2 5.3 %collective-permute-start.12 = (bf16[112,512]{1,0:T(8,128)(2,1)S(1)}, bf16[112,512]{1,0:T(8,128)(2,1)S(1)}, u32[]{:S(2)}, u32[]{:S(2)}) collective-permute-start(bf16[112,512]{1,0:T(8,128)(2,1)S(1)} %get-tuple-element.145), channel_id=1, source_target_pairs={{0,2},{2,4},{4,6},{6,7},{7,5},{5,3},{3,1},{1,0},{8,10},{10,12},{12... | collective-permute-start | bytes 344072 | tf_op jit(solution)/shard_map/ppermute | solution.py:657
  49.5 7.8 %collective-permute-start.17 = (bf16[48,512]{1,0:T(8,128)(2,1)S(1)}, bf16[48,512]{1,0:T(8,128)(2,1)S(1)}, u32[]{:S(2)}, u32[]{:S(2)}) collective-permute-start(bf16[48,512]{1,0:T(8,128)(2,1)S(1)} %get-tuple-element.163), channel_id=1, source_target_pairs={{2,0},{4,2},{6,4},{7,6},{5,7},{3,5},{1,3},{0,1},{10,8},{12,10},{14... | collective-permute-start | bytes 147464 | tf_op jit(solution)/shard_map/ppermute | solution.py:657
  51.0 6.3 %collective-permute-start.18 = (bf16[48,512]{1,0:T(8,128)(2,1)S(1)}, bf16[48,512]{1,0:T(8,128)(2,1)S(1)}, u32[]{:S(2)}, u32[]{:S(2)}) collective-permute-start(bf16[48,512]{1,0:T(8,128)(2,1)S(1)} %get-tuple-element.164), channel_id=1, source_target_pairs={{0,2},{2,4},{4,6},{6,7},{7,5},{5,3},{3,1},{1,0},{8,10},{10,12},{12... | collective-permute-start | bytes 147464 | tf_op jit(solution)/shard_map/ppermute | solution.py:657
  51.7 11.9 %collective-permute-start.15 = (bf16[208,512]{1,0:T(8,128)(2,1)S(1)}, bf16[208,512]{1,0:T(8,128)(2,1)S(1)}, u32[]{:S(2)}, u32[]{:S(2)}) collective-permute-start(bf16[208,512]{1,0:T(8,128)(2,1)S(1)} %get-tuple-element.161), channel_id=1, source_target_pairs={{2,0},{4,2},{6,4},{7,6},{5,7},{3,5},{1,3},{0,1},{10,8},{12,10},{14... | collective-permute-start | bytes 638984 | tf_op jit(solution)/shard_map/ppermute | solution.py:657
  53.3 10.2 %collective-permute-start.16 = (bf16[208,512]{1,0:T(8,128)(2,1)S(1)}, bf16[208,512]{1,0:T(8,128)(2,1)S(1)}, u32[]{:S(2)}, u32[]{:S(2)}) collective-permute-start(bf16[208,512]{1,0:T(8,128)(2,1)S(1)} %get-tuple-element.162), channel_id=1, source_target_pairs={{0,2},{2,4},{4,6},{6,7},{7,5},{5,3},{3,1},{1,0},{8,10},{10,12},{12... | collective-permute-start | bytes 638984 | tf_op jit(solution)/shard_map/ppermute | solution.py:657
  53.7 14.3 %copy-start.6 = (bf16[1,2048,576]{1,2,0:T(8,128)(2,1)S(1)}, bf16[1,2048,576]{1,2,0:T(8,128)(2,1)}, u32[]{:S(2)}) copy-start(bf16[1,2048,576]{1,2,0:T(8,128)(2,1)} %param.9) | copy-start | bytes 7077892
  57.4 4.5 %collective-permute-start.19 = (bf16[80,512]{1,0:T(8,128)(2,1)S(1)}, bf16[80,512]{1,0:T(8,128)(2,1)S(1)}, u32[]{:S(2)}, u32[]{:S(2)}) collective-permute-start(bf16[80,512]{1,0:T(8,128)(2,1)S(1)} %get-tuple-element.182), channel_id=1, source_target_pairs={{2,0},{4,2},{6,4},{7,6},{5,7},{3,5},{1,3},{0,1},{10,8},{12,10},{14... | collective-permute-start | bytes 245768 | tf_op jit(solution)/shard_map/ppermute | solution.py:657
  59.1 4.4 %collective-permute-start.20 = (bf16[80,512]{1,0:T(8,128)(2,1)S(1)}, bf16[80,512]{1,0:T(8,128)(2,1)S(1)}, u32[]{:S(2)}, u32[]{:S(2)}) collective-permute-start(bf16[80,512]{1,0:T(8,128)(2,1)S(1)} %get-tuple-element.183), channel_id=1, source_target_pairs={{0,2},{2,4},{4,6},{6,7},{7,5},{5,3},{3,1},{1,0},{8,10},{10,12},{12... | collective-permute-start | bytes 245768 | tf_op jit(solution)/shard_map/ppermute | solution.py:657
  63.7 8.6 %collective-permute-start.21 = (bf16[208,512]{1,0:T(8,128)(2,1)S(1)}, bf16[208,512]{1,0:T(8,128)(2,1)S(1)}, u32[]{:S(2)}, u32[]{:S(2)}) collective-permute-start(bf16[208,512]{1,0:T(8,128)(2,1)S(1)} %get-tuple-element.190), channel_id=1, source_target_pairs={{2,0},{4,2},{6,4},{7,6},{5,7},{3,5},{1,3},{0,1},{10,8},{12,10},{14... | collective-permute-start | bytes 638984 | tf_op jit(solution)/shard_map/ppermute | solution.py:657
  65.4 7.0 %collective-permute-start.22 = (bf16[208,512]{1,0:T(8,128)(2,1)S(1)}, bf16[208,512]{1,0:T(8,128)(2,1)S(1)}, u32[]{:S(2)}, u32[]{:S(2)}) collective-permute-start(bf16[208,512]{1,0:T(8,128)(2,1)S(1)} %get-tuple-element.191), channel_id=1, source_target_pairs={{0,2},{2,4},{4,6},{6,7},{7,5},{5,3},{3,1},{1,0},{8,10},{10,12},{12... | collective-permute-start | bytes 638984 | tf_op jit(solution)/shard_map/ppermute | solution.py:657
  66.0 4.9 %collective-permute-start.23 = (bf16[80,512]{1,0:T(8,128)(2,1)S(1)}, bf16[80,512]{1,0:T(8,128)(2,1)S(1)}, u32[]{:S(2)}, u32[]{:S(2)}) collective-permute-start(bf16[80,512]{1,0:T(8,128)(2,1)S(1)} %get-tuple-element.198), channel_id=1, source_target_pairs={{2,0},{4,2},{6,4},{7,6},{5,7},{3,5},{1,3},{0,1},{10,8},{12,10},{14... | collective-permute-start | bytes 245768 | tf_op jit(solution)/shard_map/ppermute | solution.py:657
  67.6 4.8 %collective-permute-start.24 = (bf16[80,512]{1,0:T(8,128)(2,1)S(1)}, bf16[80,512]{1,0:T(8,128)(2,1)S(1)}, u32[]{:S(2)}, u32[]{:S(2)}) collective-permute-start(bf16[80,512]{1,0:T(8,128)(2,1)S(1)} %get-tuple-element.199), channel_id=1, source_target_pairs={{0,2},{2,4},{4,6},{6,7},{7,5},{5,3},{3,1},{1,0},{8,10},{10,12},{12... | collective-permute-start | bytes 245768 | tf_op jit(solution)/shard_map/ppermute | solution.py:657
  72.6 9.5 %collective-permute-start.25 = (bf16[208,512]{1,0:T(8,128)(2,1)S(1)}, bf16[208,512]{1,0:T(8,128)(2,1)S(1)}, u32[]{:S(2)}, u32[]{:S(2)}) collective-permute-start(bf16[208,512]{1,0:T(8,128)(2,1)S(1)} %get-tuple-element.208), channel_id=1, source_target_pairs={{2,0},{4,2},{6,4},{7,6},{5,7},{3,5},{1,3},{0,1},{10,8},{12,10},{14... | collective-permute-start | bytes 638984 | tf_op jit(solution)/shard_map/ppermute | solution.py:657
  73.3 8.9 %collective-permute-start.26 = (bf16[208,512]{1,0:T(8,128)(2,1)S(1)}, bf16[208,512]{1,0:T(8,128)(2,1)S(1)}, u32[]{:S(2)}, u32[]{:S(2)}) collective-permute-start(bf16[208,512]{1,0:T(8,128)(2,1)S(1)} %get-tuple-element.209), channel_id=1, source_target_pairs={{0,2},{2,4},{4,6},{6,7},{7,5},{5,3},{3,1},{1,0},{8,10},{10,12},{12... | collective-permute-start | bytes 638984 | tf_op jit(solution)/shard_map/ppermute | solution.py:657
  74.8 7.3 %collective-permute-start.27 = (bf16[80,512]{1,0:T(8,128)(2,1)S(1)}, bf16[80,512]{1,0:T(8,128)(2,1)S(1)}, u32[]{:S(2)}, u32[]{:S(2)}) collective-permute-start(bf16[80,512]{1,0:T(8,128)(2,1)S(1)} %get-tuple-element.216), channel_id=1, source_target_pairs={{2,0},{4,2},{6,4},{7,6},{5,7},{3,5},{1,3},{0,1},{10,8},{12,10},{14... | collective-permute-start | bytes 245768 | tf_op jit(solution)/shard_map/ppermute | solution.py:657
  75.5 6.7 %copy-start = (bf16[16,512,128]{2,1,0:T(8,128)(2,1)S(1)}, bf16[16,512,128]{2,1,0:T(8,128)(2,1)}, u32[]{:S(2)}) copy-start(bf16[16,512,128]{2,1,0:T(8,128)(2,1)} %refs_8_.1) | copy-start | bytes 6291460
  75.5 6.6 %collective-permute-start.28 = (bf16[80,512]{1,0:T(8,128)(2,1)S(1)}, bf16[80,512]{1,0:T(8,128)(2,1)S(1)}, u32[]{:S(2)}, u32[]{:S(2)}) collective-permute-start(bf16[80,512]{1,0:T(8,128)(2,1)S(1)} %get-tuple-element.217), channel_id=1, source_target_pairs={{0,2},{2,4},{4,6},{6,7},{7,5},{5,3},{3,1},{1,0},{8,10},{10,12},{12... | collective-permute-start | bytes 245768 | tf_op jit(solution)/shard_map/ppermute | solution.py:657

commit v5 on v4

--- a/solution.py
+++ b/solution.py
@@ -677,7 +677,7 @@
     late_came = hop_back(merge_back(late_came, late_near, late_sections))
     early_came, late_came = tie(early_came, late_came)
 
-    early_parts[0] = attend_more(["own"], pieces_of(0, 0, cut), 0, fresh, (0, heads))
+    early_parts[0] = attend_more(["own"], pieces_of(0, 0, cut), 2, fresh, (0, heads))
     late_parts = [[results[0]]]
     for hop in range(1, near):
         late_parts.append(results[2 * hop - 1 : 2 * hop + 1])

time: 98.1 us -> 96.9 us (0.988)
  waiting for transfers between devices: 13.9 us -> 11.6 us
    ppermute x16, waiting for transfers between devices: 7.56 us -> 5.09 us  [hop_back(): send(block)]
    pallas_call x7, Pallas kernels: 28.1 us -> 30.2 us  [attend(): pl.pallas_call(functools.partial(attend_kernel, tuple(kinds), rows, takes...]
    pallas_call x1, Pallas kernels: 5.18 us -> 3.22 us  [load_alone(): pl.pallas_call(functools.partial(load_kernel, start, stop), out_shape=plt...]
    ppermute x6, waiting for transfers between devices: 4.42 us -> 5.87 us  [body(): came = (right(lefts[-1]), left(rights[-1]))]
    ppermute x1, starting transfers between devices: 0.67 us -> 1.69 us  [body(): right(lefts[-1][:half])]
  transfers between devices with their start and end apart: 27 -> 27, of which waited for: 11 -> 10; matrix products, arithmetic and copies ran while one was open for 0% -> 0% of each run, Pallas kernels for 38% -> 38%
where the time goes in v5:
time: 96.9 us; the launch traced here: 96.5 us
  Pallas kernels  41.9 us (43%)
  starting transfers between devices  27.4 us (28%)
  waiting for transfers between devices  11.6 us (12%)
  blocking collectives  11.3 us (12%)
  local copies, waits for them, and re-layouts  3.39 us (3%)
    pallas_call x7, Pallas kernels, attend(): pl.pallas_call(functools.partial(attend_kernel, tuple(kinds), rows, takes...  30.2 us
    ppermute x16, starting transfers between devices, hop_back(): send(block)  16.6 us
    all_to_all x1, blocking collectives, body(): lax.all_to_all(term, 'ctx', split_axis=0, concat_axis=0, tiled=True)  11.3 us
    ppermute x6, starting transfers between devices, body(): came = (right(lefts[-1]), left(rights[-1]))  6.63 us
    ppermute x6, waiting for transfers between devices, body(): came = (right(lefts[-1]), left(rights[-1]))  5.87 us
    ppermute x16, waiting for transfers between devices, hop_back(): send(block)  5.09 us
    pallas_call x1, Pallas kernels, finish(): pl.pallas_call(functools.partial(finish_kernel, len(chunk_parts), heads,...  4.48 us
    pallas_call x1, Pallas kernels, load_alone(): pl.pallas_call(functools.partial(load_kernel, start, stop), out_shape=plt...  3.22 us
  transfers between devices with their start and end apart: 27, of which 10 were waited for; matrix products, arithmetic and copies ran while one was open for 0% of the time, Pallas kernels for 38%

profile of v5, /device:TPU:0, one launch (start us, length us, event | category | flops | bytes accessed | tf_op | source)
XLA Modules:
  0.0 96.5 jit_solution(9369492262682194601)
XLA Ops:
  0.0 0.5 collective-permute-start.4
  0.5 2.6 %collective-permute-start.2 = (bf16[256,576]{1,0:T(8,128)(2,1)}, bf16[256,576]{1,0:T(8,128)(2,1)S(1)}, u32[]{:S(2)}, u32[]{:S(2)}) collective-permute-start(bf16[256,576]{1,0:T(8,128)(2,1)} %bitcast.9), channel_id=1, source_target_pairs={{0,2},{2,4},{4,6},{6,7},{7,5},{5,3},{3,1},{1,0},{8,10},{10,12},{12... | collective-permute-start | bytes 884744 | tf_op jit(solution)/shard_map/ppermute | solution.py:612
  3.0 0.7 copy-done.3
  3.7 0.7 copy-done.4
  4.3 1.2 %plan.1 = (s32[6]{0:T(128)S(1)}, s32[1]{0:T(128)}) custom-call(s32[1]{0:T(128)} %bitcast.1.group_ref, s32[1]{0:T(128)} %bitcast.2.place_ref, s32[4]{0:T(128)S(1)} %copy-done.3, s32[4]{0:T(128)S(1)} %copy-done.4), custom_call_target="tpu_custom_call" | custom-call | tf_op jit(solution)/shard_map/plan/pallas_call | solution.py:472
  5.5 1.4 %copy-done.7 = bf16[576,2048]{1,0:T(8,128)(2,1)} copy-done((bf16[576,2048]{1,0:T(8,128)(2,1)}, bf16[576,2048]{1,0:T(8,128)(2,1)S(1)}, u32[]{:S(2)}) %copy-start.7) | copy-done | bytes 2359320
  6.9 1.8 %offer.1 = bf16[288,2048]{1,0:T(8,128)(2,1)S(1)} custom-call(s32[6]{0:T(128)S(1)} %get-tuple-element.123.info_ref.refs_0_, bf16[576,2048]{1,0:T(8,128)(2,1)} %bitcast.16, bf16[576,2048]{1,0:T(8,128)(2,1)} %copy-done.7), custom_call_target="tpu_custom_call" | custom-call | bytes 2097152 | tf_op jit(solution)/shard_map/offer/pallas_call | solution.py:506
  8.8 2.8 %collective-permute-done.2.refs_2_.refs_3_ = bf16[256,576]{1,0:T(8,128)(2,1)S(1)} collective-permute-done((bf16[256,576]{1,0:T(8,128)(2,1)}, bf16[256,576]{1,0:T(8,128)(2,1)S(1)}, u32[]{:S(2)}, u32[]{:S(2)}) %collective-permute-start.2) | collective-permute-done | bytes 294944 | tf_op jit(solution)/shard_map/ppermute | solution.py:612
  11.5 1.5 %collective-permute-done.3.refs_3_.refs_4_ = bf16[256,576]{1,0:T(8,128)(2,1)S(1)} collective-permute-done((bf16[256,576]{1,0:T(8,128)(2,1)}, bf16[256,576]{1,0:T(8,128)(2,1)S(1)}, u32[]{:S(2)}, u32[]{:S(2)}) %collective-permute-start.3) | collective-permute-done | bytes 294944 | tf_op jit(solution)/shard_map/ppermute | solution.py:612
  13.1 1.5 %collective-permute-start.13 = (bf16[288,2048]{1,0:T(8,128)(2,1)S(1)}, bf16[288,2048]{1,0:T(8,128)(2,1)S(1)}, u32[]{:S(2)}, u32[]{:S(2)}) collective-permute-start(bf16[288,2048]{1,0:T(8,128)(2,1)S(1)} %offer.1), channel_id=1, source_target_pairs={{0,16},{8,24},{16,0},{24,8},{1,17},{9,25},{17,1},{25,9},{2,18},{10... | collective-permute-start | bytes 3538952 | tf_op jit(solution)/shard_map/ppermute | solution.py:627
  14.6 1.6 %collective-permute-start.5 = (bf16[256,576]{1,0:T(8,128)(2,1)S(1)}, bf16[256,576]{1,0:T(8,128)(2,1)S(1)}, u32[]{:S(2)}, u32[]{:S(2)}) collective-permute-start(bf16[256,576]{1,0:T(8,128)(2,1)S(1)} %collective-permute-done.2.refs_2_.refs_3_), channel_id=1, source_target_pairs={{0,2},{2,4},{4,6},{6,7},{7,5},{5,3},{3,1},{1,0},{8,10},{10,12},{12... | collective-permute-start | bytes 884744 | tf_op jit(solution)/shard_map/ppermute | solution.py:612
  16.2 0.4 collective-permute-start.6
  17.2 6.9 %attend_keep_keep.3 = (f32[192,512]{1,0:T(8,128)S(1)}, f32[8,96]{1,0:T(8,128)S(1)}, f32[192,512]{1,0:T(8,128)S(1)}, f32[8,96]{1,0:T(8,128)S(1)}, bf16[2048,1792]{1,0:T(8,128)(2,1)S(1)}) custom-call(s32[6]{0:T(128)S(1)} %get-tuple-element.123.info_ref.refs_0_, bf16[576,2048]{1,0:T(8,128)(2,1)} %bitcast.18, ...), custom_call_target="tpu_custom_call" | custom-call | flops 1711276032 | bytes 4194304 | tf_op jit(solution)/shard_map/attend_keep_keep/pallas_call | solution.py:289
  24.2 0.6 collective-permute-done.6.refs_3_.refs_6_
  24.7 1.6 %collective-permute-start.7 = (bf16[256,576]{1,0:T(8,128)(2,1)S(1)}, bf16[256,576]{1,0:T(8,128)(2,1)S(1)}, u32[]{:S(2)}, u32[]{:S(2)}) collective-permute-start(bf16[256,576]{1,0:T(8,128)(2,1)S(1)} %collective-permute-done.5.refs_2_.refs_5_), channel_id=1, source_target_pairs={{0,2},{2,4},{4,6},{6,7},{7,5},{5,3},{3,1},{1,0},{8,10},{10,12},{12... | collective-permute-start | bytes 884744 | tf_op jit(solution)/shard_map/ppermute | solution.py:612
  26.3 0.4 collective-permute-start.8
  26.8 6.5 %attend_keep_keep.4 = (f32[192,512]{1,0:T(8,128)S(1)}, f32[8,96]{1,0:T(8,128)S(1)}, f32[192,512]{1,0:T(8,128)S(1)}, f32[8,96]{1,0:T(8,128)S(1)}, bf16[2048,1792]{1,0:T(8,128)(2,1)S(1)}) custom-call(s32[6]{0:T(128)S(1)} %get-tuple-element.123.info_ref.refs_0_, bf16[576,2048]{1,0:T(8,128)(2,1)S(1)} %bitcast.20, ...), custom_call_target="tpu_custom_call" | custom-call | flops 1711276032 | bytes 4194304 | tf_op jit(solution)/shard_map/attend_keep_keep/pallas_call | solution.py:289
  33.3 1.0 %collective-permute-done.8.refs_3_.refs_8_ = bf16[256,576]{1,0:T(8,128)(2,1)S(1)} collective-permute-done((bf16[256,576]{1,0:T(8,128)(2,1)}, bf16[256,576]{1,0:T(8,128)(2,1)S(1)}, u32[]{:S(2)}, u32[]{:S(2)}) %collective-permute-start.8) | collective-permute-done | bytes 294944 | tf_op jit(solution)/shard_map/ppermute | solution.py:612
  34.3 0.4 collective-permute-start.10
  34.8 1.7 %collective-permute-start.9 = (bf16[128,576]{1,0:T(8,128)(2,1)S(1)}, bf16[128,576]{1,0:T(8,128)(2,1)S(1)}, u32[]{:S(2)}, u32[]{:S(2)}) collective-permute-start(bf16[128,576]{1,0:T(8,128)(2,1)S(1)} %slice.12), channel_id=1, source_target_pairs={{0,2},{2,4},{4,6},{6,7},{7,5},{5,3},{3,1},{1,0},{8,10},{10,12},{12... | collective-permute-start | bytes 442376 | tf_op jit(solution)/shard_map/ppermute | solution.py:615
  36.5 3.2 %attend_keep_keep.5 = (f32[192,512]{1,0:T(8,128)S(1)}, f32[8,96]{1,0:T(8,128)S(1)}, f32[192,512]{1,0:T(8,128)S(1)}, f32[8,96]{1,0:T(8,128)S(1)}) custom-call(s32[6]{0:T(128)S(1)} %get-tuple-element.123.info_ref.refs_0_, bf16[576,2048]{1,0:T(8,128)(2,1)S(1)} %bitcast.21, bf16[256,576]{1,0:T(8,128)(2,1)S(1)} %collective-permute-done.7.refs_2_.refs_7_, ...), custom_call_target="tpu_custom_call" | custom-call | flops 1711276032 | bytes 4194304 | tf_op jit(solution)/shard_map/attend_keep_keep/pallas_call | solution.py:289
  39.7 0.4 collective-permute-done.9.refs_2_
  40.4 2.3 %attend_ends.1 = (bf16[112,512]{1,0:T(8,128)(2,1)S(1)}, bf16[112,512]{1,0:T(8,128)(2,1)S(1)}) custom-call(s32[6]{0:T(128)S(1)} %get-tuple-element.123.info_ref.refs_0_, bf16[576,2048]{1,0:T(8,128)(2,1)S(1)} %bitcast.22, bf16[128,576]{1,0:T(8,128)(2,1)S(1)} %collective-permute-done.9.refs_2_, bf16[128,576]{1,0:T(8,128)(2,1)S(1)} %collective-permute-done.10.refs_3_.refs_6_), custom_call_target="tpu_custom_call" | custom-call | flops 855638016 | bytes 4194304 | tf_op jit(solution)/shard_map/attend_ends/pallas_call | solution.py:289
  42.6 0.7 collective-permute-start.11
  43.3 1.4 %collective-permute-start.12 = (bf16[112,512]{1,0:T(8,128)(2,1)S(1)}, bf16[112,512]{1,0:T(8,128)(2,1)S(1)}, u32[]{:S(2)}, u32[]{:S(2)}) collective-permute-start(bf16[112,512]{1,0:T(8,128)(2,1)S(1)} %get-tuple-element.146), channel_id=1, source_target_pairs={{0,2},{2,4},{4,6},{6,7},{7,5},{5,3},{3,1},{1,0},{8,10},{10,12},{12... | collective-permute-start | bytes 344072 | tf_op jit(solution)/shard_map/ppermute | solution.py:657
  44.7 4.0 %attend_ends_keep_keep.1 = (bf16[48,512]{1,0:T(8,128)(2,1)S(1)}, bf16[48,512]{1,0:T(8,128)(2,1)S(1)}, f32[64,512]{1,0:T(8,128)S(1)}, f32[8,32]{1,0:T(8,128)S(1)}...) custom-call(s32[6]{0:T(128)S(1)} %get-tuple-element.123.info_ref.refs_0_, ...), custom_call_target="tpu_custom_call" | custom-call | flops 855638016 | bytes 4194304 | tf_op jit(solution)/shard_map/attend_ends_keep_keep/pallas_call | solution.py:289
  48.7 1.3 %collective-permute-start.17 = (bf16[48,512]{1,0:T(8,128)(2,1)S(1)}, bf16[48,512]{1,0:T(8,128)(2,1)S(1)}, u32[]{:S(2)}, u32[]{:S(2)}) collective-permute-start(bf16[48,512]{1,0:T(8,128)(2,1)S(1)} %get-tuple-element.164), channel_id=1, source_target_pairs={{2,0},{4,2},{6,4},{7,6},{5,7},{3,5},{1,3},{0,1},{10,8},{12,10},{14... | collective-permute-start | bytes 147464 | tf_op jit(solution)/shard_map/ppermute | solution.py:657
  50.1 0.7 collective-permute-start.18
  51.0 1.3 %collective-permute-start.15 = (bf16[208,512]{1,0:T(8,128)(2,1)S(1)}, bf16[208,512]{1,0:T(8,128)(2,1)S(1)}, u32[]{:S(2)}, u32[]{:S(2)}) collective-permute-start(bf16[208,512]{1,0:T(8,128)(2,1)S(1)} %get-tuple-element.162), channel_id=1, source_target_pairs={{2,0},{4,2},{6,4},{7,6},{5,7},{3,5},{1,3},{0,1},{10,8},{12,10},{14... | collective-permute-start | bytes 638984 | tf_op jit(solution)/shard_map/ppermute | solution.py:657
  52.3 0.7 collective-permute-start.16
  53.1 3.6 %attend_own_keep_keep_keep_keep.1 = (f32[64,512]{1,0:T(8,128)S(1)}, f32[8,32]{1,0:T(8,128)S(1)}, f32[64,512]{1,0:T(8,128)S(1)}, f32[8,32]{1,0:T(8,128)S(1)}, f32...) custom-call(s32[6]{0:T(128)S(1)} %get-tuple-element.123.info_ref.ref, ...), custom_call_target="tpu_custom_call" | custom-call | flops 1426063360 | bytes 4194304 | tf_op jit(solution)/shard_map/attend_own_keep_keep_keep_keep/pallas_call | solution.py:289
  56.8 1.3 %collective-permute-start.19 = (bf16[80,512]{1,0:T(8,128)(2,1)S(1)}, bf16[80,512]{1,0:T(8,128)(2,1)S(1)}, u32[]{:S(2)}, u32[]{:S(2)}) collective-permute-start(bf16[80,512]{1,0:T(8,128)(2,1)S(1)} %get-tuple-element.183), channel_id=1, source_target_pairs={{2,0},{4,2},{6,4},{7,6},{5,7},{3,5},{1,3},{0,1},{10,8},{12,10},{14... | collective-permute-start | bytes 245768 | tf_op jit(solution)/shard_map/ppermute | solution.py:657
  58.1 0.7 collective-permute-start.20
  58.9 2.4 %collective-permute-done.19.refs_0_ = bf16[80,512]{1,0:T(8,128)(2,1)S(1)} collective-permute-done((bf16[80,512]{1,0:T(8,128)(2,1)S(1)}, bf16[80,512]{1,0:T(8,128)(2,1)S(1)}, u32[]{:S(2)}, u32[]{:S(2)}) %collective-permute-start.19) | collective-permute-done | bytes 81952 | tf_op jit(solution)/shard_map/ppermute | solution.py:657
  61.3 1.3 %collective-permute-done.20.refs_3_ = bf16[80,512]{1,0:T(8,128)(2,1)S(1)} collective-permute-done((bf16[80,512]{1,0:T(8,128)(2,1)S(1)}, bf16[80,512]{1,0:T(8,128)(2,1)S(1)}, u32[]{:S(2)}, u32[]{:S(2)}) %collective-permute-start.20) | collective-permute-done | bytes 81952 | tf_op jit(solution)/shard_map/ppermute | solution.py:657
  62.8 1.6 %collective-permute-start.21 = (bf16[208,512]{1,0:T(8,128)(2,1)S(1)}, bf16[208,512]{1,0:T(8,128)(2,1)S(1)}, u32[]{:S(2)}, u32[]{:S(2)}) collective-permute-start(bf16[208,512]{1,0:T(8,128)(2,1)S(1)} %get-tuple-element.191), channel_id=1, source_target_pairs={{2,0},{4,2},{6,4},{7,6},{5,7},{3,5},{1,3},{0,1},{10,8},{12,10},{14... | collective-permute-start | bytes 638984 | tf_op jit(solution)/shard_map/ppermute | solution.py:657
  64.4 0.4 collective-permute-start.22
  65.0 1.6 %collective-permute-start.23 = (bf16[80,512]{1,0:T(8,128)(2,1)S(1)}, bf16[80,512]{1,0:T(8,128)(2,1)S(1)}, u32[]{:S(2)}, u32[]{:S(2)}) collective-permute-start(bf16[80,512]{1,0:T(8,128)(2,1)S(1)} %get-tuple-element.199), channel_id=1, source_target_pairs={{2,0},{4,2},{6,4},{7,6},{5,7},{3,5},{1,3},{0,1},{10,8},{12,10},{14... | collective-permute-start | bytes 245768 | tf_op jit(solution)/shard_map/ppermute | solution.py:657
  66.7 0.4 collective-permute-start.24
  67.1 3.7 %attend_own.1 = (f32[192,512]{1,0:T(8,128)S(1)}, f32[8,96]{1,0:T(8,128)S(1)}, bf16[2048,1792]{1,0:T(8,128)(2,1)S(1)}) custom-call(s32[6]{0:T(128)S(1)} %get-tuple-element.123.info_ref.refs_0_, bf16[576,2048]{1,0:T(8,128)(2,1)S(1)} %bitcast.23, bf16[256,576]{1,0:T(8,128)(2,1)S(1)} %bitcast.12, bf16[4,4,576]{2,1,0:T(4,128)(2,1)S(1)} %bitcast.14, ...), custom_call_target="tpu_custom_call" | custom-call | flops 855638016 | bytes 4194304 | tf_op jit(solution)/shard_map/attend_own/pallas_call | solution.py:289
  70.8 0.4 collective-permute-done.24.refs_3_
  71.4 1.8 %collective-permute-start.25 = (bf16[208,512]{1,0:T(8,128)(2,1)S(1)}, bf16[208,512]{1,0:T(8,128)(2,1)S(1)}, u32[]{:S(2)}, u32[]{:S(2)}) collective-permute-start(bf16[208,512]{1,0:T(8,128)(2,1)S(1)} %get-tuple-element.209), channel_id=1, source_target_pairs={{2,0},{4,2},{6,4},{7,6},{5,7},{3,5},{1,3},{0,1},{10,8},{12,10},{14... | collective-permute-start | bytes 638984 | tf_op jit(solution)/shard_map/ppermute | solution.py:657
  73.6 1.8 %collective-permute-start.27 = (bf16[80,512]{1,0:T(8,128)(2,1)S(1)}, bf16[80,512]{1,0:T(8,128)(2,1)S(1)}, u32[]{:S(2)}, u32[]{:S(2)}) collective-permute-start(bf16[80,512]{1,0:T(8,128)(2,1)S(1)} %get-tuple-element.217), channel_id=1, source_target_pairs={{2,0},{4,2},{6,4},{7,6},{5,7},{3,5},{1,3},{0,1},{10,8},{12,10},{14... | collective-permute-start | bytes 245768 | tf_op jit(solution)/shard_map/ppermute | solution.py:657
  75.7 3.2 %load.1.refs_12_ = bf16[2048,1792]{1,0:T(8,128)(2,1)S(1)} custom-call(bf16[2048,7168]{1,0:T(8,128)(2,1)} %weight_ref.1), custom_call_target="tpu_custom_call" | custom-call | bytes 7340032 | tf_op jit(solution)/shard_map/load/pallas_call | solution.py:319
  79.0 1.0 %collective-permute-done.28.refs_5_ = bf16[80,512]{1,0:T(8,128)(2,1)S(1)} collective-permute-done((bf16[80,512]{1,0:T(8,128)(2,1)S(1)}, bf16[80,512]{1,0:T(8,128)(2,1)S(1)}, u32[]{:S(2)}, u32[]{:S(2)}) %collective-permute-start.28) | collective-permute-done | bytes 81952 | tf_op jit(solution)/shard_map/ppermute | solution.py:657
  80.0 4.5 %finish.1 = bf16[8,16,896]{2,1,0:T(8,128)(2,1)S(1)} custom-call(bf16[208,512]{1,0:T(8,128)(2,1)S(1)} %collective-permute-done.25.refs_0_, bf16[208,512]{1,0:T(8,128)(2,1)S(1)} %collective-permute-done.26.refs_1_, f32[192,512]{1,0:T(8,128)S(1)} %get-tuple-element.223.refs_2_, f32[8,96]{1,0:T(8,128)S(1)} %get-tuple-element.224.refs_3_, ...), custom_call_target="tpu_custom_call" | custom-call | flops 469762048 | bytes 29360128 | tf_op jit(solution)/shard_map/finish/pallas_call | solution.py:427
  84.5 11.3 %all_to_all.5 = bf16[8,16,896]{2,1,0:T(8,128)(2,1)S(1)} all-to-all(bf16[8,16,896]{2,1,0:T(8,128)(2,1)S(1)} %finish.1), channel_id=1, replica_groups=mesh['grp'=4,'ctx'=8] {'ctx'}, dimensions={0} | all-to-all | bytes 458752 | tf_op jit(solution)/shard_map/all_to_all | solution.py:697
  95.8 0.6 reshape.27
  (46 shorter events, 1.9 us)
Async XLA Ops:
  0.0 5.5 %collective-permute-start.4 = (bf16[576,2048]{1,0:T(8,128)(2,1)}, bf16[576,2048]{1,0:T(8,128)(2,1)S(1)}, u32[]{:S(2)}, u32[]{:S(2)}) collective-permute-start(bf16[576,2048]{1,0:T(8,128)(2,1)} %bitcast.15), channel_id=1, source_target_pairs={{0,8},{8,0},{16,24},{24,16},{1,9},{9,1},{17,25},{25,17},{2,10},{10... | collective-permute-start | bytes 7077896 | tf_op jit(solution)/shard_map/ppermute | solution.py:569
  0.5 11.1 %collective-permute-start.2 = (bf16[256,576]{1,0:T(8,128)(2,1)}, bf16[256,576]{1,0:T(8,128)(2,1)S(1)}, u32[]{:S(2)}, u32[]{:S(2)}) collective-permute-start(bf16[256,576]{1,0:T(8,128)(2,1)} %bitcast.9), channel_id=1, source_target_pairs={{0,2},{2,4},{4,6},{6,7},{7,5},{5,3},{3,1},{1,0},{8,10},{10,12},{12... | collective-permute-start | bytes 884744 | tf_op jit(solution)/shard_map/ppermute | solution.py:612
  3.0 10.1 %collective-permute-start.3 = (bf16[256,576]{1,0:T(8,128)(2,1)}, bf16[256,576]{1,0:T(8,128)(2,1)S(1)}, u32[]{:S(2)}, u32[]{:S(2)}) collective-permute-start(bf16[256,576]{1,0:T(8,128)(2,1)} %bitcast.10), channel_id=1, source_target_pairs={{2,0},{4,2},{6,4},{7,6},{5,7},{3,5},{1,3},{0,1},{10,8},{12,10},{14... | collective-permute-start | bytes 884744 | tf_op jit(solution)/shard_map/ppermute | solution.py:612
  3.0 0.7 copy-start.3
  3.7 0.7 copy-start.4
  5.5 1.4 %copy-start.7 = (bf16[576,2048]{1,0:T(8,128)(2,1)}, bf16[576,2048]{1,0:T(8,128)(2,1)S(1)}, u32[]{:S(2)}) copy-start(bf16[576,2048]{1,0:T(8,128)(2,1)S(1)} %collective-permute-done.4.beside_ref.refs_2_) | copy-start | bytes 7077892
  13.1 27.3 %collective-permute-start.13 = (bf16[288,2048]{1,0:T(8,128)(2,1)S(1)}, bf16[288,2048]{1,0:T(8,128)(2,1)S(1)}, u32[]{:S(2)}, u32[]{:S(2)}) collective-permute-start(bf16[288,2048]{1,0:T(8,128)(2,1)S(1)} %offer.1), channel_id=1, source_target_pairs={{0,16},{8,24},{16,0},{24,8},{1,17},{9,25},{17,1},{25,9},{2,18},{10... | collective-permute-start | bytes 3538952 | tf_op jit(solution)/shard_map/ppermute | solution.py:627
  14.6 9.6 %collective-permute-start.5 = (bf16[256,576]{1,0:T(8,128)(2,1)S(1)}, bf16[256,576]{1,0:T(8,128)(2,1)S(1)}, u32[]{:S(2)}, u32[]{:S(2)}) collective-permute-start(bf16[256,576]{1,0:T(8,128)(2,1)S(1)} %collective-permute-done.2.refs_2_.refs_3_), channel_id=1, source_target_pairs={{0,2},{2,4},{4,6},{6,7},{7,5},{5,3},{3,1},{1,0},{8,10},{10,12},{12... | collective-permute-start | bytes 884744 | tf_op jit(solution)/shard_map/ppermute | solution.py:612
  16.2 8.6 %collective-permute-start.6 = (bf16[256,576]{1,0:T(8,128)(2,1)S(1)}, bf16[256,576]{1,0:T(8,128)(2,1)}, u32[]{:S(2)}, u32[]{:S(2)}) collective-permute-start(bf16[256,576]{1,0:T(8,128)(2,1)S(1)} %collective-permute-done.3.refs_3_.refs_4_), channel_id=1, source_target_pairs={{2,0},{4,2},{6,4},{7,6},{5,7},{3,5},{1,3},{0,1},{10,8},{12,10},{14... | collective-permute-start | bytes 884744 | tf_op jit(solution)/shard_map/ppermute | solution.py:612
  17.2 9.6 %copy-start.5 = (bf16[1,2048,576]{1,2,0:T(8,128)(2,1)S(1)}, bf16[1,2048,576]{1,2,0:T(8,128)(2,1)}, u32[]{:S(2)}) copy-start(bf16[1,2048,576]{1,2,0:T(8,128)(2,1)} %param.9) | copy-start | bytes 7077892
  24.7 8.6 %collective-permute-start.7 = (bf16[256,576]{1,0:T(8,128)(2,1)S(1)}, bf16[256,576]{1,0:T(8,128)(2,1)S(1)}, u32[]{:S(2)}, u32[]{:S(2)}) collective-permute-start(bf16[256,576]{1,0:T(8,128)(2,1)S(1)} %collective-permute-done.5.refs_2_.refs_5_), channel_id=1, source_target_pairs={{0,2},{2,4},{4,6},{6,7},{7,5},{5,3},{3,1},{1,0},{8,10},{10,12},{12... | collective-permute-start | bytes 884744 | tf_op jit(solution)/shard_map/ppermute | solution.py:612
  26.3 8.0 %collective-permute-start.8 = (bf16[256,576]{1,0:T(8,128)(2,1)}, bf16[256,576]{1,0:T(8,128)(2,1)S(1)}, u32[]{:S(2)}, u32[]{:S(2)}) collective-permute-start(bf16[256,576]{1,0:T(8,128)(2,1)} %collective-permute-done.6.refs_3_.refs_6_), channel_id=1, source_target_pairs={{2,0},{4,2},{6,4},{7,6},{5,7},{3,5},{1,3},{0,1},{10,8},{12,10},{14... | collective-permute-start | bytes 884744 | tf_op jit(solution)/shard_map/ppermute | solution.py:612
  34.3 5.4 %collective-permute-start.10 = (bf16[128,576]{1,0:T(8,128)(2,1)S(1)}, bf16[128,576]{1,0:T(8,128)(2,1)S(1)}, u32[]{:S(2)}, u32[]{:S(2)}) collective-permute-start(bf16[128,576]{1,0:T(8,128)(2,1)S(1)} %slice.13), channel_id=1, source_target_pairs={{2,0},{4,2},{6,4},{7,6},{5,7},{3,5},{1,3},{0,1},{10,8},{12,10},{14... | collective-permute-start | bytes 442376 | tf_op jit(solution)/shard_map/ppermute | solution.py:616
  34.8 5.4 %collective-permute-start.9 = (bf16[128,576]{1,0:T(8,128)(2,1)S(1)}, bf16[128,576]{1,0:T(8,128)(2,1)S(1)}, u32[]{:S(2)}, u32[]{:S(2)}) collective-permute-start(bf16[128,576]{1,0:T(8,128)(2,1)S(1)} %slice.12), channel_id=1, source_target_pairs={{0,2},{2,4},{4,6},{6,7},{7,5},{5,3},{3,1},{1,0},{8,10},{10,12},{12... | collective-permute-start | bytes 442376 | tf_op jit(solution)/shard_map/ppermute | solution.py:615
  40.4 4.4 %collective-permute-start.14 = (bf16[288,2048]{1,0:T(8,128)(2,1)S(1)}, bf16[288,2048]{1,0:T(8,128)(2,1)S(1)}, u32[]{:S(2)}, u32[]{:S(2)}) collective-permute-start(bf16[288,2048]{1,0:T(8,128)(2,1)S(1)} %collective-permute-done.13.refs_3_), channel_id=1, source_target_pairs={{0,8},{8,0},{16,24},{24,16},{1,9},{9,1},{17,25},{25,17},{2,10},{10... | collective-permute-start | bytes 3538952 | tf_op jit(solution)/shard_map/ppermute | solution.py:637
  42.6 6.1 %collective-permute-start.11 = (bf16[112,512]{1,0:T(8,128)(2,1)S(1)}, bf16[112,512]{1,0:T(8,128)(2,1)S(1)}, u32[]{:S(2)}, u32[]{:S(2)}) collective-permute-start(bf16[112,512]{1,0:T(8,128)(2,1)S(1)} %get-tuple-element.145), channel_id=1, source_target_pairs={{2,0},{4,2},{6,4},{7,6},{5,7},{3,5},{1,3},{0,1},{10,8},{12,10},{14... | collective-permute-start | bytes 344072 | tf_op jit(solution)/shard_map/ppermute | solution.py:657
  43.3 9.7 %copy-start.1 = (bf16[4,1,4,16,576]{4,3,2,1,0:T(8,128)(2,1)S(1)}, bf16[4,1,4,16,576]{4,3,2,1,0:T(8,128)(2,1)}, u32[]{:S(2)}) copy-start(bf16[4,1,4,16,576]{4,3,2,1,0:T(8,128)(2,1)} %param.10) | copy-start | bytes 884740
  43.3 9.7 %copy-start.2 = (bf16[4,1,4,576]{3,2,1,0:T(4,128)(2,1)S(1)}, bf16[4,1,4,576]{3,2,1,0:T(4,128)(2,1)}, u32[]{:S(2)}) copy-start(bf16[4,1,4,576]{3,2,1,0:T(4,128)(2,1)} %param.11) | copy-start | bytes 55300
  43.3 5.4 %collective-permute-start.12 = (bf16[112,512]{1,0:T(8,128)(2,1)S(1)}, bf16[112,512]{1,0:T(8,128)(2,1)S(1)}, u32[]{:S(2)}, u32[]{:S(2)}) collective-permute-start(bf16[112,512]{1,0:T(8,128)(2,1)S(1)} %get-tuple-element.146), channel_id=1, source_target_pairs={{0,2},{2,4},{4,6},{6,7},{7,5},{5,3},{3,1},{1,0},{8,10},{10,12},{12... | collective-permute-start | bytes 344072 | tf_op jit(solution)/shard_map/ppermute | solution.py:657
  48.7 7.9 %collective-permute-start.17 = (bf16[48,512]{1,0:T(8,128)(2,1)S(1)}, bf16[48,512]{1,0:T(8,128)(2,1)S(1)}, u32[]{:S(2)}, u32[]{:S(2)}) collective-permute-start(bf16[48,512]{1,0:T(8,128)(2,1)S(1)} %get-tuple-element.164), channel_id=1, source_target_pairs={{2,0},{4,2},{6,4},{7,6},{5,7},{3,5},{1,3},{0,1},{10,8},{12,10},{14... | collective-permute-start | bytes 147464 | tf_op jit(solution)/shard_map/ppermute | solution.py:657
  50.1 6.6 %collective-permute-start.18 = (bf16[48,512]{1,0:T(8,128)(2,1)S(1)}, bf16[48,512]{1,0:T(8,128)(2,1)S(1)}, u32[]{:S(2)}, u32[]{:S(2)}) collective-permute-start(bf16[48,512]{1,0:T(8,128)(2,1)S(1)} %get-tuple-element.165), channel_id=1, source_target_pairs={{0,2},{2,4},{4,6},{6,7},{7,5},{5,3},{3,1},{1,0},{8,10},{10,12},{12... | collective-permute-start | bytes 147464 | tf_op jit(solution)/shard_map/ppermute | solution.py:657
  51.0 11.6 %collective-permute-start.15 = (bf16[208,512]{1,0:T(8,128)(2,1)S(1)}, bf16[208,512]{1,0:T(8,128)(2,1)S(1)}, u32[]{:S(2)}, u32[]{:S(2)}) collective-permute-start(bf16[208,512]{1,0:T(8,128)(2,1)S(1)} %get-tuple-element.162), channel_id=1, source_target_pairs={{2,0},{4,2},{6,4},{7,6},{5,7},{3,5},{1,3},{0,1},{10,8},{12,10},{14... | collective-permute-start | bytes 638984 | tf_op jit(solution)/shard_map/ppermute | solution.py:657
  52.3 10.3 %collective-permute-start.16 = (bf16[208,512]{1,0:T(8,128)(2,1)S(1)}, bf16[208,512]{1,0:T(8,128)(2,1)S(1)}, u32[]{:S(2)}, u32[]{:S(2)}) collective-permute-start(bf16[208,512]{1,0:T(8,128)(2,1)S(1)} %get-tuple-element.163), channel_id=1, source_target_pairs={{0,2},{2,4},{4,6},{6,7},{7,5},{5,3},{3,1},{1,0},{8,10},{10,12},{12... | collective-permute-start | bytes 638984 | tf_op jit(solution)/shard_map/ppermute | solution.py:657
  53.1 14.0 %copy-start.6 = (bf16[1,2048,576]{1,2,0:T(8,128)(2,1)S(1)}, bf16[1,2048,576]{1,2,0:T(8,128)(2,1)}, u32[]{:S(2)}) copy-start(bf16[1,2048,576]{1,2,0:T(8,128)(2,1)} %param.9) | copy-start | bytes 7077892
  56.8 4.5 %collective-permute-start.19 = (bf16[80,512]{1,0:T(8,128)(2,1)S(1)}, bf16[80,512]{1,0:T(8,128)(2,1)S(1)}, u32[]{:S(2)}, u32[]{:S(2)}) collective-permute-start(bf16[80,512]{1,0:T(8,128)(2,1)S(1)} %get-tuple-element.183), channel_id=1, source_target_pairs={{2,0},{4,2},{6,4},{7,6},{5,7},{3,5},{1,3},{0,1},{10,8},{12,10},{14... | collective-permute-start | bytes 245768 | tf_op jit(solution)/shard_map/ppermute | solution.py:657
  58.1 4.4 %collective-permute-start.20 = (bf16[80,512]{1,0:T(8,128)(2,1)S(1)}, bf16[80,512]{1,0:T(8,128)(2,1)S(1)}, u32[]{:S(2)}, u32[]{:S(2)}) collective-permute-start(bf16[80,512]{1,0:T(8,128)(2,1)S(1)} %get-tuple-element.184), channel_id=1, source_target_pairs={{0,2},{2,4},{4,6},{6,7},{7,5},{5,3},{3,1},{1,0},{8,10},{10,12},{12... | collective-permute-start | bytes 245768 | tf_op jit(solution)/shard_map/ppermute | solution.py:657
  62.8 8.4 %collective-permute-start.21 = (bf16[208,512]{1,0:T(8,128)(2,1)S(1)}, bf16[208,512]{1,0:T(8,128)(2,1)S(1)}, u32[]{:S(2)}, u32[]{:S(2)}) collective-permute-start(bf16[208,512]{1,0:T(8,128)(2,1)S(1)} %get-tuple-element.191), channel_id=1, source_target_pairs={{2,0},{4,2},{6,4},{7,6},{5,7},{3,5},{1,3},{0,1},{10,8},{12,10},{14... | collective-permute-start | bytes 638984 | tf_op jit(solution)/shard_map/ppermute | solution.py:657
  64.4 6.7 %collective-permute-start.22 = (bf16[208,512]{1,0:T(8,128)(2,1)S(1)}, bf16[208,512]{1,0:T(8,128)(2,1)S(1)}, u32[]{:S(2)}, u32[]{:S(2)}) collective-permute-start(bf16[208,512]{1,0:T(8,128)(2,1)S(1)} %get-tuple-element.192), channel_id=1, source_target_pairs={{0,2},{2,4},{4,6},{6,7},{7,5},{5,3},{3,1},{1,0},{8,10},{10,12},{12... | collective-permute-start | bytes 638984 | tf_op jit(solution)/shard_map/ppermute | solution.py:657
  65.0 5.8 %collective-permute-start.23 = (bf16[80,512]{1,0:T(8,128)(2,1)S(1)}, bf16[80,512]{1,0:T(8,128)(2,1)S(1)}, u32[]{:S(2)}, u32[]{:S(2)}) collective-permute-start(bf16[80,512]{1,0:T(8,128)(2,1)S(1)} %get-tuple-element.199), channel_id=1, source_target_pairs={{2,0},{4,2},{6,4},{7,6},{5,7},{3,5},{1,3},{0,1},{10,8},{12,10},{14... | collective-permute-start | bytes 245768 | tf_op jit(solution)/shard_map/ppermute | solution.py:657
  66.7 4.5 %collective-permute-start.24 = (bf16[80,512]{1,0:T(8,128)(2,1)S(1)}, bf16[80,512]{1,0:T(8,128)(2,1)S(1)}, u32[]{:S(2)}, u32[]{:S(2)}) collective-permute-start(bf16[80,512]{1,0:T(8,128)(2,1)S(1)} %get-tuple-element.200), channel_id=1, source_target_pairs={{0,2},{2,4},{4,6},{6,7},{7,5},{5,3},{3,1},{1,0},{8,10},{10,12},{12... | collective-permute-start | bytes 245768 | tf_op jit(solution)/shard_map/ppermute | solution.py:657
  71.4 8.5 %collective-permute-start.25 = (bf16[208,512]{1,0:T(8,128)(2,1)S(1)}, bf16[208,512]{1,0:T(8,128)(2,1)S(1)}, u32[]{:S(2)}, u32[]{:S(2)}) collective-permute-start(bf16[208,512]{1,0:T(8,128)(2,1)S(1)} %get-tuple-element.209), channel_id=1, source_target_pairs={{2,0},{4,2},{6,4},{7,6},{5,7},{3,5},{1,3},{0,1},{10,8},{12,10},{14... | collective-permute-start | bytes 638984 | tf_op jit(solution)/shard_map/ppermute | solution.py:657
  73.2 6.7 %collective-permute-start.26 = (bf16[208,512]{1,0:T(8,128)(2,1)S(1)}, bf16[208,512]{1,0:T(8,128)(2,1)S(1)}, u32[]{:S(2)}, u32[]{:S(2)}) collective-permute-start(bf16[208,512]{1,0:T(8,128)(2,1)S(1)} %get-tuple-element.210), channel_id=1, source_target_pairs={{0,2},{2,4},{4,6},{6,7},{7,5},{5,3},{3,1},{1,0},{8,10},{10,12},{12... | collective-permute-start | bytes 638984 | tf_op jit(solution)/shard_map/ppermute | solution.py:657
  73.6 5.3 %collective-permute-start.27 = (bf16[80,512]{1,0:T(8,128)(2,1)S(1)}, bf16[80,512]{1,0:T(8,128)(2,1)S(1)}, u32[]{:S(2)}, u32[]{:S(2)}) collective-permute-start(bf16[80,512]{1,0:T(8,128)(2,1)S(1)} %get-tuple-element.217), channel_id=1, source_target_pairs={{2,0},{4,2},{6,4},{7,6},{5,7},{3,5},{1,3},{0,1},{10,8},{12,10},{14... | collective-permute-start | bytes 245768 | tf_op jit(solution)/shard_map/ppermute | solution.py:657
  75.5 4.5 %copy-start = (bf16[16,512,128]{2,1,0:T(8,128)(2,1)S(1)}, bf16[16,512,128]{2,1,0:T(8,128)(2,1)}, u32[]{:S(2)}) copy-start(bf16[16,512,128]{2,1,0:T(8,128)(2,1)} %refs_8_.1) | copy-start | bytes 6291460
  75.5 4.5 %collective-permute-start.28 = (bf16[80,512]{1,0:T(8,128)(2,1)S(1)}, bf16[80,512]{1,0:T(8,128)(2,1)S(1)}, u32[]{:S(2)}, u32[]{:S(2)}) collective-permute-start(bf16[80,512]{1,0:T(8,128)(2,1)S(1)} %get-tuple-element.218), channel_id=1, source_target_pairs={{0,2},{2,4},{4,6},{6,7},{7,5},{5,3},{3,1},{1,0},{8,10},{10,12},{12... | collective-permute-start | bytes 245768 | tf_op jit(solution)/shard_map/ppermute | solution.py:657
